TPU v7x, 32 devices: a whole 2x2x4 slice. The times are simulated.
32 devices in a mesh: sector: 8 (over z, x), band: 4 (over y, core).
Axes of the slice: x: 2, y: 2, z: 4, core: 2. Of those that a mesh axis runs over, the one named last changes fastest.
Arguments:
- given_load: float32 [3, 64, 64, 256], P(None, 'sector', 'band'), may hold values from -20 to 20, as said below
- displacement: float32 [3, 64, 64, 256], P(None, 'sector', 'band'), may hold values from -3 to 3
- mass_coef: float32 [64, 64, 256], P('sector', 'band'), may hold values from 0.05 to 0.5
- stiffness: float32 [64, 64, 256], P('sector', 'band'), may hold values from 0.5 to 2
- bearing_node: int32 [128], P(('sector', 'band')), may hold values from 0 to 2047
- stick_state: int32 [128], P(('sector', 'band')), may hold values 0 or 1
- slip_prev: float32 [2, 128], P(None, ('sector', 'band')), may hold values from -3 to 3
- bearing_old: float32 [2, 128], P(None, ('sector', 'band')), may hold values from -3 to 3
- bearing_weight: float32 [128], P(('sector', 'band')), may hold values from 4 to 16
Outputs:
- increment: float32 [3, 64, 64, 256], P(None, 'sector', 'band')
- cg_residual: float32 [3, 64, 64, 256], P(None, 'sector', 'band')
- bearing_force: float32 [3, 128], P(None, ('sector', 'band'))
Inputs may be any that keep to these rules, and one draw needn't show every extreme that they name: `bearing_node`: each index names a node of the raft-base layer within the bearing's own sector; several bearings may share a node. `given_load`: loads of order one to a few tens.
All inputs are finite; a program needn't handle non-finite values. No bound on the sum of `stick_state` on one device may be relied on, other than what follows from the above.
Results may differ from a plain program's by a relative error of at most 0.00021.
Values sent between devices are 32-bit elements; how exact they have to be, the bound alone decides.
No kernel may reach another device: no remote copies, remote signals or barrier semaphores. Data moves between devices by JAX's collectives and lax.ppermute only.
A program may use at most 64 MiB of HBM per device.

v0:
```python
import jax
import jax.numpy as jnp
from jax import lax
from jax.sharding import PartitionSpec as P

ITERS = 4


K_STICK = 4.0
K_VERT = 8.0
MU_FAST = 0.15
MU_SLOW = 0.04
RATE_GAIN = 2.0
RATE_DECAY = 2.0
V_FLOOR = 0.05
COMPONENT_SCALE = (1.0, 1.0, 2.0)
HIGHEST = lax.Precision.HIGHEST


def padded(x, sides, width, wrap):
    for axis, dim in sides:
        size, length = (lax.axis_size(axis), x.shape[dim])
        up = [(i, (i + 1) % size) for i in range(size if wrap else size - 1)]
        down = [(j, i) for i, j in up]
        last = lax.slice_in_dim(x, length - width, length, axis=dim)
        leading = lax.slice_in_dim(x, 0, width, axis=dim)
        before = lax.ppermute(last, axis, up)
        after = lax.ppermute(leading, axis, down)
        x = jnp.concatenate([before, x, after], axis=dim)
    return x


def from_root(value, axis, source):
    kept = jnp.where(lax.axis_index(axis) == source, value, 0).astype(value.dtype)
    return lax.psum(kept, axis)


def face_conductance(left, right):
    return 2.0 * left * right / (left + right)


def local_conductances(stiffness):
    cycle_padded = padded(stiffness, (("sector", 0),), 1, True)
    cond_sector = face_conductance(cycle_padded[:-1], cycle_padded[1:])
    height_padded = padded(stiffness, (("band", 1),), 1, False)
    cond_height = face_conductance(height_padded[:, :-1], height_padded[:, 1:])
    cond_radial = face_conductance(stiffness[:, :, :-1], stiffness[:, :, 1:])
    return (cond_sector, cond_height, cond_radial)


def field_faces(field):
    cycle_padded = padded(field, (("sector", 1),), 1, True)
    height_padded = padded(field, (("band", 2),), 1, False)
    return (cycle_padded, height_padded)


def operate(field, mass_coef, conds, bottom_diag):
    cond_sector, cond_height, cond_radial = conds
    scales = jnp.array(COMPONENT_SCALE, jnp.float32)[:, None, None, None]
    cycle_padded, height_padded = field_faces(field)
    flux_sector = cond_sector[None] * (cycle_padded[:, 1:] - cycle_padded[:, :-1])
    total = -(flux_sector[:, 1:] - flux_sector[:, :-1])
    flux_height = cond_height[None] * (height_padded[:, :, 1:] - height_padded[:, :, :-1])
    total = total - (flux_height[:, :, 1:] - flux_height[:, :, :-1])
    flux_radial = cond_radial[None] * (field[..., 1:] - field[..., :-1])
    flux_radial = jnp.pad(flux_radial, ((0, 0), (0, 0), (0, 0), (1, 1)))
    total = total - (flux_radial[..., 1:] - flux_radial[..., :-1])
    layers = field.shape[2]
    diag_full = jnp.pad(bottom_diag[:, :, None, :], ((0, 0), (0, 0), (0, layers - 1), (0, 0)))
    return mass_coef[None] * field + scales * total + diag_full * field


def bearing_law(at_node, stick_state, slip_prev, bearing_old, bearing_weight):
    moved = at_node[:2]
    trial = K_STICK * (moved - slip_prev)
    slip_rate = RATE_GAIN * (moved - bearing_old)
    slip_speed = jnp.sqrt(
        slip_rate[0] * slip_rate[0] + slip_rate[1] * slip_rate[1] + V_FLOOR * V_FLOOR
    )
    friction = MU_FAST - (MU_FAST - MU_SLOW) * jnp.exp(-RATE_DECAY * slip_speed)
    capacity = friction * bearing_weight
    magnitude = jnp.sqrt(trial[0] * trial[0] + trial[1] * trial[1])
    sliding = capacity[None] * trial / jnp.maximum(magnitude, capacity)[None]
    sticking = stick_state[None] == 1
    horizontal = jnp.where(sticking, trial, sliding)
    vertical = K_VERT * at_node[2]
    force = jnp.concatenate([horizontal, vertical[None]], axis=0)
    stick_k = jnp.where(stick_state == 1, K_STICK, 0.0).astype(jnp.float32)
    stiff = jnp.stack([stick_k, stick_k, jnp.full_like(stick_k, K_VERT)], axis=0)
    return (force, stiff)


def node_selector(nodes, count):
    positions = jnp.arange(count, dtype=jnp.int32)
    return (nodes[:, None] == positions[None, :]).astype(jnp.float32)


def bearings_on_row(raft_flat, nodes, stick_state, slip_prev, bearing_old, bearing_weight):
    selector = node_selector(nodes, raft_flat.shape[1])
    at_node = jnp.dot(raft_flat, selector.T, precision=HIGHEST, preferred_element_type=jnp.float32)
    force, stiff = bearing_law(at_node, stick_state, slip_prev, bearing_old, bearing_weight)
    loads = jnp.dot(force, selector, precision=HIGHEST, preferred_element_type=jnp.float32)
    bottom = jnp.dot(stiff, selector, precision=HIGHEST, preferred_element_type=jnp.float32)
    return (force, loads, bottom)


def paired_products(residual, image):
    return lax.psum((jnp.sum(residual * residual), jnp.sum(residual * image)), ("sector", "band"))


def per_device(
    given_load,
    displacement,
    mass_coef,
    stiffness,
    bearing_node,
    stick_state,
    slip_prev,
    bearing_old,
    bearing_weight,
):
    comps, rows_here, layers, radial = displacement.shape
    conds = local_conductances(stiffness)
    band_index = lax.axis_index("band")
    on_raft = (band_index == 0).astype(jnp.float32)
    raft_local = displacement[:, :, 0, :].reshape(comps, rows_here * radial)
    raft_flat = from_root(raft_local, "band", 0)
    own_force, loads, bottom = bearings_on_row(
        raft_flat, bearing_node, stick_state, slip_prev, bearing_old, bearing_weight
    )
    loads, bottom = lax.psum((loads, bottom), "band")
    loads = (loads * on_raft).reshape(comps, rows_here, radial)
    bottom = (bottom * on_raft).reshape(comps, rows_here, radial)
    zero_diag = jnp.zeros_like(bottom)
    load_full = jnp.pad(loads[:, :, None, :], ((0, 0), (0, 0), (0, layers - 1), (0, 0)))
    newton_rhs = given_load - operate(displacement, mass_coef, conds, zero_diag) - load_full
    increment = jnp.zeros_like(newton_rhs)
    residual = newton_rhs
    image = operate(residual, mass_coef, conds, bottom)
    norm_now, product = paired_products(residual, image)
    alpha = norm_now / product
    direction = residual
    along = image
    for iteration in range(ITERS):
        increment = increment + alpha * direction
        residual = residual - alpha * along
        if iteration + 1 < ITERS:
            image = operate(residual, mass_coef, conds, bottom)
            norm_next, product = paired_products(residual, image)
            ratio = norm_next / norm_now
            alpha = norm_next / (product - ratio * norm_next / alpha)
            direction = residual + ratio * direction
            along = image + ratio * along
            norm_now = norm_next
    return (increment, residual, own_force)


def solution(mesh):
    return jax.shard_map(
        per_device,
        mesh=mesh,
        in_specs=(
            P(None, "sector", "band", None),
            P(None, "sector", "band", None),
            P("sector", "band", None),
            P("sector", "band", None),
            P(("sector", "band")),
            P(("sector", "band")),
            P(None, ("sector", "band")),
            P(None, ("sector", "band")),
            P(("sector", "band")),
        ),
        out_specs=(
            P(None, "sector", "band", None),
            P(None, "sector", "band", None),
            P(None, ("sector", "band")),
        ),
        check_vma=False,
    )
```

profile of v0, /device:TPU:0, one launch (start us, length us, event | category | flops | bytes accessed | tf_op | source)
XLA Modules:
  0.0 287.2 jit_solution(16826672943593096671)
XLA Ops:
  0.6 0.9 fusion.78
  1.6 2.4 collective-permute-start.4
  3.9 1.3 collective-permute-start.5
  5.2 0.7 fusion.77
  6.0 5.4 %collective-permute-start.1 = (f32[1,16,256]{2,1,0:T(8,128)S(1)}, f32[1,16,256]{2,1,0:T(8,128)S(1)}, u32[]{:S(2)}, u32[]{:S(2)}) collective-permute-start(f32[1,16,256]{2,1,0:T(8,128)S(1)} %get-tuple-element.52), channel_id=1, source_target_pairs={{4,0},{8,4},{12,8},{16,12},{20,16},{24,20},{28,24},{0,28},{5,1},{9... | collective-permute-start | bytes 49160 | tf_op jit(solution)/shard_map/ppermute | solution.py:28
  11.3 1.1 fusion.54
  12.5 1.3 collective-permute-start.6
  14.0 14.9 %psum.77 = f32[3,2048]{1,0:T(4,128)S(1)} all-reduce(f32[3,2048]{1,0:T(4,128)S(1)} %bitcast.11), channel_id=1, replica_groups=mesh['sector'=8,'band'=4] {'band'}, use_global_device_ids=true, to_apply=%region_0.1 | all-reduce | flops 6144 | bytes 49152 | tf_op jit(solution)/shard_map/psum | solution.py:35
  29.2 0.4 copy-done.7
  29.6 0.3 copy-done.5
  29.9 0.7 copy-done.8
  30.6 0.2 fusion.52
  30.8 0.3 copy-done.6
  31.2 0.2 fusion.51
  31.4 10.8 %all-reduce.11 = (f32[3,2048]{1,0:T(4,128)S(1)}, f32[3,2048]{1,0:T(4,128)S(1)}) all-reduce(f32[3,2048]{1,0:T(4,128)S(1)} %fusion.52, f32[3,2048]{1,0:T(4,128)S(1)} %fusion.51), channel_id=1, replica_groups=mesh['sector'=8,'band'=4] {'band'}, use_global_device_ids=true, to_apply=%region_1.2 | all-reduce | flops 12288 | bytes 98304 | tf_op jit(solution)/shard_map/psum | solution.py:131
  42.5 1.5 collective-permute-start.7
  44.2 4.8 %collective-permute-start.2 = (f32[3,1,16,256]{3,2,1,0:T(8,128)S(1)}, f32[3,1,16,256]{3,2,1,0:T(8,128)S(1)}, u32[]{:S(2)}, u32[]{:S(2)}) collective-permute-start(f32[3,1,16,256]{3,2,1,0:T(8,128)S(1)} %get-tuple-element.51), channel_id=1, source_target_pairs={{4,0},{8,4},{12,8},{16,12},{20,16},{24,20},{28,24},{0,28},{5,1},{9... | collective-permute-start | bytes 147464 | tf_op jit(solution)/shard_map/ppermute | solution.py:28
  49.3 2.0 collective-permute-done.3
  51.4 0.3 fusion.16
  52.0 2.0 collective-permute-start.11
  54.0 1.3 collective-permute-start.10
  55.4 4.9 %collective-permute-start.8 = (f32[3,1,16,256]{3,2,1,0:T(8,128)S(1)}, f32[3,1,16,256]{3,2,1,0:T(8,128)S(1)}, u32[]{:S(2)}, u32[]{:S(2)}) collective-permute-start(f32[3,1,16,256]{3,2,1,0:T(8,128)S(1)} %get-tuple-element.44), channel_id=1, source_target_pairs={{4,0},{8,4},{12,8},{16,12},{20,16},{24,20},{28,24},{0,28},{5,1},{9... | collective-permute-start | bytes 147464 | tf_op jit(solution)/shard_map/ppermute | solution.py:28
  60.3 2.0 collective-permute-done.9
  62.4 0.9 multiply_reduce_fusion.6
  63.4 41.6 %all-reduce.10 = (f32[]{:T(128)}, f32[]{:T(128)}) all-reduce(f32[]{:T(128)} %get-tuple-element.10, f32[]{:T(128)} %get-tuple-element.9), channel_id=1, replica_groups=mesh['sector'=8,'band'=4] {'sector','band'}, use_global_device_ids=true, to_apply=%region_3.4 | all-reduce | flops 2 | bytes 16 | tf_op jit(solution)/shard_map/psum | solution.py:108
  106.6 1.3 collective-permute-start.15
  107.9 1.3 collective-permute-start.14
  109.2 2.3 collective-permute-start.13
  111.5 2.4 collective-permute-start.12
  114.1 2.1 collective-permute-done.13
  116.2 1.0 multiply_reduce_fusion.4
  117.2 44.4 %all-reduce.9 = (f32[]{:T(128)}, f32[]{:T(128)}) all-reduce(f32[]{:T(128)} %get-tuple-element.8, f32[]{:T(128)} %get-tuple-element.7), channel_id=1, replica_groups=mesh['sector'=8,'band'=4] {'sector','band'}, use_global_device_ids=true, to_apply=%region_8.9 | all-reduce | flops 2 | bytes 16 | tf_op jit(solution)/shard_map/psum | solution.py:108
  166.6 1.3 collective-permute-start.19
  167.9 1.3 collective-permute-start.18
  169.2 2.3 collective-permute-start.17
  171.6 2.4 collective-permute-start.16
  174.1 2.1 collective-permute-done.17
  176.2 1.8 multiply_reduce_fusion.2
  178.0 44.3 %all-reduce.8 = (f32[]{:T(128)}, f32[]{:T(128)}) all-reduce(f32[]{:T(128)} %get-tuple-element.6, f32[]{:T(128)} %get-tuple-element.5), channel_id=1, replica_groups=mesh['sector'=8,'band'=4] {'sector','band'}, use_global_device_ids=true, to_apply=%region_12.13 | all-reduce | flops 2 | bytes 16 | tf_op jit(solution)/shard_map/psum | solution.py:108
  225.9 1.2 multiply_subtract_fusion.1
  227.3 1.3 collective-permute-start.23
  228.6 1.3 collective-permute-start.22
  229.9 2.3 collective-permute-start.21
  232.2 2.4 collective-permute-start.20
  234.8 2.1 collective-permute-done.21
  236.9 0.9 multiply_reduce_fusion
  237.9 44.4 %all-reduce.7 = (f32[]{:T(128)}, f32[]{:T(128)}) all-reduce(f32[]{:T(128)} %get-tuple-element.4, f32[]{:T(128)} %get-tuple-element.3), channel_id=1, replica_groups=mesh['sector'=8,'band'=4] {'sector','band'}, use_global_device_ids=true, to_apply=%region_16.17 | all-reduce | flops 2 | bytes 16 | tf_op jit(solution)/shard_map/psum | solution.py:108
  286.1 1.2 multiply_subtract_fusion
  (88 shorter events, 2.9 us)
Async XLA Ops:
  0.6 13.2 %copy-start.2 = (f32[8,16,256]{2,1,0:T(8,128)S(1)}, f32[8,16,256]{2,1,0:T(8,128)}, u32[]{:S(2)}) copy-start(f32[8,16,256]{2,1,0:T(8,128)} %param.17) | copy-start | bytes 393220
  1.6 47.5 %collective-permute-start.4 = (f32[8,1,256]{2,1,0:T(1,128)S(1)}, f32[8,1,256]{2,1,0:T(1,128)S(1)}, u32[]{:S(2)}, u32[]{:S(2)}) collective-permute-start(f32[8,1,256]{2,1,0:T(1,128)S(1)} %get-tuple-element.57), channel_id=1, source_target_pairs={{0,1},{1,2},{2,3},{4,5},{5,6},{6,7},{8,9},{9,10},{10,11},{12,13},{... | collective-permute-start | bytes 24584 | tf_op jit(solution)/shard_map/ppermute | solution.py:27
  3.9 40.3 %collective-permute-start.5 = (f32[8,1,256]{2,1,0:T(1,128)S(1)}, f32[8,1,256]{2,1,0:T(1,128)S(1)}, u32[]{:S(2)}, u32[]{:S(2)}) collective-permute-start(f32[8,1,256]{2,1,0:T(1,128)S(1)} %get-tuple-element.58), channel_id=1, source_target_pairs={{1,0},{2,1},{3,2},{5,4},{6,5},{7,6},{9,8},{10,9},{11,10},{13,12},{... | collective-permute-start | bytes 24584 | tf_op jit(solution)/shard_map/ppermute | solution.py:28
  6.0 38.1 %collective-permute-start.1 = (f32[1,16,256]{2,1,0:T(8,128)S(1)}, f32[1,16,256]{2,1,0:T(8,128)S(1)}, u32[]{:S(2)}, u32[]{:S(2)}) collective-permute-start(f32[1,16,256]{2,1,0:T(8,128)S(1)} %get-tuple-element.52), channel_id=1, source_target_pairs={{4,0},{8,4},{12,8},{16,12},{20,16},{24,20},{28,24},{0,28},{5,1},{9... | collective-permute-start | bytes 49160 | tf_op jit(solution)/shard_map/ppermute | solution.py:28
  11.3 31.2 %collective-permute-start = (f32[1,16,256]{2,1,0:T(8,128)S(1)}, f32[1,16,256]{2,1,0:T(8,128)S(1)}, u32[]{:S(2)}, u32[]{:S(2)}) collective-permute-start(f32[1,16,256]{2,1,0:T(8,128)S(1)} %get-tuple-element.53), channel_id=1, source_target_pairs={{0,4},{4,8},{8,12},{12,16},{16,20},{20,24},{24,28},{28,0},{1,5},{5... | collective-permute-start | bytes 49160 | tf_op jit(solution)/shard_map/ppermute | solution.py:27
  12.4 1.3 copy-start.9
  12.5 36.7 %collective-permute-start.6 = (f32[3,8,1,256]{3,2,1,0:T(1,128)S(1)}, f32[3,8,1,256]{3,2,1,0:T(1,128)S(1)}, u32[]{:S(2)}, u32[]{:S(2)}) collective-permute-start(f32[3,8,1,256]{3,2,1,0:T(1,128)S(1)} %get-tuple-element.48), channel_id=1, source_target_pairs={{1,0},{2,1},{3,2},{5,4},{6,5},{7,6},{9,8},{10,9},{11,10},{13,12},{... | collective-permute-start | bytes 73736 | tf_op jit(solution)/shard_map/ppermute | solution.py:28
  13.8 28.4 %copy-start = (f32[3,8,16,256]{3,2,1,0:T(8,128)S(1)}, f32[3,8,16,256]{3,2,1,0:T(8,128)}, u32[]{:S(2)}) copy-start(f32[3,8,16,256]{3,2,1,0:T(8,128)} %param.15) | copy-start | bytes 1179652
  14.0 15.0 %copy-start.10 = (s32[4]{0:T(128)S(1)}, s32[4]{0:T(128)}, u32[]{:S(2)}) copy-start(s32[4]{0:T(128)} %param.18) | copy-start | bytes 52
  28.9 0.7 copy-start.7
  29.1 0.7 copy-start.5
  29.9 0.7 copy-start.8
  30.6 0.6 copy-start.6
  42.5 6.7 %collective-permute-start.7 = (f32[3,8,1,256]{3,2,1,0:T(1,128)S(1)}, f32[3,8,1,256]{3,2,1,0:T(1,128)S(1)}, u32[]{:S(2)}, u32[]{:S(2)}) collective-permute-start(f32[3,8,1,256]{3,2,1,0:T(1,128)S(1)} %get-tuple-element.49), channel_id=1, source_target_pairs={{0,1},{1,2},{2,3},{4,5},{5,6},{6,7},{8,9},{9,10},{10,11},{12,13},{... | collective-permute-start | bytes 73736 | tf_op jit(solution)/shard_map/ppermute | solution.py:27
  44.1 7.2 %collective-permute-start.3 = (f32[3,1,16,256]{3,2,1,0:T(8,128)S(1)}, f32[3,1,16,256]{3,2,1,0:T(8,128)S(1)}, u32[]{:S(2)}, u32[]{:S(2)}) collective-permute-start(f32[3,1,16,256]{3,2,1,0:T(8,128)S(1)} %get-tuple-element.50), channel_id=1, source_target_pairs={{0,4},{4,8},{8,12},{12,16},{16,20},{20,24},{24,28},{28,0},{1,5},{5... | collective-permute-start | bytes 147464 | tf_op jit(solution)/shard_map/ppermute | solution.py:27
  44.2 7.1 %collective-permute-start.2 = (f32[3,1,16,256]{3,2,1,0:T(8,128)S(1)}, f32[3,1,16,256]{3,2,1,0:T(8,128)S(1)}, u32[]{:S(2)}, u32[]{:S(2)}) collective-permute-start(f32[3,1,16,256]{3,2,1,0:T(8,128)S(1)} %get-tuple-element.51), channel_id=1, source_target_pairs={{4,0},{8,4},{12,8},{16,12},{20,16},{24,20},{28,24},{0,28},{5,1},{9... | collective-permute-start | bytes 147464 | tf_op jit(solution)/shard_map/ppermute | solution.py:28
  49.3 2.1 copy-start.1
  49.3 2.1 copy-start.3
  49.3 2.1 copy-start.4
  52.0 8.3 %collective-permute-start.11 = (f32[3,8,1,256]{3,2,1,0:T(1,128)S(1)}, f32[3,8,1,256]{3,2,1,0:T(1,128)S(1)}, u32[]{:S(2)}, u32[]{:S(2)}) collective-permute-start(f32[3,8,1,256]{3,2,1,0:T(1,128)S(1)} %get-tuple-element.45), channel_id=1, source_target_pairs={{0,1},{1,2},{2,3},{4,5},{5,6},{6,7},{8,9},{9,10},{10,11},{12,13},{... | collective-permute-start | bytes 73736 | tf_op jit(solution)/shard_map/ppermute | solution.py:27
  54.0 6.2 %collective-permute-start.10 = (f32[3,8,1,256]{3,2,1,0:T(1,128)S(1)}, f32[3,8,1,256]{3,2,1,0:T(1,128)S(1)}, u32[]{:S(2)}, u32[]{:S(2)}) collective-permute-start(f32[3,8,1,256]{3,2,1,0:T(1,128)S(1)} %get-tuple-element.46), channel_id=1, source_target_pairs={{1,0},{2,1},{3,2},{5,4},{6,5},{7,6},{9,8},{10,9},{11,10},{13,12},{... | collective-permute-start | bytes 73736 | tf_op jit(solution)/shard_map/ppermute | solution.py:28
  55.3 7.0 %collective-permute-start.9 = (f32[3,1,16,256]{3,2,1,0:T(8,128)S(1)}, f32[3,1,16,256]{3,2,1,0:T(8,128)S(1)}, u32[]{:S(2)}, u32[]{:S(2)}) collective-permute-start(f32[3,1,16,256]{3,2,1,0:T(8,128)S(1)} %get-tuple-element.43), channel_id=1, source_target_pairs={{0,4},{4,8},{8,12},{12,16},{16,20},{20,24},{24,28},{28,0},{1,5},{5... | collective-permute-start | bytes 147464 | tf_op jit(solution)/shard_map/ppermute | solution.py:27
  55.4 7.0 %collective-permute-start.8 = (f32[3,1,16,256]{3,2,1,0:T(8,128)S(1)}, f32[3,1,16,256]{3,2,1,0:T(8,128)S(1)}, u32[]{:S(2)}, u32[]{:S(2)}) collective-permute-start(f32[3,1,16,256]{3,2,1,0:T(8,128)S(1)} %get-tuple-element.44), channel_id=1, source_target_pairs={{4,0},{8,4},{12,8},{16,12},{20,16},{24,20},{28,24},{0,28},{5,1},{9... | collective-permute-start | bytes 147464 | tf_op jit(solution)/shard_map/ppermute | solution.py:28
  106.6 7.4 %collective-permute-start.15 = (f32[3,8,1,256]{3,2,1,0:T(1,128)S(1)}, f32[3,8,1,256]{3,2,1,0:T(1,128)S(1)}, u32[]{:S(2)}, u32[]{:S(2)}) collective-permute-start(f32[3,8,1,256]{3,2,1,0:T(1,128)S(1)} %get-tuple-element.41), channel_id=1, source_target_pairs={{0,1},{1,2},{2,3},{4,5},{5,6},{6,7},{8,9},{9,10},{10,11},{12,13},{... | collective-permute-start | bytes 73736 | tf_op jit(solution)/shard_map/ppermute | solution.py:27
  107.9 6.1 %collective-permute-start.14 = (f32[3,8,1,256]{3,2,1,0:T(1,128)S(1)}, f32[3,8,1,256]{3,2,1,0:T(1,128)S(1)}, u32[]{:S(2)}, u32[]{:S(2)}) collective-permute-start(f32[3,8,1,256]{3,2,1,0:T(1,128)S(1)} %get-tuple-element.42), channel_id=1, source_target_pairs={{1,0},{2,1},{3,2},{5,4},{6,5},{7,6},{9,8},{10,9},{11,10},{13,12},{... | collective-permute-start | bytes 73736 | tf_op jit(solution)/shard_map/ppermute | solution.py:28
  109.2 6.9 %collective-permute-start.13 = (f32[3,1,16,256]{3,2,1,0:T(8,128)S(1)}, f32[3,1,16,256]{3,2,1,0:T(8,128)S(1)}, u32[]{:S(2)}, u32[]{:S(2)}) collective-permute-start(f32[3,1,16,256]{3,2,1,0:T(8,128)S(1)} %get-tuple-element.39), channel_id=1, source_target_pairs={{0,4},{4,8},{8,12},{12,16},{16,20},{20,24},{24,28},{28,0},{1,5},{5... | collective-permute-start | bytes 147464 | tf_op jit(solution)/shard_map/ppermute | solution.py:27
  111.5 4.6 %collective-permute-start.12 = (f32[3,1,16,256]{3,2,1,0:T(8,128)S(1)}, f32[3,1,16,256]{3,2,1,0:T(8,128)S(1)}, u32[]{:S(2)}, u32[]{:S(2)}) collective-permute-start(f32[3,1,16,256]{3,2,1,0:T(8,128)S(1)} %get-tuple-element.40), channel_id=1, source_target_pairs={{4,0},{8,4},{12,8},{16,12},{20,16},{24,20},{28,24},{0,28},{5,1},{9... | collective-permute-start | bytes 147464 | tf_op jit(solution)/shard_map/ppermute | solution.py:28
  166.6 7.4 %collective-permute-start.19 = (f32[3,8,1,256]{3,2,1,0:T(1,128)S(1)}, f32[3,8,1,256]{3,2,1,0:T(1,128)S(1)}, u32[]{:S(2)}, u32[]{:S(2)}) collective-permute-start(f32[3,8,1,256]{3,2,1,0:T(1,128)S(1)} %get-tuple-element.37), channel_id=1, source_target_pairs={{0,1},{1,2},{2,3},{4,5},{5,6},{6,7},{8,9},{9,10},{10,11},{12,13},{... | collective-permute-start | bytes 73736 | tf_op jit(solution)/shard_map/ppermute | solution.py:27
  167.9 6.1 %collective-permute-start.18 = (f32[3,8,1,256]{3,2,1,0:T(1,128)S(1)}, f32[3,8,1,256]{3,2,1,0:T(1,128)S(1)}, u32[]{:S(2)}, u32[]{:S(2)}) collective-permute-start(f32[3,8,1,256]{3,2,1,0:T(1,128)S(1)} %get-tuple-element.38), channel_id=1, source_target_pairs={{1,0},{2,1},{3,2},{5,4},{6,5},{7,6},{9,8},{10,9},{11,10},{13,12},{... | collective-permute-start | bytes 73736 | tf_op jit(solution)/shard_map/ppermute | solution.py:28
  169.2 6.9 %collective-permute-start.17 = (f32[3,1,16,256]{3,2,1,0:T(8,128)S(1)}, f32[3,1,16,256]{3,2,1,0:T(8,128)S(1)}, u32[]{:S(2)}, u32[]{:S(2)}) collective-permute-start(f32[3,1,16,256]{3,2,1,0:T(8,128)S(1)} %get-tuple-element.35), channel_id=1, source_target_pairs={{0,4},{4,8},{8,12},{12,16},{16,20},{20,24},{24,28},{28,0},{1,5},{5... | collective-permute-start | bytes 147464 | tf_op jit(solution)/shard_map/ppermute | solution.py:27
  171.6 4.6 %collective-permute-start.16 = (f32[3,1,16,256]{3,2,1,0:T(8,128)S(1)}, f32[3,1,16,256]{3,2,1,0:T(8,128)S(1)}, u32[]{:S(2)}, u32[]{:S(2)}) collective-permute-start(f32[3,1,16,256]{3,2,1,0:T(8,128)S(1)} %get-tuple-element.36), channel_id=1, source_target_pairs={{4,0},{8,4},{12,8},{16,12},{20,16},{24,20},{28,24},{0,28},{5,1},{9... | collective-permute-start | bytes 147464 | tf_op jit(solution)/shard_map/ppermute | solution.py:28
  227.3 7.4 %collective-permute-start.23 = (f32[3,8,1,256]{3,2,1,0:T(1,128)S(1)}, f32[3,8,1,256]{3,2,1,0:T(1,128)S(1)}, u32[]{:S(2)}, u32[]{:S(2)}) collective-permute-start(f32[3,8,1,256]{3,2,1,0:T(1,128)S(1)} %get-tuple-element.33), channel_id=1, source_target_pairs={{0,1},{1,2},{2,3},{4,5},{5,6},{6,7},{8,9},{9,10},{10,11},{12,13},{... | collective-permute-start | bytes 73736 | tf_op jit(solution)/shard_map/ppermute | solution.py:27
  228.6 6.1 %collective-permute-start.22 = (f32[3,8,1,256]{3,2,1,0:T(1,128)S(1)}, f32[3,8,1,256]{3,2,1,0:T(1,128)S(1)}, u32[]{:S(2)}, u32[]{:S(2)}) collective-permute-start(f32[3,8,1,256]{3,2,1,0:T(1,128)S(1)} %get-tuple-element.34), channel_id=1, source_target_pairs={{1,0},{2,1},{3,2},{5,4},{6,5},{7,6},{9,8},{10,9},{11,10},{13,12},{... | collective-permute-start | bytes 73736 | tf_op jit(solution)/shard_map/ppermute | solution.py:28
  229.9 6.9 %collective-permute-start.21 = (f32[3,1,16,256]{3,2,1,0:T(8,128)S(1)}, f32[3,1,16,256]{3,2,1,0:T(8,128)S(1)}, u32[]{:S(2)}, u32[]{:S(2)}) collective-permute-start(f32[3,1,16,256]{3,2,1,0:T(8,128)S(1)} %get-tuple-element.31), channel_id=1, source_target_pairs={{0,4},{4,8},{8,12},{12,16},{16,20},{20,24},{24,28},{28,0},{1,5},{5... | collective-permute-start | bytes 147464 | tf_op jit(solution)/shard_map/ppermute | solution.py:27
  232.2 4.6 %collective-permute-start.20 = (f32[3,1,16,256]{3,2,1,0:T(8,128)S(1)}, f32[3,1,16,256]{3,2,1,0:T(8,128)S(1)}, u32[]{:S(2)}, u32[]{:S(2)}) collective-permute-start(f32[3,1,16,256]{3,2,1,0:T(8,128)S(1)} %get-tuple-element.32), channel_id=1, source_target_pairs={{4,0},{8,4},{12,8},{16,12},{20,16},{24,20},{28,24},{0,28},{5,1},{9... | collective-permute-start | bytes 147464 | tf_op jit(solution)/shard_map/ppermute | solution.py:28
where the time goes:
time: 289 us; the launch traced here: 287 us
  blocking collectives  200 us (69%)
  starting transfers between devices  47 us (16%)
  between operations  14.7 us (5%)
  other arithmetic  10.6 us (4%)
  waiting for transfers between devices  10.2 us (4%)
  local copies, waits for them, and re-layouts  3.76 us (1%)
    psum x4, blocking collectives, paired_products(): lax.psum((jnp.sum(residual * residual), jnp.sum(residual * image)), ('sec...  175 us
    ppermute x12, starting transfers between devices, padded(): after = lax.ppermute(leading, axis, down)  30.1 us
    ppermute x12, starting transfers between devices, padded(): before = lax.ppermute(last, axis, up)  16.9 us
    psum x1, blocking collectives, from_root(): return lax.psum(kept, axis)  14.9 us
    psum x1, blocking collectives, per_device(): loads, bottom = lax.psum((loads, bottom), 'band')  10.8 us
    ppermute x12, waiting for transfers between devices, padded(): before = lax.ppermute(last, axis, up)  10.2 us
  transfers between devices with their start and end apart: 24, of which 5 were waited for; matrix products, arithmetic and copies ran while one was open for 1% of the time, Pallas kernels for 0%

commit v1 on v0

v1 whole, which is shorter than its diff:
```python
import functools

import jax
import jax.numpy as jnp
from jax import lax
from jax.experimental import pallas as pl
from jax.experimental.pallas import tpu as pltpu
from jax.sharding import PartitionSpec as P

ITERS = 4
DEPTH = ITERS

K_STICK = 4.0
K_VERT = 8.0
MU_FAST = 0.15
MU_SLOW = 0.04
RATE_GAIN = 2.0
RATE_DECAY = 2.0
V_FLOOR = 0.05
COMPONENT_SCALE = (1.0, 1.0, 2.0)

CENTER = 12.0
SPREAD = 12.0
FLOOR = 0.25

AXES = ("sector", "band")
F32 = jnp.float32
PARAM_ROW, PARAM_LANE, PARAM_STICK, PARAM_SLIP, PARAM_OLD, PARAM_WEIGHT = (0, 1, 2, 3, 5, 7)
VMEM_LIMIT = 48 * 1024 * 1024


def conductance(left, right):
    return 2.0 * left * right / jnp.maximum(left + right, FLOOR)


def ahead(x, axis):
    return pltpu.roll(x, x.shape[axis] - 1, axis)


def behind(x, axis):
    return pltpu.roll(x, 1, axis)


def round_up(n, multiple):
    return -(-n // multiple) * multiple


class SectorSlab:
    def __init__(self, comps, layers, bearings):
        d = DEPTH
        self.comps, self.layers, self.bearings = comps, layers, bearings
        self.stiff = comps * d * layers
        self.mass = self.stiff + d * layers
        self.disp = self.mass + (d - 1) * layers
        self.low = self.disp + comps * layers
        self.params = self.low + comps * d
        self.high = self.params + bearings
        self.rows = round_up(self.high + comps * d, 8)

    def residual_at(self, c, i):
        return (c * DEPTH + i) * self.layers


def local_kernel(
    u, load, mass, stiff, node, stick, slip, old, weight, r, slab_a, slab_b, band_a, band_b, own, *, radial
):
    comps, rows, layers, width = u.shape
    bearings = node.shape[0]
    d = DEPTH
    lane = lax.broadcasted_iota(jnp.int32, (layers, width), 1)
    layer = lax.broadcasted_iota(jnp.int32, (layers, width), 0)
    before = [None] * comps
    for a in range(rows):
        k = stiff[a]
        k_r = jnp.where(lane < width - 1, conductance(k, ahead(k, 1)), 0.0)
        k_h = jnp.where(layer < layers - 1, conductance(k, ahead(k, 0)), 0.0)
        k_s = conductance(k, stiff[a + 1]) if a + 1 < rows else None
        m = mass[a]
        for c in range(comps):
            v = u[c, a]
            flux_r = k_r * (ahead(v, 1) - v)
            flux_h = k_h * (ahead(v, 0) - v)
            total = flux_r - behind(flux_r, 1) + flux_h - behind(flux_h, 0)
            if before[c] is not None:
                total = total - before[c]
            if k_s is not None:
                before[c] = k_s * (u[c, a + 1] - v)
                total = total + before[c]
            r[c, a] = load[c, a] - m * v + COMPONENT_SCALE[c] * total

    at = lax.broadcasted_iota(jnp.int32, (8, 128), 0)
    col = lax.broadcasted_iota(jnp.int32, (8, 128), 1)
    tile = jnp.zeros((8, 128), F32)
    for j in range(bearings):
        row = node[j] // radial
        values = {
            PARAM_ROW: row.astype(F32),
            PARAM_LANE: (node[j] - row * radial).astype(F32),
            PARAM_STICK: stick[j].astype(F32),
            PARAM_SLIP: slip[0, j],
            PARAM_SLIP + 1: slip[1, j],
            PARAM_OLD: old[0, j],
            PARAM_OLD + 1: old[1, j],
            PARAM_WEIGHT: weight[j],
        }
        for p, value in values.items():
            tile = jnp.where((at == j) & (col == p), value, tile)
    own[...] = tile

    slab = SectorSlab(comps, layers, bearings)
    even = lax.rem(lax.axis_index("sector"), 2) == 0
    for out, upper in ((slab_a, even), (slab_b, jnp.logical_not(even))):
        first = jnp.where(upper, rows - d, 0)
        for i in range(d):
            for c in range(comps):
                out[pl.ds(slab.residual_at(c, i), layers)] = r[c, first + i]
                out[pl.ds(slab.low + c * d + i, 1)] = u[c, first + i, 0:1]
                out[pl.ds(slab.high + c * d + i, 1)] = u[c, first + i, layers - 1 : layers]
            out[pl.ds(slab.stiff + i * layers, layers)] = stiff[first + i]
        for i in range(d - 1):
            out[pl.ds(slab.mass + i * layers, layers)] = mass[jnp.where(upper, rows - (d - 1), 0) + i]
        for c in range(comps):
            out[pl.ds(slab.disp + c * layers, layers)] = u[c, jnp.where(upper, rows - 1, 0)]
        out[pl.ds(slab.params, bearings)] = jnp.zeros((bearings, width), F32)
        out[pl.ds(slab.params, bearings), 0:128] = tile[0:bearings]
        end = slab.high + comps * d
        if slab.rows > end:
            out[pl.ds(end, slab.rows - end)] = jnp.zeros((slab.rows - end, width), F32)

    even = lax.rem(lax.axis_index("band"), 2) == 0
    fields = [r.at[c] for c in range(comps)] + [u.at[c] for c in range(comps)] + [stiff, mass]
    for f, field in enumerate(fields):
        for pair in range(rows // 2):
            planes = [field[2 * pair + i] for i in range(2)]
            top = jnp.concatenate([x[layers - d :] for x in planes], axis=0)
            low = jnp.concatenate([x[:d] for x in planes], axis=0)
            band_a[f * (rows // 2) + pair] = jnp.where(even, top, low)
            band_b[f * (rows // 2) + pair] = jnp.where(even, low, top)


class CornerSlab:
    def __init__(self, comps, bearings):
        pairs = DEPTH // 2
        self.pairs = pairs
        self.stiff = comps * 2 * pairs
        self.mass = self.stiff + 2 * pairs
        self.disp = self.mass + 2 * pairs
        self.edge = self.disp + comps
        self.params = self.edge + comps
        self.bearing_rows = round_up(3 * bearings, 8)
        self.blocks = self.params + self.bearing_rows // 8


def corner_kernel(slab_a, slab_b, own, corner_a, corner_b, params, *, comps, layers, bearings):
    d = DEPTH
    slab, corner = SectorSlab(comps, layers, bearings), CornerSlab(comps, bearings)
    even = lax.rem(lax.axis_index("band"), 2) == 0

    def put(block, planes):
        top = jnp.concatenate([x[layers - d :] for x in planes], axis=0)
        low = jnp.concatenate([x[:d] for x in planes], axis=0)
        corner_a[block] = jnp.where(even, top, low)
        corner_b[block] = jnp.where(even, low, top)

    sides = (slab_a, slab_b)
    for n, side in enumerate(sides):

        def plane(offset):
            return side[pl.ds(offset, layers)]

        for pair in range(corner.pairs):
            rows = (2 * pair, 2 * pair + 1)
            at = n * corner.pairs + pair
            for c in range(comps):
                put(c * 2 * corner.pairs + at, [plane(slab.residual_at(c, i)) for i in rows])
            put(corner.stiff + at, [plane(slab.stiff + i * layers) for i in rows])
            put(corner.mass + at, [plane(slab.mass + min(i, d - 2) * layers) for i in rows])
    for c in range(comps):
        put(corner.disp + c, [x[pl.ds(slab.disp + c * layers, layers)] for x in sides])
        high = jnp.concatenate([x[pl.ds(slab.high + c * d, d)] for x in sides], axis=0)
        low = jnp.concatenate([x[pl.ds(slab.low + c * d, d)] for x in sides], axis=0)
        corner_a[corner.edge + c] = jnp.where(even, high, low)
        corner_b[corner.edge + c] = jnp.where(even, low, high)
    known = [own[0:bearings]] + [x[pl.ds(slab.params, bearings), 0:128] for x in sides]
    spare = corner.bearing_rows - 3 * bearings
    if spare:
        known.append(jnp.full((spare, 128), -1.0, F32))
    known = jnp.concatenate(known, axis=0)
    params[...] = known
    for i in range(corner.bearing_rows // 8):
        for out in (corner_a, corner_b):
            out[corner.params + i] = jnp.zeros(out.shape[1:], F32)
            out[corner.params + i, :, 0:128] = known[8 * i : 8 * i + 8]


def bearing_law(moved, vertical, stick, slip, old, weight):
    trial = [K_STICK * (moved[i] - slip[i]) for i in range(2)]
    rate = [RATE_GAIN * (moved[i] - old[i]) for i in range(2)]
    slip_speed = jnp.sqrt(rate[0] * rate[0] + rate[1] * rate[1] + V_FLOOR * V_FLOOR)
    friction = MU_FAST - (MU_FAST - MU_SLOW) * jnp.exp(-RATE_DECAY * slip_speed)
    capacity = friction * weight
    magnitude = jnp.sqrt(trial[0] * trial[0] + trial[1] * trial[1])
    largest = jnp.maximum(magnitude, capacity)
    forces = [jnp.where(stick == 1.0, t, capacity * t / largest) for t in trial]
    return forces + [K_VERT * vertical]


def power_kernel(
    r, u, mass, stiff, slab_a, slab_b, band_a, band_b, corner_a, corner_b, params, params_2, params_3,
    b0, b1, b2, b3, b4, payload,
    t0, t1, t2, t3, t4, ux, kx, mx, ks, kh, kr, diag, raft,
    *, bearings, sectors, bands,
):
    comps, rows, layers, width = r.shape
    d = DEPTH
    slab, corner = SectorSlab(comps, layers, bearings), CornerSlab(comps, bearings)
    sector, band = lax.axis_index("sector"), lax.axis_index("band")
    sector_even = lax.rem(sector, 2) == 0
    band_even = lax.rem(band, 2) == 0
    all_rows, all_layers = rows + 2 * d, layers + 2 * d
    own = pl.ds(d, layers)

    def place(a, carry):
        for c in range(comps):
            t0[c, d + a, own] = r[c, a]
            ux[c, d + a, own] = u[c, a]
        kx[d + a, own] = stiff[a]
        mx[d + a, own] = mass[a]
        return carry

    lax.fori_loop(0, rows, place, 0)
    first = {}
    for n, (side, above) in enumerate(((slab_a, sector_even), (slab_b, jnp.logical_not(sector_even)))):
        base = jnp.where(above, d + rows, 0)
        first[n] = base
        nearest = jnp.where(above, d + rows, d - 1)
        for i in range(d):
            for c in range(comps):
                t0[c, base + i, own] = side[pl.ds(slab.residual_at(c, i), layers)]
                ux[c, base + i, d : d + 1] = side[pl.ds(slab.low + c * d + i, 1)]
                ux[c, base + i, d + layers - 1 : d + layers] = side[pl.ds(slab.high + c * d + i, 1)]
            kx[base + i, own] = side[pl.ds(slab.stiff + i * layers, layers)]
        for i in range(d - 1):
            mx[jnp.where(above, d + rows, 1) + i, own] = side[pl.ds(slab.mass + i * layers, layers)]
        for c in range(comps):
            ux[c, nearest, own] = side[pl.ds(slab.disp + c * layers, layers)]

    def place_bands(a_above):
        for n, (side, corners) in enumerate(((band_a, corner_a), (band_b, corner_b))):
            above = a_above == (n == 0)
            at = d + layers if above else 0
            near = d + layers if above else d - 1
            where = pl.ds(at, d)

            def own_pair(pair, carry):
                for i in range(2):
                    part = slice(i * d, i * d + d)
                    row = d + 2 * pair + i
                    for c in range(comps):
                        t0[c, row, where] = side[c * (rows // 2) + pair, part]
                        ux[c, row, where] = side[(comps + c) * (rows // 2) + pair, part]
                    kx[row, where] = side[2 * comps * (rows // 2) + pair, part]
                    mx[row, where] = side[(2 * comps + 1) * (rows // 2) + pair, part]
                return carry

            lax.fori_loop(0, rows // 2, own_pair, 0)
            for m in range(2):
                base = first[m]
                above_m = sector_even if m == 0 else jnp.logical_not(sector_even)
                mass_base = jnp.where(above_m, d + rows, 1)
                nearest = jnp.where(above_m, d + rows, d - 1)
                for i in range(d):
                    part = slice((i % 2) * d, (i % 2) * d + d)
                    block = m * corner.pairs + i // 2
                    for c in range(comps):
                        t0[c, base + i, where] = corners[c * 2 * corner.pairs + block, part]
                        ux[c, base + i, near : near + 1] = corners[corner.edge + c, m * d + i : m * d + i + 1]
                    kx[base + i, where] = corners[corner.stiff + block, part]
                    if i < d - 1:
                        mx[mass_base + i, where] = corners[corner.mass + block, part]
                for c in range(comps):
                    ux[c, nearest, where] = corners[corner.disp + c, m * d : m * d + d]

    @pl.when(band_even)
    def _():
        place_bands(True)

    @pl.when(jnp.logical_not(band_even))
    def _():
        place_bands(False)

    lane = lax.broadcasted_iota(jnp.int32, (all_layers, width), 1)
    layer = lax.broadcasted_iota(jnp.int32, (all_layers, width), 0)

    raft[...] = jnp.zeros_like(raft)
    payload[...] = jnp.zeros_like(payload)

    @pl.when(band == 0)
    def _():
        sources = [params[...]]
        sources.append(corner_a[pl.ds(corner.params, corner.bearing_rows // 8), :, 0:128].reshape(corner.bearing_rows, 128))
        sources += [params_2[...], params_3[...]]
        known = jnp.concatenate(sources[:bands], axis=0)
        count = known.shape[0]
        within = lax.rem(lax.broadcasted_iota(jnp.int32, (count, 1), 0), corner.bearing_rows)
        shift_a = jnp.where(sector_even, d + rows, d - rows)
        shift_b = jnp.where(sector_even, d - rows, d + rows)
        shift = jnp.where(within < bearings, d, jnp.where(within < 2 * bearings, shift_a, shift_b))
        column = lambda p: known[:, p : p + 1]
        row_of = column(PARAM_ROW).astype(jnp.int32) + shift
        row_of = jnp.where(within < 3 * bearings, row_of, -1)
        row_of = jnp.broadcast_to(row_of, (count, width))
        lane_of = jnp.broadcast_to(column(PARAM_LANE).astype(jnp.int32), (count, width))
        here = lane_of == lax.broadcasted_iota(jnp.int32, (count, width), 1)
        at_node = [jnp.zeros((count, width), F32) for _ in range(comps)]
        for a in range(all_rows):
            hit = row_of == a
            for c in range(comps):
                at_node[c] = jnp.where(hit, ux[c, a, d : d + 1], at_node[c])
        stick = jnp.broadcast_to(column(PARAM_STICK), (count, width))
        force = bearing_law(
            at_node[:2], at_node[2], stick,
            [column(PARAM_SLIP), column(PARAM_SLIP + 1)], [column(PARAM_OLD), column(PARAM_OLD + 1)], column(PARAM_WEIGHT),
        )
        force = [jnp.where(here, f, 0.0) for f in force]
        stiffness = [jnp.where(here & (stick == 1.0), K_STICK, 0.0), jnp.where(here, K_VERT, 0.0)]
        for a in range(all_rows):
            hit = row_of == a
            for q, value in enumerate(force + stiffness):
                raft[q, a : a + 1] = jnp.sum(jnp.where(hit, value, 0.0), axis=0, keepdims=True)
        place_of = lax.broadcasted_iota(jnp.int32, payload.shape, 0) - sector * bands
        col = lax.broadcasted_iota(jnp.int32, payload.shape, 1)
        reply = jnp.zeros(payload.shape, F32)
        for c in range(comps):
            total = jnp.sum(force[c], axis=1, keepdims=True)
            for q in range(bands):
                for j in range(bearings):
                    value = total[q * corner.bearing_rows + j : q * corner.bearing_rows + j + 1]
                    reply = jnp.where((place_of == q) & (col == 64 + c * bearings + j), value, reply)
        payload[...] = reply

    interface = (layer == d - 1) | (layer == d + layers - 1)

    def faces(a, carry):
        k = kx[a]
        k_h = conductance(k, ahead(k, 0))
        kh[a] = k_h
        kr[a] = jnp.where(lane < width - 1, conductance(k, ahead(k, 1)), 0.0)
        ks[a] = conductance(k, kx[jnp.minimum(a + 1, all_rows - 1)])
        for c in range(comps):
            v = ux[c, a]
            flux = jnp.where(interface, k_h * (ahead(v, 0) - v), 0.0)
            change = COMPONENT_SCALE[c] * (flux - behind(flux, 0))
            change = change - jnp.where(layer == d, raft[c, pl.ds(a, 1)], 0.0)
            t0[c, a] = t0[c, a] + change
        return carry

    lax.fori_loop(0, all_rows, faces, 0)
    for a in (d - 1, d + rows - 1):
        for c in range(comps):
            flux = COMPONENT_SCALE[c] * (ks[a] * (ux[c, a + 1] - ux[c, a]))
            t0[c, a] = t0[c, a] + flux
            t0[c, a + 1] = t0[c, a + 1] - flux

    def diagonals(a, carry):
        k_h, k_r = kh[a], kr[a]
        around = k_h + behind(k_h, 0) + k_r + behind(k_r, 1) + ks[a] + ks[a - 1]
        centre = mx[a] - CENTER
        diag[0, a] = (centre + COMPONENT_SCALE[0] * around + jnp.where(layer == d, raft[comps, pl.ds(a, 1)], 0.0)) * (1.0 / SPREAD)
        diag[1, a] = (centre + COMPONENT_SCALE[2] * around + jnp.where(layer == d, raft[comps + 1, pl.ds(a, 1)], 0.0)) * (1.0 / SPREAD)
        return carry

    lax.fori_loop(1, all_rows - 1, diagonals, 0)

    levels = (t0, t1, t2, t3, t4)
    for step in range(1, ITERS + 1):
        src, dst = levels[step - 1], levels[step]
        factor = 1.0 if step == 1 else 2.0

        def apply(a, carry):
            k_h, k_r, k_next, k_back = kh[a], kr[a], ks[a], ks[a - 1]
            for c in range(comps):
                v = src[c, a]
                around = k_next * src[c, a + 1] + k_back * src[c, a - 1]
                around = around + (k_h * ahead(v, 0) + behind(k_h * v, 0))
                around = around + (k_r * ahead(v, 1) + behind(k_r * v, 1))
                centre = diag[0 if c < 2 else 1, a] * v
                if step > 1:
                    centre = 2.0 * centre - levels[step - 2][c, a]
                dst[c, a] = centre - (factor * COMPONENT_SCALE[c] / SPREAD) * around
            return carry

        lax.fori_loop(step, all_rows - step, apply, 0)

    pairs = ((0, 0), (0, 1), (0, 2), (0, 3), (0, 4), (1, 4), (2, 4), (3, 4))
    outs = (b0, b1, b2, b3, b4)

    def products(a, sums):
        for c in range(comps):
            block = [t[c, d + a, own] for t in levels]
            for out, x in zip(outs, block):
                out[c, a] = x
            sums = tuple(
                s + jnp.sum((block[i] * block[j]).reshape(layers // 8, 8, width), axis=0) for s, (i, j) in zip(sums, pairs)
            )
        return sums

    sums = lax.fori_loop(0, rows, products, tuple(jnp.zeros((8, width), F32) for _ in pairs))
    col = lax.broadcasted_iota(jnp.int32, payload.shape, 1)
    reply = payload[...]
    for p, s in enumerate(sums):
        total = jnp.sum(jnp.sum(s, axis=0, keepdims=True), axis=1, keepdims=True)
        reply = jnp.where(col == p, total, reply)
    payload[...] = reply


def combine_kernel(received, b0, b1, b2, b3, b4, increment, residual, force, *, bearings, bands):
    comps, rows, layers, width = b0.shape
    sector = lax.axis_index("sector")
    total = jnp.sum(received[...], axis=0, keepdims=True)
    col = lax.broadcasted_iota(jnp.int32, total.shape, 1)
    mu = [jnp.sum(jnp.where(col == p, total, 0.0), axis=1, keepdims=True) for p in range(8)]
    mu[5] = 2.0 * mu[5] - mu[3]
    mu[6] = 2.0 * mu[6] - mu[2]
    mu[7] = 2.0 * mu[7] - mu[1]
    gram = lambda i, j: mu[0] if i + j == 0 else 0.5 * (mu[i + j] + mu[abs(i - j)])
    table = {(i, j): gram(min(i, j), max(i, j)) for i in range(ITERS) for j in range(i, ITERS + 1)}
    g = lambda i, j: table[min(i, j), max(i, j)]
    zero, one = jnp.zeros_like(mu[0]), jnp.ones_like(mu[0])
    res = [one] + [zero] * ITERS
    direction, inc = list(res), [zero] * (ITERS + 1)
    norm = mu[0]
    for it in range(ITERS):
        image = [CENTER * x for x in direction]
        for i in range(it + 1):
            if i == 0:
                image[1] = image[1] + SPREAD * direction[0]
            else:
                image[i + 1] = image[i + 1] + (0.5 * SPREAD) * direction[i]
                image[i - 1] = image[i - 1] + (0.5 * SPREAD) * direction[i]
        product = sum(
            direction[i] * sum(image[j] * g(i, j) for j in range(it + 2)) for i in range(it + 1)
        )
        alpha = norm / product
        inc = [x + alpha * y for x, y in zip(inc, direction)]
        res = [x - alpha * y for x, y in zip(res, image)]
        if it + 1 < ITERS:
            norm_next = sum(res[i] * sum(res[j] * g(i, j) for j in range(it + 2)) for i in range(it + 2))
            ratio = norm_next / norm
            direction = [x + ratio * y for x, y in zip(res, direction)]
            norm = norm_next
    basis = (b0, b1, b2, b3, b4)
    inc = [jnp.broadcast_to(x, (layers, width)) for x in inc[:ITERS]]
    res = [jnp.broadcast_to(x, (layers, width)) for x in res]

    def combine(a, carry):
        for c in range(comps):
            x = [b[c, a] for b in basis]
            increment[c, a] = sum(y * z for y, z in zip(inc, x))
            residual[c, a] = sum(y * z for y, z in zip(res, x))
        return carry

    lax.fori_loop(0, rows, combine, 0)
    mine = received[pl.ds(sector * bands, 1)]
    for c in range(comps):
        force[c : c + 1] = mine[:, 64 + c * bearings : 64 + (c + 1) * bearings]


def kernel_call(body, outs, operands, scratch=(), smem=()):
    vmem = pl.BlockSpec(memory_space=pltpu.VMEM)
    specs = [pl.BlockSpec(memory_space=pltpu.SMEM) if i in smem else vmem for i in range(len(operands))]
    return pl.pallas_call(
        body,
        out_shape=[jax.ShapeDtypeStruct(s, F32) for s in outs],
        in_specs=specs,
        out_specs=[vmem] * len(outs),
        scratch_shapes=[pltpu.VMEM(s, F32) for s in scratch],
        compiler_params=pltpu.CompilerParams(vmem_limit_bytes=VMEM_LIMIT),
    )(*operands)


def pair_up(i, n):
    return i ^ 1


def pair_down(i, n):
    return (((i + 1) % n) ^ 1) - 1 if ((i + 1) % n) ^ 1 else n - 1


def per_device(
    given_load, displacement, mass_coef, stiffness, bearing_node, stick_state, slip_prev, bearing_old, bearing_weight
):
    comps, rows, layers, radial = displacement.shape
    bearings = bearing_node.shape[0]
    sectors, bands = lax.axis_size("sector"), lax.axis_size("band")
    d = DEPTH
    slab, corner = SectorSlab(comps, layers, bearings), CornerSlab(comps, bearings)

    def along_sector(x, partner):
        return lax.ppermute(
            x, AXES, [(s * bands + b, partner(s, sectors) * bands + b) for s in range(sectors) for b in range(bands)]
        )

    def along_band(x, partner):
        pairs = [(b, partner(b)) for b in range(bands) if 0 <= partner(b) < bands and partner(b) != b]
        return lax.ppermute(x, AXES, [(s * bands + i, s * bands + j) for s in range(sectors) for i, j in pairs])

    inner = lambda b: -1 if b in (0, bands - 1) else ((b + 1) ^ 1) - 1

    field = displacement.shape
    slab_shape, band_shape = (slab.rows, radial), ((2 * comps + 2) * (rows // 2), 2 * d, radial)
    r, slab_a, slab_b, band_a, band_b, own = kernel_call(
        functools.partial(local_kernel, radial=radial),
        [field, slab_shape, slab_shape, band_shape, band_shape, (8, 128)],
        (displacement, given_load, mass_coef, stiffness, bearing_node, stick_state, slip_prev, bearing_old, bearing_weight),
        smem=(4, 5, 6, 7, 8),
    )
    slab_b = along_sector(slab_b, pair_down)
    slab_a = along_sector(slab_a, pair_up)
    band_a = along_band(band_a, lambda b: b ^ 1)
    band_b = along_band(band_b, inner)
    corner_shape = (corner.blocks, 2 * d, radial)
    corner_a, corner_b, params = kernel_call(
        functools.partial(corner_kernel, comps=comps, layers=layers, bearings=bearings),
        [corner_shape, corner_shape, (corner.bearing_rows, 128)],
        (slab_a, slab_b, own),
    )
    corner_a = along_band(corner_a, lambda b: b ^ 1)
    params_2 = along_band(params, lambda b: b ^ 2)
    params_3 = along_band(params, lambda b: b ^ 3)
    corner_b = along_band(corner_b, inner)
    devices = sectors * bands
    extended = (rows + 2 * d, layers + 2 * d, radial)
    *basis, payload = kernel_call(
        functools.partial(power_kernel, bearings=bearings, sectors=sectors, bands=bands),
        [field] * (ITERS + 1) + [(devices, 128)],
        (r, displacement, mass_coef, stiffness, slab_a, slab_b, band_a, band_b, corner_a, corner_b, params, params_2, params_3),
        scratch=[(comps, *extended)] * (ITERS + 2) + [extended] * 5 + [(2, *extended), (comps + 2, rows + 2 * d, radial)],
    )
    received = lax.all_to_all(payload, AXES, 0, 0, tiled=True)
    increment, residual, force = kernel_call(
        functools.partial(combine_kernel, bearings=bearings, bands=bands),
        [field, field, (comps, bearings)],
        (received, *basis),
    )
    return (increment, residual, force)


def solution(mesh):
    return jax.shard_map(
        per_device,
        mesh=mesh,
        in_specs=(
            P(None, "sector", "band", None),
            P(None, "sector", "band", None),
            P("sector", "band", None),
            P("sector", "band", None),
            P(("sector", "band")),
            P(("sector", "band")),
            P(None, ("sector", "band")),
            P(None, ("sector", "band")),
            P(("sector", "band")),
        ),
        out_specs=(
            P(None, "sector", "band", None),
            P(None, "sector", "band", None),
            P(None, ("sector", "band")),
        ),
        check_vma=False,
    )
```

time: 289 us -> 62.2 us (0.22)
  blocking collectives: 200 us -> 12.1 us
  starting transfers between devices: 47 us -> 12.9 us
  between operations: 14.7 us -> 0.72 us
  Pallas kernels: 0 us -> 13.1 us
  other arithmetic: 10.6 us -> 0 us
  waiting for transfers between devices: 10.2 us -> 15.9 us
  local copies, waits for them, and re-layouts: 3.76 us -> 7.13 us
    psum x6 -> x0, blocking collectives: 200 us -> none  [the longest x4 175 us: paired_products(): lax.psum((jnp.sum(residual * residual), jnp.sum(residual * image)), ('sec...]
    ppermute x24 -> x8, starting transfers between devices: 47 us -> 12.9 us  [the longest x2 6.58 us: along_sector(): lax.ppermute(x, AXES, [(s * bands + b, partner(s, sectors) * bands + b) f...]
    pallas_call x0 -> x4, Pallas kernels: none -> 13.1 us  [kernel_call(): pl.pallas_call(body, out_shape=[jax.ShapeDtypeStruct(s, F32) for s in out...]
    all_to_all x0 -> x1, blocking collectives: none -> 12.1 us  [per_device(): received = lax.all_to_all(payload, AXES, 0, 0, tiled=True)]
    ppermute x24 -> x8, waiting for transfers between devices: 10.2 us -> 15.9 us  [the longest x2 13.3 us: along_sector(): lax.ppermute(x, AXES, [(s * bands + b, partner(s, sectors) * bands + b) f...]
    unnamed x25 -> x24, local copies, waits for them, and re-layouts: 1.77 us -> 7.13 us
    reduce_sum x4 -> x0, other arithmetic: 4.66 us -> none  [paired_products(): jnp.sum(residual * image)]
  transfers between devices with their start and end apart: 24 -> 8, of which waited for: 5 -> 2; matrix products, arithmetic and copies ran while one was open for 1% -> 0% of each run, Pallas kernels for 0% -> 0%
where the time goes in v1:
time: 62.2 us; the launch traced here: 61.9 us
  waiting for transfers between devices  15.9 us (26%)
  Pallas kernels  13.1 us (21%)
  starting transfers between devices  12.9 us (21%)
  blocking collectives  12.1 us (19%)
  local copies, waits for them, and re-layouts  7.13 us (11%)
  between operations  0.72 us (1%)
    ppermute x2, waiting for transfers between devices, along_sector(): lax.ppermute(x, AXES, [(s * bands + b, partner(s, sectors) * bands + b) f...  13.3 us
    pallas_call x4, Pallas kernels, kernel_call(): pl.pallas_call(body, out_shape=[jax.ShapeDtypeStruct(s, F32) for s in out...  13.1 us
    all_to_all x1, blocking collectives, per_device(): received = lax.all_to_all(payload, AXES, 0, 0, tiled=True)  12.1 us
    unnamed x24, local copies, waits for them, and re-layouts  7.13 us
    ppermute x2, starting transfers between devices, along_sector(): lax.ppermute(x, AXES, [(s * bands + b, partner(s, sectors) * bands + b) f...  6.58 us
    ppermute x6, starting transfers between devices, along_band(): lax.ppermute(x, AXES, [(s * bands + i, s * bands + j) for s in range(sect...  6.36 us
    ppermute x6, waiting for transfers between devices, along_band(): lax.ppermute(x, AXES, [(s * bands + i, s * bands + j) for s in range(sect...  2.64 us
  transfers between devices with their start and end apart: 8, of which 2 were waited for; matrix products, arithmetic and copies ran while one was open for 0% of the time, Pallas kernels for 0%

profile of v1, /device:TPU:0, one launch (start us, length us, event | category | flops | bytes accessed | tf_op | source)
XLA Modules:
  0.0 61.9 jit_solution(4063087256579074015)
XLA Ops:
  0.6 0.0 copy-start
  0.6 1.0 %copy-done = f32[3,8,16,256]{3,2,1,0:T(8,128)S(1)} copy-done((f32[3,8,16,256]{3,2,1,0:T(8,128)S(1)}, f32[3,8,16,256]{3,2,1,0:T(8,128)}, u32[]{:S(2)}) %copy-start) | copy-done | bytes 393240
  1.6 0.0 copy-start.2
  1.6 0.9 %copy-done.2 = f32[8,16,256]{2,1,0:T(8,128)S(1)} copy-done((f32[8,16,256]{2,1,0:T(8,128)S(1)}, f32[8,16,256]{2,1,0:T(8,128)}, u32[]{:S(2)}) %copy-start.2) | copy-done | bytes 131096
  2.5 0.0 copy-start.4
  2.5 0.9 %copy-done.4 = f32[8,16,256]{2,1,0:T(8,128)S(1)} copy-done((f32[8,16,256]{2,1,0:T(8,128)S(1)}, f32[8,16,256]{2,1,0:T(8,128)}, u32[]{:S(2)}) %copy-start.4) | copy-done | bytes 131096
  3.4 0.0 copy-start.6
  3.4 1.0 %copy-done.6 = f32[3,8,16,256]{3,2,1,0:T(8,128)S(1)} copy-done((f32[3,8,16,256]{3,2,1,0:T(8,128)S(1)}, f32[3,8,16,256]{3,2,1,0:T(8,128)}, u32[]{:S(2)}) %copy-start.6) | copy-done | bytes 393240
  4.4 0.0 copy-start.7
  4.4 0.7 %copy-done.7 = f32[2,4]{1,0:T(2,128)S(1)} copy-done((f32[2,4]{1,0:T(2,128)S(1)}, f32[2,4]{1,0:T(2,128)}, u32[]{:S(2)}) %copy-start.7) | copy-done | bytes 56
  5.1 0.0 copy-start.8
  5.1 0.7 %copy-done.8 = f32[2,4]{1,0:T(2,128)S(1)} copy-done((f32[2,4]{1,0:T(2,128)S(1)}, f32[2,4]{1,0:T(2,128)}, u32[]{:S(2)}) %copy-start.8) | copy-done | bytes 56
  5.8 0.0 copy-start.9
  5.8 0.7 %copy-done.9 = s32[4]{0:T(128)S(1)} copy-done((s32[4]{0:T(128)S(1)}, s32[4]{0:T(128)}, u32[]{:S(2)}) %copy-start.9) | copy-done | bytes 40
  6.5 0.0 copy-start.10
  6.5 0.7 %copy-done.10 = s32[4]{0:T(128)S(1)} copy-done((s32[4]{0:T(128)S(1)}, s32[4]{0:T(128)}, u32[]{:S(2)}) %copy-start.10) | copy-done | bytes 40
  7.1 0.0 copy-start.11
  7.1 0.7 %copy-done.11 = f32[4]{0:T(128)S(1)} copy-done((f32[4]{0:T(128)S(1)}, f32[4]{0:T(128)}, u32[]{:S(2)}) %copy-start.11) | copy-done | bytes 40
  7.8 1.5 %shard_map.112 = (f32[3,8,16,256]{3,2,1,0:T(8,128)S(1)}, f32[384,256]{1,0:T(8,128)S(1)}, f32[384,256]{1,0:T(8,128)S(1)}, f32[32,8,256]{2,1,0:T(8,128)S(1)}, f32[...) custom-call(f32[3,8,16,256]{3,2,1,0:T(8,128)S(1)} %copy-done, f32[3,8,16,256]{3,2,1,0:T(8,128)S(1)} %copy-done.6, ...), custom_call_target="tpu_custom_call" | custom-call | tf_op jit(solution)/shard_map/pallas_call | solution.py:472
  9.3 3.0 %collective-permute-start = (f32[384,256]{1,0:T(8,128)S(1)}, f32[384,256]{1,0:T(8,128)S(1)}, u32[]{:S(2)}, u32[]{:S(2)}) collective-permute-start(f32[384,256]{1,0:T(8,128)S(1)} %get-tuple-element.19), channel_id=1, source_target_pairs={{0,4},{1,5},{2,6},{3,7},{4,0},{5,1},{6,2},{7,3},{8,12},{9,13},{10,... | collective-permute-start | bytes 1179656 | tf_op jit(solution)/shard_map/ppermute | solution.py:500
  12.3 3.6 %collective-permute-start.1 = (f32[384,256]{1,0:T(8,128)S(1)}, f32[384,256]{1,0:T(8,128)S(1)}, u32[]{:S(2)}, u32[]{:S(2)}) collective-permute-start(f32[384,256]{1,0:T(8,128)S(1)} %get-tuple-element.20), channel_id=1, source_target_pairs={{0,28},{1,29},{2,30},{3,31},{4,8},{5,9},{6,10},{7,11},{8,4},{9,5},... | collective-permute-start | bytes 1179656 | tf_op jit(solution)/shard_map/ppermute | solution.py:500
  15.9 0.0 collective-permute-start.2
  15.9 0.7 %collective-permute-start.3 = (f32[32,8,256]{2,1,0:T(8,128)S(1)}, f32[32,8,256]{2,1,0:T(8,128)S(1)}, u32[]{:S(2)}, u32[]{:S(2)}) collective-permute-start(f32[32,8,256]{2,1,0:T(8,128)S(1)} %get-tuple-element.22), channel_id=1, source_target_pairs={{1,2},{2,1},{5,6},{6,5},{9,10},{10,9},{13,14},{14,13},{17,18},{18,... | collective-permute-start | bytes 786440 | tf_op jit(solution)/shard_map/ppermute | solution.py:506
  16.6 13.3 %collective-permute-done.slab_a = f32[384,256]{1,0:T(8,128)S(1)} collective-permute-done((f32[384,256]{1,0:T(8,128)S(1)}, f32[384,256]{1,0:T(8,128)S(1)}, u32[]{:S(2)}, u32[]{:S(2)}) %collective-permute-start) | collective-permute-done | bytes 393248 | tf_op jit(solution)/shard_map/ppermute | solution.py:500
  29.8 0.0 collective-permute-done.1.slab_b
  29.8 0.0 copy-start.1
  29.8 0.0 copy-start.3
  29.9 0.0 copy-start.5
  29.9 0.1 shard_map.113
  29.9 0.1 collective-permute-start.4
  30.0 0.8 %collective-permute-start.5 = (f32[28,8,256]{2,1,0:T(8,128)S(1)}, f32[28,8,256]{2,1,0:T(8,128)S(1)}, u32[]{:S(2)}, u32[]{:S(2)}) collective-permute-start(f32[28,8,256]{2,1,0:T(8,128)S(1)} %get-tuple-element.25), channel_id=1, source_target_pairs={{1,2},{2,1},{5,6},{6,5},{9,10},{10,9},{13,14},{14,13},{17,18},{18,... | collective-permute-start | bytes 688136 | tf_op jit(solution)/shard_map/ppermute | solution.py:506
  30.8 1.8 %collective-permute-start.7 = (f32[16,128]{1,0:T(8,128)S(1)}, f32[16,128]{1,0:T(8,128)S(1)}, u32[]{:S(2)}, u32[]{:S(2)}) collective-permute-start(f32[16,128]{1,0:T(8,128)S(1)} %get-tuple-element.26.params), channel_id=1, source_target_pairs={{0,3},{1,2},{2,1},{3,0},{4,7},{5,6},{6,5},{7,4},{8,11},{9,10},{10,... | collective-permute-start | bytes 24584 | tf_op jit(solution)/shard_map/ppermute | solution.py:506
  32.6 0.0 collective-permute-done.2.band_a
  32.6 3.0 %collective-permute-start.6 = (f32[16,128]{1,0:T(8,128)S(1)}, f32[16,128]{1,0:T(8,128)S(1)}, u32[]{:S(2)}, u32[]{:S(2)}) collective-permute-start(f32[16,128]{1,0:T(8,128)S(1)} %get-tuple-element.26.params), channel_id=1, source_target_pairs={{0,2},{1,3},{2,0},{3,1},{4,6},{5,7},{6,4},{7,5},{8,10},{9,11},{10,... | collective-permute-start | bytes 24584 | tf_op jit(solution)/shard_map/ppermute | solution.py:506
  35.6 0.0 collective-permute-done.3.band_b
  35.6 0.0 collective-permute-done.7.params_3
  35.6 2.6 %collective-permute-done.6.params_2 = f32[16,128]{1,0:T(8,128)S(1)} collective-permute-done((f32[16,128]{1,0:T(8,128)S(1)}, f32[16,128]{1,0:T(8,128)S(1)}, u32[]{:S(2)}, u32[]{:S(2)}) %collective-permute-start.6) | collective-permute-done | bytes 8224 | tf_op jit(solution)/shard_map/ppermute | solution.py:506
  38.3 0.0 collective-permute-done.4.corner_a
  38.3 0.0 collective-permute-done.5.corner_b
  38.3 0.0 copy-done.1
  38.3 0.0 copy-done.3
  38.3 0.0 copy-done.5
  38.3 10.2 %shard_map.114 = (f32[3,8,16,256]{3,2,1,0:T(8,128)S(1)}, f32[3,8,16,256]{3,2,1,0:T(8,128)S(1)}, f32[3,8,16,256]{3,2,1,0:T(8,128)S(1)}, f32[3,8,16,256]{3,2,1,0:T...) custom-call(f32[3,8,16,256]{3,2,1,0:T(8,128)S(1)} %get-tuple-element.18.r, ...), custom_call_target="tpu_custom_call" | custom-call | tf_op jit(solution)/shard_map/pallas_call | solution.py:472
  48.5 12.1 %all_to_all.11 = f32[32,1,128]{2,1,0:T(1,128)S(1)} all-to-all(f32[32,1,128]{2,1,0:T(1,128)S(1)} %bitcast.5), channel_id=1, replica_groups=mesh['sector'=8,'band'=4] {'sector','band'}, dimensions={0} | all-to-all | bytes 32768 | tf_op jit(solution)/shard_map/all_to_all | solution.py:540
  60.6 1.3 %shard_map.115 = (f32[3,8,16,256]{3,2,1,0:T(8,128)}, f32[3,8,16,256]{3,2,1,0:T(8,128)}, f32[3,4]{1,0:T(4,128)}) custom-call(f32[32,128]{1,0:T(8,128)S(1)} %bitcast.4, f32[3,8,16,256]{3,2,1,0:T(8,128)S(1)} %get-tuple-element.28.b0, f32[3,8,16,256]{3,2,1,0:T(8,128)S(1)} %get-tuple-element.29.b1, f32[3,8,16,256]{3,2,1,0:T(8,128)S(1)} %get-tuple-element.30.b2, ...), custom_call_target="tpu_custom_call" | custom-call | tf_op jit(solution)/shard_map/pallas_call | solution.py:472
Async XLA Ops:
  0.6 1.0 %copy-start = (f32[3,8,16,256]{3,2,1,0:T(8,128)S(1)}, f32[3,8,16,256]{3,2,1,0:T(8,128)}, u32[]{:S(2)}) copy-start(f32[3,8,16,256]{3,2,1,0:T(8,128)} %u.3) | copy-start | bytes 1179652
  1.6 0.9 %copy-start.2 = (f32[8,16,256]{2,1,0:T(8,128)S(1)}, f32[8,16,256]{2,1,0:T(8,128)}, u32[]{:S(2)}) copy-start(f32[8,16,256]{2,1,0:T(8,128)} %mass.3) | copy-start | bytes 393220
  2.5 0.9 %copy-start.4 = (f32[8,16,256]{2,1,0:T(8,128)S(1)}, f32[8,16,256]{2,1,0:T(8,128)}, u32[]{:S(2)}) copy-start(f32[8,16,256]{2,1,0:T(8,128)} %stiff.3) | copy-start | bytes 393220
  3.4 1.0 %copy-start.6 = (f32[3,8,16,256]{3,2,1,0:T(8,128)S(1)}, f32[3,8,16,256]{3,2,1,0:T(8,128)}, u32[]{:S(2)}) copy-start(f32[3,8,16,256]{3,2,1,0:T(8,128)} %load.1) | copy-start | bytes 1179652
  4.4 0.7 %copy-start.7 = (f32[2,4]{1,0:T(2,128)S(1)}, f32[2,4]{1,0:T(2,128)}, u32[]{:S(2)}) copy-start(f32[2,4]{1,0:T(2,128)} %slip.1) | copy-start | bytes 100
  5.1 0.7 %copy-start.8 = (f32[2,4]{1,0:T(2,128)S(1)}, f32[2,4]{1,0:T(2,128)}, u32[]{:S(2)}) copy-start(f32[2,4]{1,0:T(2,128)} %old.1) | copy-start | bytes 100
  5.8 0.7 %copy-start.9 = (s32[4]{0:T(128)S(1)}, s32[4]{0:T(128)}, u32[]{:S(2)}) copy-start(s32[4]{0:T(128)} %node.1) | copy-start | bytes 52
  6.5 0.7 %copy-start.10 = (s32[4]{0:T(128)S(1)}, s32[4]{0:T(128)}, u32[]{:S(2)}) copy-start(s32[4]{0:T(128)} %stick.1) | copy-start | bytes 52
  7.1 0.7 %copy-start.11 = (f32[4]{0:T(128)S(1)}, f32[4]{0:T(128)}, u32[]{:S(2)}) copy-start(f32[4]{0:T(128)} %weight.1) | copy-start | bytes 52
  9.3 20.5 %collective-permute-start = (f32[384,256]{1,0:T(8,128)S(1)}, f32[384,256]{1,0:T(8,128)S(1)}, u32[]{:S(2)}, u32[]{:S(2)}) collective-permute-start(f32[384,256]{1,0:T(8,128)S(1)} %get-tuple-element.19), channel_id=1, source_target_pairs={{0,4},{1,5},{2,6},{3,7},{4,0},{5,1},{6,2},{7,3},{8,12},{9,13},{10,... | collective-permute-start | bytes 1179656 | tf_op jit(solution)/shard_map/ppermute | solution.py:500
  12.3 17.5 %collective-permute-start.1 = (f32[384,256]{1,0:T(8,128)S(1)}, f32[384,256]{1,0:T(8,128)S(1)}, u32[]{:S(2)}, u32[]{:S(2)}) collective-permute-start(f32[384,256]{1,0:T(8,128)S(1)} %get-tuple-element.20), channel_id=1, source_target_pairs={{0,28},{1,29},{2,30},{3,31},{4,8},{5,9},{6,10},{7,11},{8,4},{9,5},... | collective-permute-start | bytes 1179656 | tf_op jit(solution)/shard_map/ppermute | solution.py:500
  15.9 16.7 %collective-permute-start.2 = (f32[32,8,256]{2,1,0:T(8,128)S(1)}, f32[32,8,256]{2,1,0:T(8,128)S(1)}, u32[]{:S(2)}, u32[]{:S(2)}) collective-permute-start(f32[32,8,256]{2,1,0:T(8,128)S(1)} %get-tuple-element.21), channel_id=1, source_target_pairs={{0,1},{1,0},{2,3},{3,2},{4,5},{5,4},{6,7},{7,6},{8,9},{9,8},{10,11... | collective-permute-start | bytes 786440 | tf_op jit(solution)/shard_map/ppermute | solution.py:506
  15.9 19.8 %collective-permute-start.3 = (f32[32,8,256]{2,1,0:T(8,128)S(1)}, f32[32,8,256]{2,1,0:T(8,128)S(1)}, u32[]{:S(2)}, u32[]{:S(2)}) collective-permute-start(f32[32,8,256]{2,1,0:T(8,128)S(1)} %get-tuple-element.22), channel_id=1, source_target_pairs={{1,2},{2,1},{5,6},{6,5},{9,10},{10,9},{13,14},{14,13},{17,18},{18,... | collective-permute-start | bytes 786440 | tf_op jit(solution)/shard_map/ppermute | solution.py:506
  29.8 8.4 %copy-start.1 = (f32[3,8,16,256]{3,2,1,0:T(8,128)S(1)}, f32[3,8,16,256]{3,2,1,0:T(8,128)}, u32[]{:S(2)}) copy-start(f32[3,8,16,256]{3,2,1,0:T(8,128)} %u.3) | copy-start | bytes 1179652
  29.8 8.4 %copy-start.3 = (f32[8,16,256]{2,1,0:T(8,128)S(1)}, f32[8,16,256]{2,1,0:T(8,128)}, u32[]{:S(2)}) copy-start(f32[8,16,256]{2,1,0:T(8,128)} %mass.3) | copy-start | bytes 393220
  29.9 8.4 %copy-start.5 = (f32[8,16,256]{2,1,0:T(8,128)S(1)}, f32[8,16,256]{2,1,0:T(8,128)}, u32[]{:S(2)}) copy-start(f32[8,16,256]{2,1,0:T(8,128)} %stiff.3) | copy-start | bytes 393220
  29.9 8.3 %collective-permute-start.4 = (f32[28,8,256]{2,1,0:T(8,128)S(1)}, f32[28,8,256]{2,1,0:T(8,128)S(1)}, u32[]{:S(2)}, u32[]{:S(2)}) collective-permute-start(f32[28,8,256]{2,1,0:T(8,128)S(1)} %get-tuple-element.24), channel_id=1, source_target_pairs={{0,1},{1,0},{2,3},{3,2},{4,5},{5,4},{6,7},{7,6},{8,9},{9,8},{10,11... | collective-permute-start | bytes 688136 | tf_op jit(solution)/shard_map/ppermute | solution.py:506
  30.0 8.3 %collective-permute-start.5 = (f32[28,8,256]{2,1,0:T(8,128)S(1)}, f32[28,8,256]{2,1,0:T(8,128)S(1)}, u32[]{:S(2)}, u32[]{:S(2)}) collective-permute-start(f32[28,8,256]{2,1,0:T(8,128)S(1)} %get-tuple-element.25), channel_id=1, source_target_pairs={{1,2},{2,1},{5,6},{6,5},{9,10},{10,9},{13,14},{14,13},{17,18},{18,... | collective-permute-start | bytes 688136 | tf_op jit(solution)/shard_map/ppermute | solution.py:506
  30.8 4.8 %collective-permute-start.7 = (f32[16,128]{1,0:T(8,128)S(1)}, f32[16,128]{1,0:T(8,128)S(1)}, u32[]{:S(2)}, u32[]{:S(2)}) collective-permute-start(f32[16,128]{1,0:T(8,128)S(1)} %get-tuple-element.26.params), channel_id=1, source_target_pairs={{0,3},{1,2},{2,1},{3,0},{4,7},{5,6},{6,5},{7,4},{8,11},{9,10},{10,... | collective-permute-start | bytes 24584 | tf_op jit(solution)/shard_map/ppermute | solution.py:506
  32.6 5.7 %collective-permute-start.6 = (f32[16,128]{1,0:T(8,128)S(1)}, f32[16,128]{1,0:T(8,128)S(1)}, u32[]{:S(2)}, u32[]{:S(2)}) collective-permute-start(f32[16,128]{1,0:T(8,128)S(1)} %get-tuple-element.26.params), channel_id=1, source_target_pairs={{0,2},{1,3},{2,0},{3,1},{4,6},{5,7},{6,4},{7,5},{8,10},{9,11},{10,... | collective-permute-start | bytes 24584 | tf_op jit(solution)/shard_map/ppermute | solution.py:506

commit v2 on v1

v2 whole, which is shorter than its diff:
```python
import functools

import jax
import jax.numpy as jnp
from jax import lax
from jax.experimental import pallas as pl
from jax.experimental.pallas import tpu as pltpu
from jax.sharding import PartitionSpec as P

ITERS = 4
DEPTH = ITERS

K_STICK = 4.0
K_VERT = 8.0
MU_FAST = 0.15
MU_SLOW = 0.04
RATE_GAIN = 2.0
RATE_DECAY = 2.0
V_FLOOR = 0.05
COMPONENT_SCALE = (1.0, 1.0, 2.0)

STATS = 1 + 2 * (ITERS - 1)
TINY = 1e-30
FLOOR = 0.25

AXES = ("sector", "band")
F32 = jnp.float32
PARAM_ROW, PARAM_LANE, PARAM_STICK, PARAM_SLIP, PARAM_OLD, PARAM_WEIGHT = (0, 1, 2, 3, 5, 7)
PARAMS = 8
PARAM_AT = 32
FORCE_AT = 64
VMEM_LIMIT = 48 * 1024 * 1024
VMEM_WHOLE = 64 * 1024 * 1024 - 65536


def conductance(left, right):
    return 2.0 * left * right / jnp.maximum(left + right, FLOOR)


def ahead(x, axis):
    return pltpu.roll(x, x.shape[axis] - 1, axis)


def behind(x, axis):
    return pltpu.roll(x, 1, axis)


def round_up(n, multiple):
    return -(-n // multiple) * multiple


def put_band(out, at, r, u, stiff, mass, top):
    comps, rows, layers, _ = r.shape
    fields = [r.at[c] for c in range(comps)] + [u.at[c] for c in range(comps)] + [stiff, mass]
    for f, field in enumerate(fields):
        for pair in range(rows // 2):
            planes = [field[2 * pair + i] for i in range(2)]
            high = jnp.concatenate([x[layers - DEPTH :] for x in planes], axis=0)
            low = jnp.concatenate([x[:DEPTH] for x in planes], axis=0)
            out[at + f * (rows // 2) + pair] = jnp.where(top, high, low)


class SectorSlab:
    def __init__(self, comps, layers):
        d = DEPTH
        self.layers = layers
        self.stiff = comps * d * layers
        self.mass = self.stiff + d * layers
        self.disp = self.mass + (d - 1) * layers
        self.low = self.disp + comps * layers
        self.high = self.low + comps * d
        self.rows = round_up(self.high + comps * d, 8)

    def residual_at(self, c, i):
        return (c * DEPTH + i) * self.layers


def parts_of(work):
    comps = (work.shape[0] - 5) // 2
    return work.at[0:comps], work.at[comps : 2 * comps], work.at[2 * comps : 2 * comps + 3], work.at[2 * comps + 3], work.at[2 * comps + 4]


def local_kernel(
    u_far, load_far, mass_far, stiff_far, node_far, stick_far, slip_far, old_far, weight_far,
    work, slab_a, slab_b, band_b,
    load, node, stick, slip, old, weight, arrived, *, radial,
):
    comps, rows, layers, width = load.shape
    d = DEPTH
    r, u, cond, mass, stiff = parts_of(work)
    fields = ((stiff_far, stiff), (u_far, u), (mass_far, mass), (load_far, load))
    small = ((node_far, node), (stick_far, stick), (slip_far, slip), (old_far, old), (weight_far, weight))
    moves = [pltpu.make_async_copy(src, dst, arrived.at[n]) for n, (src, dst) in enumerate(fields + small)]
    for move in moves:
        move.start()
    lane = lax.broadcasted_iota(jnp.int32, (layers, width), 1)
    layer = lax.broadcasted_iota(jnp.int32, (layers, width), 0)
    moves[0].wait()
    for a in range(rows):
        k = stiff[a]
        cond[0, a] = jnp.where(lane < width - 1, conductance(k, ahead(k, 1)), 0.0)
        cond[1, a] = jnp.where(layer < layers - 1, conductance(k, ahead(k, 0)), 0.0)
        cond[2, a] = conductance(k, stiff[a + 1]) if a + 1 < rows else jnp.zeros((layers, width), F32)
    for move in moves[1 : len(fields)]:
        move.wait()
    before = [None] * comps
    for a in range(rows):
        k_r, k_h, k_s = cond[0, a], cond[1, a], cond[2, a]
        m = mass[a]
        for c in range(comps):
            v = u[c, a]
            flux_r = k_r * (ahead(v, 1) - v)
            flux_h = k_h * (ahead(v, 0) - v)
            total = flux_r - behind(flux_r, 1) + flux_h - behind(flux_h, 0)
            if before[c] is not None:
                total = total - before[c]
            if a + 1 < rows:
                before[c] = k_s * (u[c, a + 1] - v)
                total = total + before[c]
            r[c, a] = load[c, a] - m * v + COMPONENT_SCALE[c] * total

    for move in moves[len(fields) :]:
        move.wait()
    col = lax.broadcasted_iota(jnp.int32, (8, 128), 1)
    tile = jnp.zeros((8, 128), F32)
    for j in range(node.shape[0]):
        at = node[j] // radial
        values = {
            PARAM_ROW: at.astype(F32),
            PARAM_LANE: (node[j] - at * radial).astype(F32),
            PARAM_STICK: stick[j].astype(F32),
            PARAM_SLIP: slip[0, j],
            PARAM_SLIP + 1: slip[1, j],
            PARAM_OLD: old[0, j],
            PARAM_OLD + 1: old[1, j],
            PARAM_WEIGHT: weight[j],
        }
        for p, value in values.items():
            tile = jnp.where(col == PARAM_AT + PARAMS * j + p, value, tile)
    cond[2, rows - 1, 0:8, 0:128] = tile

    slab = SectorSlab(comps, layers)
    even = lax.rem(lax.axis_index("sector"), 2) == 0
    for out, upper in ((slab_a, even), (slab_b, jnp.logical_not(even))):
        first = jnp.where(upper, rows - d, 0)
        for i in range(d):
            for c in range(comps):
                out[pl.ds(slab.residual_at(c, i), layers)] = r[c, first + i]
                out[pl.ds(slab.low + c * d + i, 1)] = u[c, first + i, 0:1]
                out[pl.ds(slab.high + c * d + i, 1)] = u[c, first + i, layers - 1 : layers]
            out[pl.ds(slab.stiff + i * layers, layers)] = stiff[first + i]
        for i in range(d - 1):
            out[pl.ds(slab.mass + i * layers, layers)] = mass[jnp.where(upper, rows - (d - 1), 0) + i]
        for c in range(comps):
            out[pl.ds(slab.disp + c * layers, layers)] = u[c, jnp.where(upper, rows - 1, 0)]
        end = slab.high + comps * d
        if slab.rows > end:
            out[pl.ds(end, slab.rows - end)] = jnp.zeros((slab.rows - end, width), F32)

    even = lax.rem(lax.axis_index("band"), 2) == 0
    put_band(band_b, 0, r, u, stiff, mass, jnp.logical_not(even))


REACH = [DEPTH] + [max(DEPTH - n, 1) for n in range(2, DEPTH + 1)]


class Wedge:
    counts = REACH
    starts = [sum(REACH[:n]) for n in range(DEPTH)]
    height = round_up(sum(REACH), 8)

    def __init__(self, comps):
        self.stiff, self.mass, self.disp = comps, comps + 1, comps + 2
        self.blocks = 2 * comps + 2


def padded_block(parts):
    parts = list(parts)
    spare = Wedge.height - sum(p.shape[0] for p in parts)
    if spare:
        parts.append(jnp.zeros((spare, parts[0].shape[1]), F32))
    return jnp.concatenate(parts, axis=0)


def put_wedge(out, at, comps, layers, top, residual, stiff, mass, disp, edges):
    wedge, d = Wedge(comps), DEPTH
    sources = [functools.partial(residual, c) for c in range(comps)] + [stiff, mass]
    for f, source in enumerate(sources):
        planes = [source(n) for n in range(1, d + 1)]
        high = padded_block(p[layers - k :] for p, k in zip(planes, wedge.counts))
        low = padded_block(p[:k] for p, k in zip(planes, wedge.counts))
        out[at + f] = jnp.where(top, high, low)
    for c in range(comps):
        row, rims = disp(c), [edges(c, n) for n in range(1, d + 1)]
        high = padded_block([row[layers - d :]] + [rim[1] for rim in rims])
        low = padded_block([row[:d]] + [rim[0] for rim in rims])
        out[at + wedge.disp + c] = jnp.where(top, high, low)


def corner_kernel(slab_a, slab_b, work, survey, band_b, corner_a, corner_b, *, comps, layers):
    d = DEPTH
    slab, wedge = SectorSlab(comps, layers), Wedge(comps)
    band_even = lax.rem(lax.axis_index("band"), 2) == 0
    sector_even = lax.rem(lax.axis_index("sector"), 2) == 0
    for n, (side, above) in enumerate(((slab_a, sector_even), (slab_b, jnp.logical_not(sector_even)))):

        def plane(offset, side=side):
            return side[pl.ds(pl.multiple_of(offset, 8), layers)]

        def step(n, count, above=above):
            return jnp.where(above, n - 1, count - n)

        for out, top in ((corner_a, band_even), (corner_b, jnp.logical_not(band_even))):
            put_wedge(
                out,
                n * wedge.blocks,
                comps,
                layers,
                top,
                lambda c, n: plane(slab.residual_at(c, step(n, d))),
                lambda n: plane(slab.stiff + step(n, d) * layers),
                lambda n: plane(slab.mass + step(min(n, d - 1), d - 1) * layers),
                lambda c: plane(slab.disp + c * layers),
                lambda c, n: [side[pl.ds(at + c * d + step(n, d), 1)] for at in (slab.low, slab.high)],
            )
    r, u, _, mass, stiff = parts_of(work)
    put_band(corner_a, 2 * wedge.blocks, r, u, stiff, mass, band_even)


def dot(x, y):
    return jnp.sum((x * y).reshape(x.shape[0] // 8, 8, x.shape[1]), axis=0)


def total_of(x):
    return jnp.sum(jnp.sum(x, axis=0, keepdims=True), axis=1, keepdims=True)


def survey_kernel(work, row, image, basis_1, basis_2):
    r, _, cond, mass, _ = parts_of(work)
    comps, rows, layers, width = r.shape
    zero = jnp.zeros((8, width), F32)

    def apply(src):
        norm, product = zero, zero
        for a in range(rows):
            k_r, k_h, k_next = cond[0, a], cond[1, a], cond[2, a]
            for c in range(comps):
                v = src[c, a]
                flux_r = k_r * (ahead(v, 1) - v)
                flux_h = k_h * (ahead(v, 0) - v)
                total = flux_r - behind(flux_r, 1) + flux_h - behind(flux_h, 0)
                if a + 1 < rows:
                    total = total + k_next * (src[c, a + 1] - v)
                if a:
                    total = total - cond[2, a - 1] * (v - src[c, a - 1])
                out = mass[a] * v - COMPONENT_SCALE[c] * total
                image[c, a] = out
                norm, product = norm + dot(v, v), product + dot(v, out)
        return total_of(norm), total_of(product)

    level, back, weight_here, stats = r, None, None, []
    outs = (basis_1, basis_2)
    norm_back = None
    for step in range(ITERS - 1):
        norm, product = apply(level)
        if step:
            stats.append(norm / jnp.maximum(norm_back, TINY))
        else:
            weight_here = norm
        stats.append(product / jnp.maximum(norm, TINY))
        if step < ITERS - 2:
            a_k = jnp.broadcast_to(stats[-1], (layers, width))
            c_k = jnp.broadcast_to(stats[-2], (layers, width)) if step else None
            for a in range(rows):
                for c in range(comps):
                    x = image[c, a] - a_k * level[c, a]
                    outs[step][c, a] = x if back is None else x - c_k * back[c, a]
            back, level, norm_back = level, outs[step], norm
        else:
            a_k = jnp.broadcast_to(stats[-1], (layers, width))
            c_k = jnp.broadcast_to(stats[-2], (layers, width))
            last = zero
            for a in range(rows):
                for c in range(comps):
                    x = image[c, a] - a_k * level[c, a] - c_k * back[c, a]
                    last = last + dot(x, x)
            stats.append(total_of(last) / jnp.maximum(norm, TINY))
    col = lax.broadcasted_iota(jnp.int32, (8, 128), 1)
    tile = jnp.where(col == 0, weight_here, 0.0)
    for n, value in enumerate(stats):
        tile = jnp.where(col == 1 + n, weight_here * value, tile)
    tile = tile + cond[2, rows - 1, 0:8, 0:128]
    for n in range(row.shape[0] // 8):
        row[8 * n : 8 * n + 8] = tile


def coefficients(survey):
    total = jnp.sum(survey, axis=0, keepdims=True)
    col = lax.broadcasted_iota(jnp.int32, total.shape, 1)
    pick = lambda n: jnp.sum(jnp.where(col == n, total, 0.0), axis=1, keepdims=True)
    weight = jnp.maximum(pick(0), TINY)
    stats = [pick(n) / weight for n in range(1, STATS)]
    a, c = stats[0::2], stats[1::2]
    return a + [a[-1]], [None] + c


def bearing_law(moved, vertical, stick, slip, old, weight):
    trial = [K_STICK * (moved[i] - slip[i]) for i in range(2)]
    rate = [RATE_GAIN * (moved[i] - old[i]) for i in range(2)]
    slip_speed = jnp.sqrt(rate[0] * rate[0] + rate[1] * rate[1] + V_FLOOR * V_FLOOR)
    friction = MU_FAST - (MU_FAST - MU_SLOW) * jnp.exp(-RATE_DECAY * slip_speed)
    capacity = friction * weight
    magnitude = jnp.sqrt(trial[0] * trial[0] + trial[1] * trial[1])
    largest = jnp.maximum(magnitude, capacity)
    forces = [jnp.where(stick == 1.0, t, capacity * t / largest) for t in trial]
    return forces + [K_VERT * vertical]


def gram_pairs():
    return [(i, j) for i in range(ITERS) for j in range(i, ITERS + 1)]


def power_kernel(
    work, slab_a, slab_b, band_b, corner_a, corner_b, survey,
    b0, b1, b2, b3, b4, payload,
    t0, t1, t2, t3, t4, ux, kx, mx, ks, kh, kr, diag, raft,
    *, bearings, sectors, bands,
):
    r, u, _, mass, stiff = parts_of(work)
    comps, rows, layers, width = r.shape
    d = DEPTH
    slab, wedge = SectorSlab(comps, layers), Wedge(comps)
    sector, band = lax.axis_index("sector"), lax.axis_index("band")
    sector_even = lax.rem(sector, 2) == 0
    band_even = lax.rem(band, 2) == 0
    all_rows, all_layers = rows + 2 * d, layers + 2 * d
    own = pl.ds(d, layers)

    def place(a, carry):
        for c in range(comps):
            t0[c, d + a, own] = r[c, a]
            ux[c, d + a, own] = u[c, a]
        kx[d + a, own] = stiff[a]
        mx[d + a, own] = mass[a]
        return carry

    lax.fori_loop(0, rows, place, 0, unroll=True)
    first = {}
    for n, (side, above) in enumerate(((slab_a, sector_even), (slab_b, jnp.logical_not(sector_even)))):
        base = jnp.where(above, d + rows, 0)
        first[n] = base
        nearest = jnp.where(above, d + rows, d - 1)
        for i in range(d):
            for c in range(comps):
                t0[c, base + i, own] = side[pl.ds(slab.residual_at(c, i), layers)]
                ux[c, base + i, d : d + 1] = side[pl.ds(slab.low + c * d + i, 1)]
                ux[c, base + i, d + layers - 1 : d + layers] = side[pl.ds(slab.high + c * d + i, 1)]
            kx[base + i, own] = side[pl.ds(slab.stiff + i * layers, layers)]
        for i in range(d - 1):
            mx[jnp.where(above, d + rows, 1) + i, own] = side[pl.ds(slab.mass + i * layers, layers)]
        for c in range(comps):
            ux[c, nearest, own] = side[pl.ds(slab.disp + c * layers, layers)]

    def place_bands(a_above):
        corners = [[(x, 0), (x, wedge.blocks)] for x in (corner_a, corner_b)]
        for n, (side, first_block) in enumerate(((corner_a, 2 * wedge.blocks), (band_b, 0))):
            above = a_above == (n == 0)
            near = d + layers if above else d - 1
            where = pl.ds(d + layers if above else 0, d)

            def own_pair(pair, carry):
                for i in range(2):
                    part = slice(i * d, i * d + d)
                    row = d + 2 * pair + i
                    for c in range(comps):
                        t0[c, row, where] = side[first_block + c * (rows // 2) + pair, part]
                        ux[c, row, where] = side[first_block + (comps + c) * (rows // 2) + pair, part]
                    kx[row, where] = side[first_block + 2 * comps * (rows // 2) + pair, part]
                    mx[row, where] = side[first_block + (2 * comps + 1) * (rows // 2) + pair, part]
                return carry

            lax.fori_loop(0, rows // 2, own_pair, 0, unroll=True)
            for m, (block, at) in enumerate(corners[n]):
                above_m = sector_even if m == 0 else jnp.logical_not(sector_even)
                for step in range(1, d + 1):
                    row = jnp.where(above_m, d + rows - 1 + step, d - step)
                    count, start = wedge.counts[step - 1], wedge.starts[step - 1]
                    part = slice(start, start + count)
                    near_rows = slice(near, near + count) if above else slice(near + 1 - count, near + 1)
                    for c in range(comps):
                        t0[c, row, near_rows] = block[at + c, part]
                        ux[c, row, near : near + 1] = block[at + wedge.disp + c, d + step - 1 : d + step]
                    kx[row, near_rows] = block[at + wedge.stiff, part]
                    mx[row, near_rows] = block[at + wedge.mass, part]
                nearest = jnp.where(above_m, d + rows, d - 1)
                for c in range(comps):
                    ux[c, nearest, where] = block[at + wedge.disp + c, 0:d]

    @pl.when(band_even)
    def _():
        place_bands(True)

    @pl.when(jnp.logical_not(band_even))
    def _():
        place_bands(False)

    lane = lax.broadcasted_iota(jnp.int32, (all_layers, width), 1)
    layer = lax.broadcasted_iota(jnp.int32, (all_layers, width), 0)

    raft[...] = jnp.zeros_like(raft)
    payload[...] = jnp.zeros_like(payload)

    @pl.when(band == 0)
    def _():
        around = (sector, lax.rem(sector + 1, sectors), lax.rem(sector + sectors - 1, sectors))
        rows_of = jnp.concatenate([survey[pl.ds(x * bands, bands)] for x in around], axis=0)
        known = jnp.concatenate(
            [pltpu.roll(rows_of, 128 - PARAM_AT - PARAMS * j, 1) for j in range(bearings)], axis=0
        )
        each = len(around) * bands
        count = bearings * each
        within = lax.rem(lax.broadcasted_iota(jnp.int32, (count, 1), 0), each)
        shift = jnp.where(within < bands, d, jnp.where(within < 2 * bands, d + rows, d - rows))
        column = lambda p: known[:, p : p + 1]
        row_of = column(PARAM_ROW).astype(jnp.int32) + shift
        row_of = jnp.broadcast_to(row_of, (count, width))
        lane_of = jnp.broadcast_to(column(PARAM_LANE).astype(jnp.int32), (count, width))
        here = lane_of == lax.broadcasted_iota(jnp.int32, (count, width), 1)
        at_node = [jnp.zeros((count, width), F32) for _ in range(comps)]
        for a in range(all_rows):
            hit = row_of == a
            for c in range(comps):
                at_node[c] = jnp.where(hit, ux[c, a, d : d + 1], at_node[c])
        stick = jnp.broadcast_to(column(PARAM_STICK), (count, width))
        force = bearing_law(
            at_node[:2], at_node[2], stick,
            [column(PARAM_SLIP), column(PARAM_SLIP + 1)], [column(PARAM_OLD), column(PARAM_OLD + 1)], column(PARAM_WEIGHT),
        )
        force = [jnp.where(here, f, 0.0) for f in force]
        stiffness = [jnp.where(here & (stick == 1.0), K_STICK, 0.0), jnp.where(here, K_VERT, 0.0)]
        for a in range(all_rows):
            hit = row_of == a
            for q, value in enumerate(force + stiffness):
                raft[q, a : a + 1] = jnp.sum(jnp.where(hit, value, 0.0), axis=0, keepdims=True)
        place_of = lax.broadcasted_iota(jnp.int32, payload.shape, 0) - sector * bands
        col = lax.broadcasted_iota(jnp.int32, payload.shape, 1)
        reply = jnp.zeros(payload.shape, F32)
        for c in range(comps):
            total = jnp.sum(force[c], axis=1, keepdims=True)
            for q in range(bands):
                for j in range(bearings):
                    value = total[j * each + q : j * each + q + 1]
                    reply = jnp.where((place_of == q) & (col == FORCE_AT + c * bearings + j), value, reply)
        payload[...] = reply

    interface = (layer == d - 1) | (layer == d + layers - 1)

    def faces(a, carry):
        k = kx[a]
        k_h = conductance(k, ahead(k, 0))
        kh[a] = k_h
        kr[a] = jnp.where(lane < width - 1, conductance(k, ahead(k, 1)), 0.0)
        ks[a] = conductance(k, kx[jnp.minimum(a + 1, all_rows - 1)])
        for c in range(comps):
            v = ux[c, a]
            flux = jnp.where(interface, k_h * (ahead(v, 0) - v), 0.0)
            change = COMPONENT_SCALE[c] * (flux - behind(flux, 0))
            change = change - jnp.where(layer == d, raft[c, pl.ds(a, 1)], 0.0)
            t0[c, a] = t0[c, a] + change
        return carry

    lax.fori_loop(0, all_rows, faces, 0, unroll=True)
    for a in (d - 1, d + rows - 1):
        for c in range(comps):
            flux = COMPONENT_SCALE[c] * (ks[a] * (ux[c, a + 1] - ux[c, a]))
            t0[c, a] = t0[c, a] + flux
            t0[c, a + 1] = t0[c, a + 1] - flux

    def diagonals(a, carry):
        k_h, k_r = kh[a], kr[a]
        around = k_h + behind(k_h, 0) + k_r + behind(k_r, 1) + ks[a] + ks[a - 1]
        diag[0, a] = mx[a] + COMPONENT_SCALE[0] * around + jnp.where(layer == d, raft[comps, pl.ds(a, 1)], 0.0)
        diag[1, a] = mx[a] + COMPONENT_SCALE[2] * around + jnp.where(layer == d, raft[comps + 1, pl.ds(a, 1)], 0.0)
        return carry

    lax.fori_loop(1, all_rows - 1, diagonals, 0, unroll=True)

    levels = (t0, t1, t2, t3, t4)
    shift_of, link_of = coefficients(survey[...])
    for step in range(1, ITERS + 1):
        src, dst = levels[step - 1], levels[step]
        a_k = jnp.broadcast_to(shift_of[step - 1], (all_layers, width))
        c_k = jnp.broadcast_to(link_of[step - 1], (all_layers, width)) if step > 1 else None

        def apply(a, carry):
            k_h, k_r, k_next, k_back = kh[a], kr[a], ks[a], ks[a - 1]
            for c in range(comps):
                v = src[c, a]
                around = k_next * src[c, a + 1] + k_back * src[c, a - 1]
                around = around + (k_h * ahead(v, 0) + behind(k_h * v, 0))
                around = around + (k_r * ahead(v, 1) + behind(k_r * v, 1))
                centre = (diag[0 if c < 2 else 1, a] - a_k) * v
                if step > 1:
                    centre = centre - c_k * levels[step - 2][c, a]
                dst[c, a] = centre - (around if COMPONENT_SCALE[c] == 1.0 else COMPONENT_SCALE[c] * around)
            return carry

        lax.fori_loop(step, all_rows - step, apply, 0, unroll=True)

    pairs = gram_pairs()
    outs = (b0, b1, b2, b3, b4)

    def products(a, sums):
        for c in range(comps):
            block = [t[c, d + a, own] for t in levels]
            for out, x in zip(outs, block):
                out[c, a] = x
            sums = tuple(
                s + dot(block[i], block[j]) for s, (i, j) in zip(sums, pairs)
            )
        return sums

    sums = lax.fori_loop(0, rows, products, tuple(jnp.zeros((8, width), F32) for _ in pairs))
    col = lax.broadcasted_iota(jnp.int32, payload.shape, 1)
    reply = payload[...]
    for p, s in enumerate(sums):
        reply = jnp.where(col == p, total_of(s), reply)
    payload[...] = reply


def combine_kernel(received, survey, b0, b1, b2, b3, b4, increment, residual, force, *, bearings, bands):
    comps, rows, layers, width = b0.shape
    sector = lax.axis_index("sector")
    total = jnp.sum(received[...], axis=0, keepdims=True)
    col = lax.broadcasted_iota(jnp.int32, total.shape, 1)
    table = {ij: jnp.sum(jnp.where(col == p, total, 0.0), axis=1, keepdims=True) for p, ij in enumerate(gram_pairs())}
    shift_of, link_of = coefficients(survey[...])
    g = lambda i, j: table[min(i, j), max(i, j)]
    zero, one = jnp.zeros_like(table[0, 0]), jnp.ones_like(table[0, 0])
    res = [one] + [zero] * ITERS
    direction, inc = list(res), [zero] * (ITERS + 1)
    norm = table[0, 0]
    for it in range(ITERS):
        image = [zero] * (ITERS + 1)
        for i in range(it + 1):
            image[i] = image[i] + shift_of[i] * direction[i]
            image[i + 1] = image[i + 1] + direction[i]
            if i:
                image[i - 1] = image[i - 1] + link_of[i] * direction[i]
        product = sum(
            direction[i] * sum(image[j] * g(i, j) for j in range(it + 2)) for i in range(it + 1)
        )
        alpha = norm / product
        inc = [x + alpha * y for x, y in zip(inc, direction)]
        res = [x - alpha * y for x, y in zip(res, image)]
        if it + 1 < ITERS:
            norm_next = sum(res[i] * sum(res[j] * g(i, j) for j in range(it + 2)) for i in range(it + 2))
            ratio = norm_next / norm
            direction = [x + ratio * y for x, y in zip(res, direction)]
            norm = norm_next
    basis = (b0, b1, b2, b3, b4)
    inc = [jnp.broadcast_to(x, (layers, width)) for x in inc[:ITERS]]
    res = [jnp.broadcast_to(x, (layers, width)) for x in res]

    def combine(a, carry):
        for c in range(comps):
            x = [b[c, a] for b in basis]
            increment[c, a] = sum(y * z for y, z in zip(inc, x))
            residual[c, a] = sum(y * z for y, z in zip(res, x))
        return carry

    lax.fori_loop(0, rows, combine, 0)
    mine = received[pl.ds(sector * bands, 1)]
    for c in range(comps):
        force[c : c + 1] = mine[:, FORCE_AT + c * bearings : FORCE_AT + (c + 1) * bearings]


def kernel_call(body, outs, operands, far=(), scratch=(), grant=VMEM_LIMIT):
    vmem = pl.BlockSpec(memory_space=pltpu.VMEM)
    return pl.pallas_call(
        body,
        out_shape=[jax.ShapeDtypeStruct(s, F32) for s in outs],
        in_specs=[pl.BlockSpec(memory_space=pltpu.HBM) if i in far else vmem for i in range(len(operands))],
        out_specs=[vmem] * len(outs),
        scratch_shapes=[pltpu.VMEM(s, F32) if isinstance(s, tuple) else s for s in scratch],
        compiler_params=pltpu.CompilerParams(vmem_limit_bytes=grant),
    )(*operands)


def pair_up(i, n):
    return i ^ 1


def pair_down(i, n):
    return (((i + 1) % n) ^ 1) - 1 if ((i + 1) % n) ^ 1 else n - 1


def per_device(
    given_load, displacement, mass_coef, stiffness, bearing_node, stick_state, slip_prev, bearing_old, bearing_weight
):
    comps, rows, layers, radial = displacement.shape
    bearings = bearing_node.shape[0]
    sectors, bands = lax.axis_size("sector"), lax.axis_size("band")
    d = DEPTH
    slab, wedge = SectorSlab(comps, layers), Wedge(comps)

    def exchange(x, sector_partner=None, band_partner=None):
        pairs = []
        for s in range(sectors):
            for b in range(bands):
                t = s if sector_partner is None else sector_partner(s, sectors)
                q = b if band_partner is None else band_partner(b)
                if 0 <= q < bands:
                    pairs.append((s * bands + b, t * bands + q))
        return lax.ppermute(x, AXES, pairs)

    inner = lambda b: -1 if b in (0, bands - 1) else ((b + 1) ^ 1) - 1

    field, block = displacement.shape, mass_coef.shape
    slab_shape, band_shape = (slab.rows, radial), ((2 * comps + 2) * (rows // 2), 2 * d, radial)
    small = [
        pltpu.SMEM((bearings,), jnp.int32),
        pltpu.SMEM((bearings,), jnp.int32),
        pltpu.SMEM((2, bearings), F32),
        pltpu.SMEM((2, bearings), F32),
        pltpu.SMEM((bearings,), F32),
    ]
    work, slab_a, slab_b, band_b = kernel_call(
        functools.partial(local_kernel, radial=radial),
        [(2 * comps + 5, *block), slab_shape, slab_shape, band_shape],
        (displacement, given_load, mass_coef, stiffness, bearing_node, stick_state, slip_prev, bearing_old, bearing_weight),
        far=range(9),
        grant=VMEM_WHOLE,
        scratch=[field, *small, pltpu.SemaphoreType.DMA((9,))],
    )
    outer = lambda b: b ^ 1
    slab_b = exchange(slab_b, pair_down)
    slab_a = exchange(slab_a, pair_up)
    band_b = exchange(band_b, None, inner)
    (survey,) = kernel_call(survey_kernel, [(sectors * bands, 128)], (work,), scratch=[field] * 3)
    survey = lax.all_to_all(survey, AXES, 0, 0, tiled=True)
    corner_a, corner_b = kernel_call(
        functools.partial(corner_kernel, comps=comps, layers=layers),
        [(2 * wedge.blocks + band_shape[0], 2 * d, radial), (2 * wedge.blocks, 2 * d, radial)],
        (slab_a, slab_b, work, survey, band_b),
    )
    corner_b = exchange(corner_b, None, inner)
    corner_a = exchange(corner_a, None, outer)
    devices = sectors * bands
    extended = (rows + 2 * d, layers + 2 * d, radial)
    *basis, payload = kernel_call(
        functools.partial(power_kernel, bearings=bearings, sectors=sectors, bands=bands),
        [field] * (ITERS + 1) + [(devices, 128)],
        (work, slab_a, slab_b, band_b, corner_a, corner_b, survey),
        scratch=[(comps, *extended)] * (ITERS + 2) + [extended] * 5 + [(2, *extended), (comps + 2, rows + 2 * d, radial)],
    )
    received = lax.all_to_all(payload, AXES, 0, 0, tiled=True)
    increment, residual, force = kernel_call(
        functools.partial(combine_kernel, bearings=bearings, bands=bands),
        [field, field, (comps, bearings)],
        (received, survey, *basis),
    )
    return (increment, residual, force)


def solution(mesh):
    return jax.shard_map(
        per_device,
        mesh=mesh,
        in_specs=(
            P(None, "sector", "band", None),
            P(None, "sector", "band", None),
            P("sector", "band", None),
            P("sector", "band", None),
            P(("sector", "band")),
            P(("sector", "band")),
            P(None, ("sector", "band")),
            P(None, ("sector", "band")),
            P(("sector", "band")),
        ),
        out_specs=(
            P(None, "sector", "band", None),
            P(None, "sector", "band", None),
            P(None, ("sector", "band")),
        ),
        check_vma=False,
    )
```

time: 62.2 us -> 51 us (0.82)
  waiting for transfers between devices: 15.9 us -> 1.03 us
  blocking collectives: 12.1 us -> 26.7 us
  local copies, waits for them, and re-layouts: 7.13 us -> 1.36 us
  starting transfers between devices: 12.9 us -> 7.98 us
    ppermute x8 -> x5, waiting for transfers between devices: 15.9 us -> 1.03 us  [exchange(): return lax.ppermute(x, AXES, pairs)]
    all_to_all x0 -> x1, blocking collectives: none -> 11.3 us  [per_device(): survey = lax.all_to_all(survey, AXES, 0, 0, tiled=True)]
    unnamed x24 -> x2, local copies, waits for them, and re-layouts: 7.13 us -> 1.36 us
    ppermute x8 -> x5, starting transfers between devices: 12.9 us -> 7.98 us  [exchange(): return lax.ppermute(x, AXES, pairs)]
    all_to_all x1, blocking collectives: 12.1 us -> 15.4 us  [per_device(): received = lax.all_to_all(payload, AXES, 0, 0, tiled=True)]
    pallas_call x4 -> x5, Pallas kernels: 13.1 us -> 13 us  [kernel_call(): pl.pallas_call(body, out_shape=[jax.ShapeDtypeStruct(s, F32) for s in out...]
  transfers between devices with their start and end apart: 8 -> 5, of which waited for: 2 -> 1; matrix products, arithmetic and copies ran while one was open for 0% -> 0% of each run, Pallas kernels for 0% -> 4%
where the time goes in v2:
time: 51 us; the launch traced here: 50.8 us
  blocking collectives  26.7 us (52%)
  Pallas kernels  13 us (25%)
  starting transfers between devices  7.98 us (16%)
  local copies, waits for them, and re-layouts  1.36 us (3%)
  waiting for transfers between devices  1.03 us (2%)
  between operations  0.7 us (1%)
    all_to_all x1, blocking collectives, per_device(): received = lax.all_to_all(payload, AXES, 0, 0, tiled=True)  15.4 us
    pallas_call x5, Pallas kernels, kernel_call(): pl.pallas_call(body, out_shape=[jax.ShapeDtypeStruct(s, F32) for s in out...  13 us
    all_to_all x1, blocking collectives, per_device(): survey = lax.all_to_all(survey, AXES, 0, 0, tiled=True)  11.3 us
    ppermute x5, starting transfers between devices, exchange(): return lax.ppermute(x, AXES, pairs)  7.98 us
    unnamed x2, local copies, waits for them, and re-layouts  1.36 us
    ppermute x5, waiting for transfers between devices, exchange(): return lax.ppermute(x, AXES, pairs)  1.03 us
  transfers between devices with their start and end apart: 5, of which 1 were waited for; matrix products, arithmetic and copies ran while one was open for 0% of the time, Pallas kernels for 4%

profile of v2, /device:TPU:0, one launch (start us, length us, event | category | flops | bytes accessed | tf_op | source)
XLA Modules:
  0.0 50.8 jit_solution(5500279318554300921)
XLA Ops:
  0.6 3.6 %shard_map.112 = (f32[11,8,16,256]{3,2,1,0:T(8,128)}, f32[376,256]{1,0:T(8,128)}, f32[376,256]{1,0:T(8,128)}, f32[32,8,256]{2,1,0:T(8,128)}) custom-call(f32[3,8,16,256]{3,2,1,0:T(8,128)} %u_far.1, f32[3,8,16,256]{3,2,1,0:T(8,128)} %load_far.1, f32[8,16,256]{2,1,0:T(8,128)} %mass_far.1, f32[8,16,256]{2,1,0:T(8,128)} %stiff_far.1, s32[4]{0:T(128)} %node_far.1, ...), custom_call_target="tpu_custom_call" | custom-call | tf_op jit(solution)/shard_map/pallas_call | solution.py:580
  4.3 3.0 %collective-permute-start = (f32[376,256]{1,0:T(8,128)}, f32[376,256]{1,0:T(8,128)S(1)}, u32[]{:S(2)}, u32[]{:S(2)}) collective-permute-start(f32[376,256]{1,0:T(8,128)} %get-tuple-element.16), channel_id=1, source_target_pairs={{0,4},{1,5},{2,6},{3,7},{4,0},{5,1},{6,2},{7,3},{8,12},{9,13},{10,... | collective-permute-start | bytes 1155080 | tf_op jit(solution)/shard_map/ppermute | solution.py:615
  7.3 3.6 %collective-permute-start.1 = (f32[376,256]{1,0:T(8,128)}, f32[376,256]{1,0:T(8,128)S(1)}, u32[]{:S(2)}, u32[]{:S(2)}) collective-permute-start(f32[376,256]{1,0:T(8,128)} %get-tuple-element.17), channel_id=1, source_target_pairs={{0,28},{1,29},{2,30},{3,31},{4,8},{5,9},{6,10},{7,11},{8,4},{9,5},... | collective-permute-start | bytes 1155080 | tf_op jit(solution)/shard_map/ppermute | solution.py:615
  10.8 0.7 %collective-permute-start.2 = (f32[32,8,256]{2,1,0:T(8,128)}, f32[32,8,256]{2,1,0:T(8,128)S(1)}, u32[]{:S(2)}, u32[]{:S(2)}) collective-permute-start(f32[32,8,256]{2,1,0:T(8,128)} %get-tuple-element.18), channel_id=1, source_target_pairs={{1,2},{2,1},{5,6},{6,5},{9,10},{10,9},{13,14},{14,13},{17,18},{18,... | collective-permute-start | bytes 786440 | tf_op jit(solution)/shard_map/ppermute | solution.py:615
  11.5 0.0 copy-start
  11.5 1.4 %copy-done = f32[11,8,16,256]{3,2,1,0:T(8,128)S(1)} copy-done((f32[11,8,16,256]{3,2,1,0:T(8,128)S(1)}, f32[11,8,16,256]{3,2,1,0:T(8,128)}, u32[]{:S(2)}) %copy-start) | copy-done | bytes 1441816
  12.9 2.0 %shard_map.113 = f32[32,128]{1,0:T(8,128)S(1)} custom-call(f32[11,8,16,256]{3,2,1,0:T(8,128)S(1)} %copy-done), custom_call_target="tpu_custom_call" | custom-call | tf_op jit(solution)/shard_map/pallas_call | solution.py:580
  14.8 11.3 %all_to_all.22 = f32[32,1,128]{2,1,0:T(1,128)S(1)} all-to-all(f32[32,1,128]{2,1,0:T(1,128)S(1)} %bitcast.12), channel_id=1, replica_groups=mesh['sector'=8,'band'=4] {'sector','band'}, dimensions={0} | all-to-all | bytes 32768 | tf_op jit(solution)/shard_map/all_to_all | solution.py:641
  26.1 0.0 collective-permute-done.2.band_b
  26.1 0.0 collective-permute-done.slab_a
  26.1 0.0 collective-permute-done.1.slab_b
  26.1 0.2 shard_map.114
  26.3 0.1 collective-permute-start.3
  26.4 0.7 %collective-permute-start.4 = (f32[16,8,256]{2,1,0:T(8,128)S(1)}, f32[16,8,256]{2,1,0:T(8,128)S(1)}, u32[]{:S(2)}, u32[]{:S(2)}) collective-permute-start(f32[16,8,256]{2,1,0:T(8,128)S(1)} %get-tuple-element.20), channel_id=1, source_target_pairs={{1,2},{2,1},{5,6},{6,5},{9,10},{10,9},{13,14},{14,13},{17,18},{18,... | collective-permute-start | bytes 393224 | tf_op jit(solution)/shard_map/ppermute | solution.py:615
  27.1 0.0 collective-permute-done.4.corner_b
  27.1 1.0 %collective-permute-done.3.corner_a = f32[48,8,256]{2,1,0:T(8,128)S(1)} collective-permute-done((f32[48,8,256]{2,1,0:T(8,128)S(1)}, f32[48,8,256]{2,1,0:T(8,128)S(1)}, u32[]{:S(2)}, u32[]{:S(2)}) %collective-permute-start.3) | collective-permute-done | bytes 393248 | tf_op jit(solution)/shard_map/ppermute | solution.py:615
  28.1 5.9 %shard_map.115 = (f32[3,8,16,256]{3,2,1,0:T(8,128)S(1)}, f32[3,8,16,256]{3,2,1,0:T(8,128)S(1)}, f32[3,8,16,256]{3,2,1,0:T(8,128)S(1)}, f32[3,8,16,256]{3,2,1,0:T...) custom-call(f32[11,8,16,256]{3,2,1,0:T(8,128)S(1)} %copy-done, ...), custom_call_target="tpu_custom_call" | custom-call | tf_op jit(solution)/shard_map/pallas_call | solution.py:580
  34.0 15.4 %all_to_all.23 = f32[32,1,128]{2,1,0:T(1,128)S(1)} all-to-all(f32[32,1,128]{2,1,0:T(1,128)S(1)} %bitcast.13), channel_id=1, replica_groups=mesh['sector'=8,'band'=4] {'sector','band'}, dimensions={0} | all-to-all | bytes 32768 | tf_op jit(solution)/shard_map/all_to_all | solution.py:657
  49.5 1.3 %shard_map.116 = (f32[3,8,16,256]{3,2,1,0:T(8,128)}, f32[3,8,16,256]{3,2,1,0:T(8,128)}, f32[3,4]{1,0:T(4,128)}) custom-call(f32[32,128]{1,0:T(8,128)S(1)} %bitcast.11, f32[32,128]{1,0:T(8,128)S(1)} %bitcast.10, f32[3,8,16,256]{3,2,1,0:T(8,128)S(1)} %get-tuple-element.22.b0, f32[3,8,16,256]{3,2,1,0:T(8,128)S(1)} %get-tuple-element.23.b1, ...), custom_call_target="tpu_custom_call" | custom-call | tf_op jit(solution)/shard_map/pallas_call | solution.py:580
Async XLA Ops:
  4.3 21.9 %collective-permute-start = (f32[376,256]{1,0:T(8,128)}, f32[376,256]{1,0:T(8,128)S(1)}, u32[]{:S(2)}, u32[]{:S(2)}) collective-permute-start(f32[376,256]{1,0:T(8,128)} %get-tuple-element.16), channel_id=1, source_target_pairs={{0,4},{1,5},{2,6},{3,7},{4,0},{5,1},{6,2},{7,3},{8,12},{9,13},{10,... | collective-permute-start | bytes 1155080 | tf_op jit(solution)/shard_map/ppermute | solution.py:615
  7.3 18.9 %collective-permute-start.1 = (f32[376,256]{1,0:T(8,128)}, f32[376,256]{1,0:T(8,128)S(1)}, u32[]{:S(2)}, u32[]{:S(2)}) collective-permute-start(f32[376,256]{1,0:T(8,128)} %get-tuple-element.17), channel_id=1, source_target_pairs={{0,28},{1,29},{2,30},{3,31},{4,8},{5,9},{6,10},{7,11},{8,4},{9,5},... | collective-permute-start | bytes 1155080 | tf_op jit(solution)/shard_map/ppermute | solution.py:615
  10.8 15.3 %collective-permute-start.2 = (f32[32,8,256]{2,1,0:T(8,128)}, f32[32,8,256]{2,1,0:T(8,128)S(1)}, u32[]{:S(2)}, u32[]{:S(2)}) collective-permute-start(f32[32,8,256]{2,1,0:T(8,128)} %get-tuple-element.18), channel_id=1, source_target_pairs={{1,2},{2,1},{5,6},{6,5},{9,10},{10,9},{13,14},{14,13},{17,18},{18,... | collective-permute-start | bytes 786440 | tf_op jit(solution)/shard_map/ppermute | solution.py:615
  11.5 1.4 %copy-start = (f32[11,8,16,256]{3,2,1,0:T(8,128)S(1)}, f32[11,8,16,256]{3,2,1,0:T(8,128)}, u32[]{:S(2)}) copy-start(f32[11,8,16,256]{3,2,1,0:T(8,128)} %get-tuple-element.15.work) | copy-start | bytes 4325380
  26.3 1.8 %collective-permute-start.3 = (f32[48,8,256]{2,1,0:T(8,128)S(1)}, f32[48,8,256]{2,1,0:T(8,128)S(1)}, u32[]{:S(2)}, u32[]{:S(2)}) collective-permute-start(f32[48,8,256]{2,1,0:T(8,128)S(1)} %get-tuple-element.19), channel_id=1, source_target_pairs={{0,1},{1,0},{2,3},{3,2},{4,5},{5,4},{6,7},{7,6},{8,9},{9,8},{10,11... | collective-permute-start | bytes 1179656 | tf_op jit(solution)/shard_map/ppermute | solution.py:615
  26.4 0.7 %collective-permute-start.4 = (f32[16,8,256]{2,1,0:T(8,128)S(1)}, f32[16,8,256]{2,1,0:T(8,128)S(1)}, u32[]{:S(2)}, u32[]{:S(2)}) collective-permute-start(f32[16,8,256]{2,1,0:T(8,128)S(1)} %get-tuple-element.20), channel_id=1, source_target_pairs={{1,2},{2,1},{5,6},{6,5},{9,10},{10,9},{13,14},{14,13},{17,18},{18,... | collective-permute-start | bytes 393224 | tf_op jit(solution)/shard_map/ppermute | solution.py:615

commit v3 on v2

--- a/solution.py
+++ b/solution.py
@@ -29,8 +29,8 @@
 PARAMS = 8
 PARAM_AT = 32
 FORCE_AT = 64
-VMEM_LIMIT = 48 * 1024 * 1024
-VMEM_WHOLE = 64 * 1024 * 1024 - 65536
+VMEM_LIMIT = 24 * 1024 * 1024
+TILE = 8
 
 
 def conductance(left, right):
@@ -320,10 +320,27 @@
     return [(i, j) for i in range(ITERS) for j in range(i, ITERS + 1)]
 
 
-def power_kernel(
-    work, slab_a, slab_b, band_b, corner_a, corner_b, survey,
-    b0, b1, b2, b3, b4, payload,
-    t0, t1, t2, t3, t4, ux, kx, mx, ks, kh, kr, diag, raft,
+def place_wedge(t, ux, kx, mx, block, at, wedge, comps, rows, above, near, upward):
+    d = DEPTH
+    for step in range(1, d + 1):
+        row = jnp.where(above, d + rows - 1 + step, d - step)
+        count, start = wedge.counts[step - 1], wedge.starts[step - 1]
+        part = slice(start, start + count)
+        where = slice(near, near + count) if upward else slice(near + 1 - count, near + 1)
+        for c in range(comps):
+            t[c, row, where] = block[at + c, part]
+            ux[c, row, near : near + 1] = block[at + wedge.disp + c, d + step - 1 : d + step]
+        kx[row, where] = block[at + wedge.stiff, part]
+        mx[row, where] = block[at + wedge.mass, part]
+    nearest = jnp.where(above, d + rows, d - 1)
+    for c in range(comps):
+        ux[c, nearest, slice(near, near + d) if upward else slice(near + 1 - d, near + 1)] = block[at + wedge.disp + c, 0:d]
+
+
+def early_kernel(
+    work, slab_a, slab_b, band_b, corner_a, survey,
+    t0, t1, t2, t3, t4, kx, kh, late_t, late_u, late_m, raft, payload,
+    raw, ux, mx, ks, kr, diag,
     *, bearings, sectors, bands,
 ):
     r, u, _, mass, stiff = parts_of(work)
@@ -336,23 +353,19 @@
     all_rows, all_layers = rows + 2 * d, layers + 2 * d
     own = pl.ds(d, layers)
 
-    def place(a, carry):
-        for c in range(comps):
-            t0[c, d + a, own] = r[c, a]
+    for a in range(rows):
+        for c in range(comps):
+            raw[c, d + a, own] = r[c, a]
             ux[c, d + a, own] = u[c, a]
         kx[d + a, own] = stiff[a]
         mx[d + a, own] = mass[a]
-        return carry
-
-    lax.fori_loop(0, rows, place, 0, unroll=True)
-    first = {}
-    for n, (side, above) in enumerate(((slab_a, sector_even), (slab_b, jnp.logical_not(sector_even)))):
+    sides = ((slab_a, sector_even), (slab_b, jnp.logical_not(sector_even)))
+    for side, above in sides:
         base = jnp.where(above, d + rows, 0)
-        first[n] = base
         nearest = jnp.where(above, d + rows, d - 1)
         for i in range(d):
             for c in range(comps):
-                t0[c, base + i, own] = side[pl.ds(slab.residual_at(c, i), layers)]
+                raw[c, base + i, own] = side[pl.ds(slab.residual_at(c, i), layers)]
                 ux[c, base + i, d : d + 1] = side[pl.ds(slab.low + c * d + i, 1)]
                 ux[c, base + i, d + layers - 1 : d + layers] = side[pl.ds(slab.high + c * d + i, 1)]
             kx[base + i, own] = side[pl.ds(slab.stiff + i * layers, layers)]
@@ -361,40 +374,26 @@
         for c in range(comps):
             ux[c, nearest, own] = side[pl.ds(slab.disp + c * layers, layers)]
 
-    def place_bands(a_above):
-        corners = [[(x, 0), (x, wedge.blocks)] for x in (corner_a, corner_b)]
-        for n, (side, first_block) in enumerate(((corner_a, 2 * wedge.blocks), (band_b, 0))):
-            above = a_above == (n == 0)
-            near = d + layers if above else d - 1
-            where = pl.ds(d + layers if above else 0, d)
-
-            def own_pair(pair, carry):
-                for i in range(2):
-                    part = slice(i * d, i * d + d)
-                    row = d + 2 * pair + i
-                    for c in range(comps):
-                        t0[c, row, where] = side[first_block + c * (rows // 2) + pair, part]
-                        ux[c, row, where] = side[first_block + (comps + c) * (rows // 2) + pair, part]
-                    kx[row, where] = side[first_block + 2 * comps * (rows // 2) + pair, part]
-                    mx[row, where] = side[first_block + (2 * comps + 1) * (rows // 2) + pair, part]
-                return carry
-
-            lax.fori_loop(0, rows // 2, own_pair, 0, unroll=True)
-            for m, (block, at) in enumerate(corners[n]):
-                above_m = sector_even if m == 0 else jnp.logical_not(sector_even)
-                for step in range(1, d + 1):
-                    row = jnp.where(above_m, d + rows - 1 + step, d - step)
-                    count, start = wedge.counts[step - 1], wedge.starts[step - 1]
-                    part = slice(start, start + count)
-                    near_rows = slice(near, near + count) if above else slice(near + 1 - count, near + 1)
-                    for c in range(comps):
-                        t0[c, row, near_rows] = block[at + c, part]
-                        ux[c, row, near : near + 1] = block[at + wedge.disp + c, d + step - 1 : d + step]
-                    kx[row, near_rows] = block[at + wedge.stiff, part]
-                    mx[row, near_rows] = block[at + wedge.mass, part]
-                nearest = jnp.where(above_m, d + rows, d - 1)
+    def place_bands(even):
+        for side, first_block, upward in ((corner_a, 2 * wedge.blocks, even), (band_b, 0, not even)):
+            where = pl.ds(d + layers if upward else 0, d)
+            for a in range(rows):
+                part = slice((a % 2) * d, (a % 2) * d + d)
+                block = lambda f: side[first_block + f * (rows // 2) + a // 2, part]
                 for c in range(comps):
-                    ux[c, nearest, where] = block[at + wedge.disp + c, 0:d]
+                    raw[c, d + a, where] = block(c)
+                    ux[c, d + a, where] = block(comps + c)
+                kx[d + a, where] = block(2 * comps)
+                mx[d + a, where] = block(2 * comps + 1)
+        near = d + layers if even else d - 1
+        for m, (_, above) in enumerate(sides):
+            place_wedge(raw, ux, kx, mx, corner_a, m * wedge.blocks, wedge, comps, rows, above, near, even)
+        late = pl.ds(0 if even else all_layers - TILE, TILE)
+        for a in range(all_rows):
+            for c in range(comps):
+                late_t[c, a] = raw[c, a, late]
+                late_u[c, a] = ux[c, a, late]
+            late_m[a] = mx[a, late]
 
     @pl.when(band_even)
     def _():
@@ -466,7 +465,7 @@
             flux = jnp.where(interface, k_h * (ahead(v, 0) - v), 0.0)
             change = COMPONENT_SCALE[c] * (flux - behind(flux, 0))
             change = change - jnp.where(layer == d, raft[c, pl.ds(a, 1)], 0.0)
-            t0[c, a] = t0[c, a] + change
+            t0[c, a] = raw[c, a] + change
         return carry
 
     lax.fori_loop(0, all_rows, faces, 0, unroll=True)
@@ -507,25 +506,113 @@
 
         lax.fori_loop(step, all_rows - step, apply, 0, unroll=True)
 
-    pairs = gram_pairs()
-    outs = (b0, b1, b2, b3, b4)
-
-    def products(a, sums):
-        for c in range(comps):
-            block = [t[c, d + a, own] for t in levels]
-            for out, x in zip(outs, block):
-                out[c, a] = x
-            sums = tuple(
-                s + dot(block[i], block[j]) for s, (i, j) in zip(sums, pairs)
-            )
-        return sums
-
-    sums = lax.fori_loop(0, rows, products, tuple(jnp.zeros((8, width), F32) for _ in pairs))
-    col = lax.broadcasted_iota(jnp.int32, payload.shape, 1)
-    reply = payload[...]
-    for p, s in enumerate(sums):
-        reply = jnp.where(col == p, total_of(s), reply)
-    payload[...] = reply
+
+def late_kernel(
+    t0, t1, t2, t3, t4, kx, kh, late_t, late_u, late_m, raft, payload_in, corner_b, survey,
+    b0, b1, b2, b3, b4, payload,
+    s0, s1, s2, s3, s4, raw, ux, k_tile, m_tile, ks, kh_tile, kh_back, kr, diag,
+):
+    comps, rows, layers, width = b0.shape
+    d = DEPTH
+    wedge = Wedge(comps)
+    all_rows, all_layers = rows + 2 * d, layers + 2 * d
+    sector_even = lax.rem(lax.axis_index("sector"), 2) == 0
+    band_even = lax.rem(lax.axis_index("band"), 2) == 0
+    lane = lax.broadcasted_iota(jnp.int32, (TILE, width), 1)
+    layer = lax.broadcasted_iota(jnp.int32, (TILE, width), 0)
+    shift_of, link_of = coefficients(survey[...])
+    wide = lambda x: None if x is None else jnp.broadcast_to(x, (TILE, width))
+    shift_of, link_of = [wide(x) for x in shift_of], [wide(x) for x in link_of]
+    early, late = (t0, t1, t2, t3, t4), (s0, s1, s2, s3, s4)
+    outs, pairs = (b0, b1, b2, b3, b4), gram_pairs()
+
+    def run(even):
+        off = 0 if even else all_layers - TILE
+
+        def upper(x, whole, *at):
+            x = ahead(x, 0)
+            return jnp.where(layer == TILE - 1, whole[(*at, slice(TILE, TILE + 1))], x) if even else x
+
+        def lower(x, whole, *at):
+            x = behind(x, 0)
+            return x if even else jnp.where(layer == 0, whole[(*at, slice(off - 1, off))], x)
+
+        for a in range(all_rows):
+            for c in range(comps):
+                raw[c, a] = late_t[c, a]
+                ux[c, a] = late_u[c, a]
+            k_tile[a] = kx[a, off : off + TILE]
+            m_tile[a] = late_m[a]
+        near = d - 1 if even else d + layers - off
+        for m, above in enumerate((sector_even, jnp.logical_not(sector_even))):
+            place_wedge(raw, ux, k_tile, m_tile, corner_b, m * wedge.blocks, wedge, comps, rows, above, near, not even)
+
+        crossing = layer == (d - 1 if even else d + layers - 1 - off)
+        on_raft = layer == d
+        for a in range(all_rows):
+            k = k_tile[a]
+            k_h = conductance(k, upper(k, kx, a))
+            kh_tile[a], kh_back[a] = k_h, lower(k_h, kh, a)
+            kr[a] = jnp.where(lane < width - 1, conductance(k, ahead(k, 1)), 0.0)
+            if a + 1 < all_rows:
+                ks[a] = conductance(k, k_tile[a + 1])
+            for c in range(comps):
+                v = ux[c, a]
+                flux = jnp.where(crossing, k_h * (ahead(v, 0) - v), 0.0)
+                change = COMPONENT_SCALE[c] * (flux - behind(flux, 0))
+                if even:
+                    change = change - jnp.where(on_raft, raft[c, a : a + 1], 0.0)
+                s0[c, a] = raw[c, a] + change
+        for a in (d - 1, d + rows - 1):
+            for c in range(comps):
+                flux = COMPONENT_SCALE[c] * (ks[a] * (ux[c, a + 1] - ux[c, a]))
+                s0[c, a] = s0[c, a] + flux
+                s0[c, a + 1] = s0[c, a + 1] - flux
+        for a in range(1, all_rows - 1):
+            k_r = kr[a]
+            around = kh_tile[a] + kh_back[a] + k_r + behind(k_r, 1) + ks[a] + ks[a - 1]
+            for n, scale in enumerate((COMPONENT_SCALE[0], COMPONENT_SCALE[2])):
+                total = m_tile[a] + scale * around
+                diag[n, a] = total + jnp.where(on_raft, raft[comps + n, a : a + 1], 0.0) if even else total
+        for step in range(1, ITERS + 1):
+            src, dst = late[step - 1], late[step]
+            for a in range(step, all_rows - step):
+                k_r = kr[a]
+                for c in range(comps):
+                    v = src[c, a]
+                    around = ks[a] * src[c, a + 1] + ks[a - 1] * src[c, a - 1]
+                    around = around + (
+                        kh_tile[a] * upper(v, early[step - 1], c, a) + kh_back[a] * lower(v, early[step - 1], c, a)
+                    )
+                    around = around + (k_r * ahead(v, 1) + behind(k_r * v, 1))
+                    centre = (diag[0 if c < 2 else 1, a] - shift_of[step - 1]) * v
+                    if step > 1:
+                        centre = centre - link_of[step - 1] * late[step - 2][c, a]
+                    dst[c, a] = centre - (around if COMPONENT_SCALE[c] == 1.0 else COMPONENT_SCALE[c] * around)
+
+        sums = [jnp.zeros((8, width), F32) for _ in pairs]
+        for a in range(rows):
+            for c in range(comps):
+                if even:
+                    block = [jnp.concatenate([x[c, d + a, d:], t[c, d + a, TILE : d + layers]], axis=0) for t, x in zip(early, late)]
+                else:
+                    block = [jnp.concatenate([t[c, d + a, d:off], x[c, d + a, : d + layers - off]], axis=0) for t, x in zip(early, late)]
+                for out, x in zip(outs, block):
+                    out[c, a] = x
+                sums = [s + dot(block[i], block[j]) for s, (i, j) in zip(sums, pairs)]
+        col = lax.broadcasted_iota(jnp.int32, payload.shape, 1)
+        reply = payload_in[...]
+        for p, s in enumerate(sums):
+            reply = jnp.where(col == p, total_of(s), reply)
+        payload[...] = reply
+
+    @pl.when(band_even)
+    def _():
+        run(True)
+
+    @pl.when(jnp.logical_not(band_even))
+    def _():
+        run(False)
 
 
 def combine_kernel(received, survey, b0, b1, b2, b3, b4, increment, residual, force, *, bearings, bands):
@@ -575,15 +662,16 @@
         force[c : c + 1] = mine[:, FORCE_AT + c * bearings : FORCE_AT + (c + 1) * bearings]
 
 
-def kernel_call(body, outs, operands, far=(), scratch=(), grant=VMEM_LIMIT):
+def kernel_call(body, outs, operands, far=(), scratch=()):
     vmem = pl.BlockSpec(memory_space=pltpu.VMEM)
+    operands = [pltpu.with_memory_space_constraint(x, pltpu.HBM) if i in far else x for i, x in enumerate(operands)]
     return pl.pallas_call(
         body,
         out_shape=[jax.ShapeDtypeStruct(s, F32) for s in outs],
         in_specs=[pl.BlockSpec(memory_space=pltpu.HBM) if i in far else vmem for i in range(len(operands))],
         out_specs=[vmem] * len(outs),
         scratch_shapes=[pltpu.VMEM(s, F32) if isinstance(s, tuple) else s for s in scratch],
-        compiler_params=pltpu.CompilerParams(vmem_limit_bytes=grant),
+        compiler_params=pltpu.CompilerParams(vmem_limit_bytes=VMEM_LIMIT),
     )(*operands)
 
 
@@ -630,7 +718,6 @@
         [(2 * comps + 5, *block), slab_shape, slab_shape, band_shape],
         (displacement, given_load, mass_coef, stiffness, bearing_node, stick_state, slip_prev, bearing_old, bearing_weight),
         far=range(9),
-        grant=VMEM_WHOLE,
         scratch=[field, *small, pltpu.SemaphoreType.DMA((9,))],
     )
     outer = lambda b: b ^ 1
@@ -648,11 +735,21 @@
     corner_a = exchange(corner_a, None, outer)
     devices = sectors * bands
     extended = (rows + 2 * d, layers + 2 * d, radial)
+    all_rows = extended[0]
+    tile_field, tile_block = (comps, all_rows, TILE, radial), (all_rows, TILE, radial)
+    *early, payload = kernel_call(
+        functools.partial(early_kernel, bearings=bearings, sectors=sectors, bands=bands),
+        [(comps, *extended)] * (ITERS + 1)
+        + [extended] * 2
+        + [tile_field, tile_field, tile_block, (comps + 2, all_rows, radial), (devices, 128)],
+        (work, slab_a, slab_b, band_b, corner_a, survey),
+        scratch=[(comps, *extended)] * 2 + [extended] * 3 + [(2, *extended)],
+    )
     *basis, payload = kernel_call(
-        functools.partial(power_kernel, bearings=bearings, sectors=sectors, bands=bands),
+        late_kernel,
         [field] * (ITERS + 1) + [(devices, 128)],
-        (work, slab_a, slab_b, band_b, corner_a, corner_b, survey),
-        scratch=[(comps, *extended)] * (ITERS + 2) + [extended] * 5 + [(2, *extended), (comps + 2, rows + 2 * d, radial)],
+        (*early, payload, corner_b, survey),
+        scratch=[tile_field] * (ITERS + 3) + [tile_block] * 6 + [(2, *tile_block)],
     )
     received = lax.all_to_all(payload, AXES, 0, 0, tiled=True)
     increment, residual, force = kernel_call(

time: 51 us -> 47.5 us (0.931)
  blocking collectives: 26.7 us -> 25 us
  local copies, waits for them, and re-layouts: 1.36 us -> 0 us
    all_to_all x1, blocking collectives: 15.4 us -> 12.6 us  [per_device(): received = lax.all_to_all(payload, AXES, 0, 0, tiled=True)]
    unnamed x2 -> x0, local copies, waits for them, and re-layouts: 1.36 us -> none
    all_to_all x1, blocking collectives: 11.3 us -> 12.3 us  [per_device(): survey = lax.all_to_all(survey, AXES, 0, 0, tiled=True)]
    pallas_call x5 -> x6, Pallas kernels: 13 us -> 12.6 us  [kernel_call(): pl.pallas_call(body, out_shape=[jax.ShapeDtypeStruct(s, F32) for s in out...]
  transfers between devices with their start and end apart: 5 -> 5, of which waited for: 1 -> 1; matrix products, arithmetic and copies ran while one was open for 0% -> 0% of each run, Pallas kernels for 4% -> 14%
where the time goes in v3:
time: 47.5 us; the launch traced here: 47.3 us
  blocking collectives  25 us (53%)
  Pallas kernels  12.6 us (27%)
  starting transfers between devices  7.98 us (17%)
  waiting for transfers between devices  1.04 us (2%)
  between operations  0.7 us (1%)
    all_to_all x1, blocking collectives, per_device(): received = lax.all_to_all(payload, AXES, 0, 0, tiled=True)  12.6 us
    pallas_call x6, Pallas kernels, kernel_call(): pl.pallas_call(body, out_shape=[jax.ShapeDtypeStruct(s, F32) for s in out...  12.6 us
    all_to_all x1, blocking collectives, per_device(): survey = lax.all_to_all(survey, AXES, 0, 0, tiled=True)  12.3 us
    ppermute x5, starting transfers between devices, exchange(): return lax.ppermute(x, AXES, pairs)  7.98 us
    ppermute x5, waiting for transfers between devices, exchange(): return lax.ppermute(x, AXES, pairs)  1.04 us
  transfers between devices with their start and end apart: 5, of which 1 were waited for; matrix products, arithmetic and copies ran while one was open for 0% of the time, Pallas kernels for 14%

profile of v3, /device:TPU:0, one launch (start us, length us, event | category | flops | bytes accessed | tf_op | source)
XLA Modules:
  0.0 47.3 jit_solution(5794466549690771782)
XLA Ops:
  0.6 2.3 %shard_map.112 = (f32[11,8,16,256]{3,2,1,0:T(8,128)S(1)}, f32[376,256]{1,0:T(8,128)S(1)}, f32[376,256]{1,0:T(8,128)S(1)}, f32[32,8,256]{2,1,0:T(8,128)S(1)}) custom-call(f32[3,8,16,256]{3,2,1,0:T(8,128)} %u_far.1, f32[3,8,16,256]{3,2,1,0:T(8,128)} %load_far.1, f32[8,16,256]{2,1,0:T(8,128)} %mass_far.1, f32[8,16,256]{2,1,0:T(8,128)} %stiff_far.1, s32[4]{0:T(128)} %node_far.1, ...), custom_call_target="tpu_custom_call" | custom-call | tf_op jit(solution)/shard_map/pallas_call | solution.py:668
  2.9 3.0 %collective-permute-start = (f32[376,256]{1,0:T(8,128)S(1)}, f32[376,256]{1,0:T(8,128)S(1)}, u32[]{:S(2)}, u32[]{:S(2)}) collective-permute-start(f32[376,256]{1,0:T(8,128)S(1)} %get-tuple-element.28), channel_id=1, source_target_pairs={{0,4},{1,5},{2,6},{3,7},{4,0},{5,1},{6,2},{7,3},{8,12},{9,13},{10,... | collective-permute-start | bytes 1155080 | tf_op jit(solution)/shard_map/ppermute | solution.py:703
  5.9 3.6 %collective-permute-start.1 = (f32[376,256]{1,0:T(8,128)S(1)}, f32[376,256]{1,0:T(8,128)S(1)}, u32[]{:S(2)}, u32[]{:S(2)}) collective-permute-start(f32[376,256]{1,0:T(8,128)S(1)} %get-tuple-element.29), channel_id=1, source_target_pairs={{0,28},{1,29},{2,30},{3,31},{4,8},{5,9},{6,10},{7,11},{8,4},{9,5},... | collective-permute-start | bytes 1155080 | tf_op jit(solution)/shard_map/ppermute | solution.py:703
  9.5 0.7 %collective-permute-start.2 = (f32[32,8,256]{2,1,0:T(8,128)S(1)}, f32[32,8,256]{2,1,0:T(8,128)S(1)}, u32[]{:S(2)}, u32[]{:S(2)}) collective-permute-start(f32[32,8,256]{2,1,0:T(8,128)S(1)} %get-tuple-element.30), channel_id=1, source_target_pairs={{1,2},{2,1},{5,6},{6,5},{9,10},{10,9},{13,14},{14,13},{17,18},{18,... | collective-permute-start | bytes 786440 | tf_op jit(solution)/shard_map/ppermute | solution.py:703
  10.2 2.0 %shard_map.113 = f32[32,128]{1,0:T(8,128)S(1)} custom-call(f32[11,8,16,256]{3,2,1,0:T(8,128)S(1)} %get-tuple-element.27.work), custom_call_target="tpu_custom_call" | custom-call | tf_op jit(solution)/shard_map/pallas_call | solution.py:668
  12.1 12.3 %all_to_all.22 = f32[32,1,128]{2,1,0:T(1,128)S(1)} all-to-all(f32[32,1,128]{2,1,0:T(1,128)S(1)} %bitcast.13), channel_id=1, replica_groups=mesh['sector'=8,'band'=4] {'sector','band'}, dimensions={0} | all-to-all | bytes 32768 | tf_op jit(solution)/shard_map/all_to_all | solution.py:728
  24.5 0.0 collective-permute-done.2.band_b
  24.5 0.0 collective-permute-done.slab_a
  24.5 0.0 collective-permute-done.1.slab_b
  24.5 0.2 shard_map.114
  24.6 0.1 collective-permute-start.3
  24.7 0.7 %collective-permute-start.4 = (f32[16,8,256]{2,1,0:T(8,128)S(1)}, f32[16,8,256]{2,1,0:T(8,128)S(1)}, u32[]{:S(2)}, u32[]{:S(2)}) collective-permute-start(f32[16,8,256]{2,1,0:T(8,128)S(1)} %get-tuple-element.44), channel_id=1, source_target_pairs={{1,2},{2,1},{5,6},{6,5},{9,10},{10,9},{13,14},{14,13},{17,18},{18,... | collective-permute-start | bytes 393224 | tf_op jit(solution)/shard_map/ppermute | solution.py:703
  25.4 1.0 %collective-permute-done.3.corner_a = f32[48,8,256]{2,1,0:T(8,128)S(1)} collective-permute-done((f32[48,8,256]{2,1,0:T(8,128)S(1)}, f32[48,8,256]{2,1,0:T(8,128)S(1)}, u32[]{:S(2)}, u32[]{:S(2)}) %collective-permute-start.3) | collective-permute-done | bytes 393248 | tf_op jit(solution)/shard_map/ppermute | solution.py:703
  26.4 4.9 %shard_map.115 = (f32[3,16,24,256]{3,2,1,0:T(8,128)S(1)}, f32[3,16,24,256]{3,2,1,0:T(8,128)S(1)}, f32[3,16,24,256]{3,2,1,0:T(8,128)S(1)}, f32[3,16,24,256]{3,2,1...) custom-call(f32[11,8,16,256]{3,2,1,0:T(8,128)S(1)} %get-tuple-elemen, ...), custom_call_target="tpu_custom_call" | custom-call | tf_op jit(solution)/shard_map/pallas_call | solution.py:668
  31.3 0.0 collective-permute-done.4.corner_b
  31.3 2.0 %shard_map.116 = (f32[3,8,16,256]{3,2,1,0:T(8,128)S(1)}, f32[3,8,16,256]{3,2,1,0:T(8,128)S(1)}, f32[3,8,16,256]{3,2,1,0:T(8,128)S(1)}, f32[3,8,16,256]{3,2,1,0:T...) custom-call(f32[3,16,24,256]{3,2,1,0:T(8,128)S(1)} %get-tuple-element.32.t0, ...), custom_call_target="tpu_custom_call" | custom-call | tf_op jit(solution)/shard_map/pallas_call | solution.py:668
  33.4 12.6 %all_to_all.23 = f32[32,1,128]{2,1,0:T(1,128)S(1)} all-to-all(f32[32,1,128]{2,1,0:T(1,128)S(1)} %bitcast.14), channel_id=1, replica_groups=mesh['sector'=8,'band'=4] {'sector','band'}, dimensions={0} | all-to-all | bytes 32768 | tf_op jit(solution)/shard_map/all_to_all | solution.py:754
  46.0 1.3 %shard_map.117 = (f32[3,8,16,256]{3,2,1,0:T(8,128)}, f32[3,8,16,256]{3,2,1,0:T(8,128)}, f32[3,4]{1,0:T(4,128)}) custom-call(f32[32,128]{1,0:T(8,128)S(1)} %bitcast.12, f32[32,128]{1,0:T(8,128)S(1)} %bitcast.11, f32[3,8,16,256]{3,2,1,0:T(8,128)S(1)} %get-tuple-element.46.b0, f32[3,8,16,256]{3,2,1,0:T(8,128)S(1)} %get-tuple-element.47.b1, ...), custom_call_target="tpu_custom_call" | custom-call | tf_op jit(solution)/shard_map/pallas_call | solution.py:668
Async XLA Ops:
  2.9 21.6 %collective-permute-start = (f32[376,256]{1,0:T(8,128)S(1)}, f32[376,256]{1,0:T(8,128)S(1)}, u32[]{:S(2)}, u32[]{:S(2)}) collective-permute-start(f32[376,256]{1,0:T(8,128)S(1)} %get-tuple-element.28), channel_id=1, source_target_pairs={{0,4},{1,5},{2,6},{3,7},{4,0},{5,1},{6,2},{7,3},{8,12},{9,13},{10,... | collective-permute-start | bytes 1155080 | tf_op jit(solution)/shard_map/ppermute | solution.py:703
  5.9 18.6 %collective-permute-start.1 = (f32[376,256]{1,0:T(8,128)S(1)}, f32[376,256]{1,0:T(8,128)S(1)}, u32[]{:S(2)}, u32[]{:S(2)}) collective-permute-start(f32[376,256]{1,0:T(8,128)S(1)} %get-tuple-element.29), channel_id=1, source_target_pairs={{0,28},{1,29},{2,30},{3,31},{4,8},{5,9},{6,10},{7,11},{8,4},{9,5},... | collective-permute-start | bytes 1155080 | tf_op jit(solution)/shard_map/ppermute | solution.py:703
  9.5 15.0 %collective-permute-start.2 = (f32[32,8,256]{2,1,0:T(8,128)S(1)}, f32[32,8,256]{2,1,0:T(8,128)S(1)}, u32[]{:S(2)}, u32[]{:S(2)}) collective-permute-start(f32[32,8,256]{2,1,0:T(8,128)S(1)} %get-tuple-element.30), channel_id=1, source_target_pairs={{1,2},{2,1},{5,6},{6,5},{9,10},{10,9},{13,14},{14,13},{17,18},{18,... | collective-permute-start | bytes 786440 | tf_op jit(solution)/shard_map/ppermute | solution.py:703
  24.6 1.8 %collective-permute-start.3 = (f32[48,8,256]{2,1,0:T(8,128)S(1)}, f32[48,8,256]{2,1,0:T(8,128)S(1)}, u32[]{:S(2)}, u32[]{:S(2)}) collective-permute-start(f32[48,8,256]{2,1,0:T(8,128)S(1)} %get-tuple-element.31), channel_id=1, source_target_pairs={{0,1},{1,0},{2,3},{3,2},{4,5},{5,4},{6,7},{7,6},{8,9},{9,8},{10,11... | collective-permute-start | bytes 1179656 | tf_op jit(solution)/shard_map/ppermute | solution.py:703
  24.7 6.6 %collective-permute-start.4 = (f32[16,8,256]{2,1,0:T(8,128)S(1)}, f32[16,8,256]{2,1,0:T(8,128)S(1)}, u32[]{:S(2)}, u32[]{:S(2)}) collective-permute-start(f32[16,8,256]{2,1,0:T(8,128)S(1)} %get-tuple-element.44), channel_id=1, source_target_pairs={{1,2},{2,1},{5,6},{6,5},{9,10},{10,9},{13,14},{14,13},{17,18},{18,... | collective-permute-start | bytes 393224 | tf_op jit(solution)/shard_map/ppermute | solution.py:703

commit v4 on v3

--- a/solution.py
+++ b/solution.py
@@ -43,6 +43,16 @@
 
 def behind(x, axis):
     return pltpu.roll(x, 1, axis)
+
+
+def shifted(x, axis, by):
+    size = 8 if axis == 0 else 128
+    count = x.shape[axis] // size
+    parts = [lax.slice_in_dim(x, i * size, (i + 1) * size, axis=axis) for i in range(count)]
+    turned = [pltpu.roll(p, size - 1 if by == 1 else 1, axis) for p in parts]
+    edge = lax.broadcasted_iota(jnp.int32, parts[0].shape, axis) == (size - 1 if by == 1 else 0)
+    out = [jnp.where(edge, turned[i + by], turned[i]) if 0 <= i + by < count else turned[i] for i in range(count)]
+    return out[0] if count == 1 else jnp.concatenate(out, axis=axis)
 
 
 def round_up(n, multiple):
@@ -88,9 +98,16 @@
     comps, rows, layers, width = load.shape
     d = DEPTH
     r, u, cond, mass, stiff = parts_of(work)
-    fields = ((stiff_far, stiff), (u_far, u), (mass_far, mass), (load_far, load))
+    half = rows // 2
+    fields = [(stiff_far, stiff)]
+    for part in (pl.ds(0, half), pl.ds(half, rows - half)):
+        fields += [
+            (u_far.at[:, part], u.at[:, part]),
+            (mass_far.at[part], mass.at[part]),
+            (load_far.at[:, part], load.at[:, part]),
+        ]
     small = ((node_far, node), (stick_far, stick), (slip_far, slip), (old_far, old), (weight_far, weight))
-    moves = [pltpu.make_async_copy(src, dst, arrived.at[n]) for n, (src, dst) in enumerate(fields + small)]
+    moves = [pltpu.make_async_copy(src, dst, arrived.at[n]) for n, (src, dst) in enumerate([*fields, *small])]
     for move in moves:
         move.start()
     lane = lax.broadcasted_iota(jnp.int32, (layers, width), 1)
@@ -101,10 +118,14 @@
         cond[0, a] = jnp.where(lane < width - 1, conductance(k, ahead(k, 1)), 0.0)
         cond[1, a] = jnp.where(layer < layers - 1, conductance(k, ahead(k, 0)), 0.0)
         cond[2, a] = conductance(k, stiff[a + 1]) if a + 1 < rows else jnp.zeros((layers, width), F32)
-    for move in moves[1 : len(fields)]:
-        move.wait()
     before = [None] * comps
     for a in range(rows):
+        if a == 0:
+            for move in moves[1:4]:
+                move.wait()
+        if a == half - 1:
+            for move in moves[4:7]:
+                move.wait()
         k_r, k_h, k_s = cond[0, a], cond[1, a], cond[2, a]
         m = mass[a]
         for c in range(comps):
@@ -340,7 +361,7 @@
 def early_kernel(
     work, slab_a, slab_b, band_b, corner_a, survey,
     t0, t1, t2, t3, t4, kx, kh, late_t, late_u, late_m, raft, payload,
-    raw, ux, mx, ks, kr, diag,
+    raw, ux, mx, ks, kr, kh_back, kr_back, diag,
     *, bearings, sectors, bands,
 ):
     r, u, _, mass, stiff = parts_of(work)
@@ -457,8 +478,8 @@
     def faces(a, carry):
         k = kx[a]
         k_h = conductance(k, ahead(k, 0))
-        kh[a] = k_h
-        kr[a] = jnp.where(lane < width - 1, conductance(k, ahead(k, 1)), 0.0)
+        k_r = jnp.where(lane < width - 1, conductance(k, ahead(k, 1)), 0.0)
+        kh[a], kh_back[a], kr[a], kr_back[a] = k_h, behind(k_h, 0), k_r, behind(k_r, 1)
         ks[a] = conductance(k, kx[jnp.minimum(a + 1, all_rows - 1)])
         for c in range(comps):
             v = ux[c, a]
@@ -476,8 +497,7 @@
             t0[c, a + 1] = t0[c, a + 1] - flux
 
     def diagonals(a, carry):
-        k_h, k_r = kh[a], kr[a]
-        around = k_h + behind(k_h, 0) + k_r + behind(k_r, 1) + ks[a] + ks[a - 1]
+        around = kh[a] + kh_back[a] + kr[a] + kr_back[a] + ks[a] + ks[a - 1]
         diag[0, a] = mx[a] + COMPONENT_SCALE[0] * around + jnp.where(layer == d, raft[comps, pl.ds(a, 1)], 0.0)
         diag[1, a] = mx[a] + COMPONENT_SCALE[2] * around + jnp.where(layer == d, raft[comps + 1, pl.ds(a, 1)], 0.0)
         return carry
@@ -486,31 +506,37 @@
 
     levels = (t0, t1, t2, t3, t4)
     shift_of, link_of = coefficients(survey[...])
+    within = lax.broadcasted_iota(jnp.int32, (8, width), 0)
     for step in range(1, ITERS + 1):
         src, dst = levels[step - 1], levels[step]
-        a_k = jnp.broadcast_to(shift_of[step - 1], (all_layers, width))
-        c_k = jnp.broadcast_to(link_of[step - 1], (all_layers, width)) if step > 1 else None
-
-        def apply(a, carry):
-            k_h, k_r, k_next, k_back = kh[a], kr[a], ks[a], ks[a - 1]
-            for c in range(comps):
-                v = src[c, a]
-                around = k_next * src[c, a + 1] + k_back * src[c, a - 1]
-                around = around + (k_h * ahead(v, 0) + behind(k_h * v, 0))
-                around = around + (k_r * ahead(v, 1) + behind(k_r * v, 1))
-                centre = (diag[0 if c < 2 else 1, a] - a_k) * v
-                if step > 1:
-                    centre = centre - c_k * levels[step - 2][c, a]
-                dst[c, a] = centre - (around if COMPONENT_SCALE[c] == 1.0 else COMPONENT_SCALE[c] * around)
-            return carry
-
-        lax.fori_loop(step, all_rows - step, apply, 0, unroll=True)
+        a_k = jnp.broadcast_to(shift_of[step - 1], (8, width))
+        c_k = jnp.broadcast_to(link_of[step - 1], (8, width)) if step > 1 else None
+        for a in range(step, all_rows - step):
+            for start in range(0, all_layers, 8):
+                part = slice(start, start + 8)
+                k_h, k_low, k_r, k_left = kh[a, part], kh_back[a, part], kr[a, part], kr_back[a, part]
+                k_next, k_back = ks[a, part], ks[a - 1, part]
+                centres = [diag[n, a, part] - a_k for n in range(2)]
+                for c in range(comps):
+                    v = src[c, a, part]
+                    upper, lower = ahead(v, 0), behind(v, 0)
+                    if start + 8 < all_layers:
+                        upper = jnp.where(within == 7, src[c, a, start + 8 : start + 9], upper)
+                    if start:
+                        lower = jnp.where(within == 0, src[c, a, start - 1 : start], lower)
+                    around = k_next * src[c, a + 1, part] + k_back * src[c, a - 1, part]
+                    around = around + (k_h * upper + k_low * lower)
+                    around = around + (k_r * shifted(v, 1, 1) + k_left * shifted(v, 1, -1))
+                    centre = centres[0 if c < 2 else 1] * v
+                    if step > 1:
+                        centre = centre - c_k * levels[step - 2][c, a, part]
+                    dst[c, a, part] = centre - (around if COMPONENT_SCALE[c] == 1.0 else COMPONENT_SCALE[c] * around)
 
 
 def late_kernel(
     t0, t1, t2, t3, t4, kx, kh, late_t, late_u, late_m, raft, payload_in, corner_b, survey,
     b0, b1, b2, b3, b4, payload,
-    s0, s1, s2, s3, s4, raw, ux, k_tile, m_tile, ks, kh_tile, kh_back, kr, diag,
+    s0, s1, s2, s3, s4, raw, ux, k_tile, m_tile, ks, kh_tile, kh_back, kr, kr_back, diag,
 ):
     comps, rows, layers, width = b0.shape
     d = DEPTH
@@ -553,7 +579,8 @@
             k = k_tile[a]
             k_h = conductance(k, upper(k, kx, a))
             kh_tile[a], kh_back[a] = k_h, lower(k_h, kh, a)
-            kr[a] = jnp.where(lane < width - 1, conductance(k, ahead(k, 1)), 0.0)
+            k_r = jnp.where(lane < width - 1, conductance(k, ahead(k, 1)), 0.0)
+            kr[a], kr_back[a] = k_r, behind(k_r, 1)
             if a + 1 < all_rows:
                 ks[a] = conductance(k, k_tile[a + 1])
             for c in range(comps):
@@ -569,23 +596,22 @@
                 s0[c, a] = s0[c, a] + flux
                 s0[c, a + 1] = s0[c, a + 1] - flux
         for a in range(1, all_rows - 1):
-            k_r = kr[a]
-            around = kh_tile[a] + kh_back[a] + k_r + behind(k_r, 1) + ks[a] + ks[a - 1]
+            around = kh_tile[a] + kh_back[a] + kr[a] + kr_back[a] + ks[a] + ks[a - 1]
             for n, scale in enumerate((COMPONENT_SCALE[0], COMPONENT_SCALE[2])):
                 total = m_tile[a] + scale * around
                 diag[n, a] = total + jnp.where(on_raft, raft[comps + n, a : a + 1], 0.0) if even else total
         for step in range(1, ITERS + 1):
             src, dst = late[step - 1], late[step]
             for a in range(step, all_rows - step):
-                k_r = kr[a]
+                centres = [diag[n, a] - shift_of[step - 1] for n in range(2)]
                 for c in range(comps):
                     v = src[c, a]
                     around = ks[a] * src[c, a + 1] + ks[a - 1] * src[c, a - 1]
                     around = around + (
                         kh_tile[a] * upper(v, early[step - 1], c, a) + kh_back[a] * lower(v, early[step - 1], c, a)
                     )
-                    around = around + (k_r * ahead(v, 1) + behind(k_r * v, 1))
-                    centre = (diag[0 if c < 2 else 1, a] - shift_of[step - 1]) * v
+                    around = around + (kr[a] * shifted(v, 1, 1) + kr_back[a] * shifted(v, 1, -1))
+                    centre = centres[0 if c < 2 else 1] * v
                     if step > 1:
                         centre = centre - link_of[step - 1] * late[step - 2][c, a]
                     dst[c, a] = centre - (around if COMPONENT_SCALE[c] == 1.0 else COMPONENT_SCALE[c] * around)
@@ -718,7 +744,7 @@
         [(2 * comps + 5, *block), slab_shape, slab_shape, band_shape],
         (displacement, given_load, mass_coef, stiffness, bearing_node, stick_state, slip_prev, bearing_old, bearing_weight),
         far=range(9),
-        scratch=[field, *small, pltpu.SemaphoreType.DMA((9,))],
+        scratch=[field, *small, pltpu.SemaphoreType.DMA((12,))],
     )
     outer = lambda b: b ^ 1
     slab_b = exchange(slab_b, pair_down)
@@ -743,13 +769,13 @@
         + [extended] * 2
         + [tile_field, tile_field, tile_block, (comps + 2, all_rows, radial), (devices, 128)],
         (work, slab_a, slab_b, band_b, corner_a, survey),
-        scratch=[(comps, *extended)] * 2 + [extended] * 3 + [(2, *extended)],
+        scratch=[(comps, *extended)] * 2 + [extended] * 5 + [(2, *extended)],
     )
     *basis, payload = kernel_call(
         late_kernel,
         [field] * (ITERS + 1) + [(devices, 128)],
         (*early, payload, corner_b, survey),
-        scratch=[tile_field] * (ITERS + 3) + [tile_block] * 6 + [(2, *tile_block)],
+        scratch=[tile_field] * (ITERS + 3) + [tile_block] * 7 + [(2, *tile_block)],
     )
     received = lax.all_to_all(payload, AXES, 0, 0, tiled=True)
     increment, residual, force = kernel_call(

time: 47.5 us -> 47 us (0.989)
  no operation moved by 1% of the time
where the time goes in v4:
time: 47 us; the launch traced here: 46.8 us
  blocking collectives  24.9 us (53%)
  Pallas kernels  12.2 us (26%)
  starting transfers between devices  7.98 us (17%)
  waiting for transfers between devices  1.04 us (2%)
  between operations  0.7 us (1%)
    all_to_all x1, blocking collectives, per_device(): received = lax.all_to_all(payload, AXES, 0, 0, tiled=True)  12.6 us
    all_to_all x1, blocking collectives, per_device(): survey = lax.all_to_all(survey, AXES, 0, 0, tiled=True)  12.3 us
    pallas_call x6, Pallas kernels, kernel_call(): pl.pallas_call(body, out_shape=[jax.ShapeDtypeStruct(s, F32) for s in out...  12.2 us
    ppermute x5, starting transfers between devices, exchange(): return lax.ppermute(x, AXES, pairs)  7.98 us
    ppermute x5, waiting for transfers between devices, exchange(): return lax.ppermute(x, AXES, pairs)  1.04 us
  transfers between devices with their start and end apart: 5, of which 1 were waited for; matrix products, arithmetic and copies ran while one was open for 0% of the time, Pallas kernels for 14%

profile of v4, /device:TPU:0, one launch (start us, length us, event | category | flops | bytes accessed | tf_op | source)
XLA Modules:
  0.0 46.8 jit_solution(16388526833489981090)
XLA Ops:
  0.6 1.9 %shard_map.112 = (f32[11,8,16,256]{3,2,1,0:T(8,128)S(1)}, f32[376,256]{1,0:T(8,128)S(1)}, f32[376,256]{1,0:T(8,128)S(1)}, f32[32,8,256]{2,1,0:T(8,128)S(1)}) custom-call(f32[3,8,16,256]{3,2,1,0:T(8,128)} %u_far.1, f32[3,8,16,256]{3,2,1,0:T(8,128)} %load_far.1, f32[8,16,256]{2,1,0:T(8,128)} %mass_far.1, f32[8,16,256]{2,1,0:T(8,128)} %stiff_far.1, s32[4]{0:T(128)} %node_far.1, ...), custom_call_target="tpu_custom_call" | custom-call | tf_op jit(solution)/shard_map/pallas_call | solution.py:694
  2.5 3.0 %collective-permute-start = (f32[376,256]{1,0:T(8,128)S(1)}, f32[376,256]{1,0:T(8,128)S(1)}, u32[]{:S(2)}, u32[]{:S(2)}) collective-permute-start(f32[376,256]{1,0:T(8,128)S(1)} %get-tuple-element.28), channel_id=1, source_target_pairs={{0,4},{1,5},{2,6},{3,7},{4,0},{5,1},{6,2},{7,3},{8,12},{9,13},{10,... | collective-permute-start | bytes 1155080 | tf_op jit(solution)/shard_map/ppermute | solution.py:729
  5.5 3.6 %collective-permute-start.1 = (f32[376,256]{1,0:T(8,128)S(1)}, f32[376,256]{1,0:T(8,128)S(1)}, u32[]{:S(2)}, u32[]{:S(2)}) collective-permute-start(f32[376,256]{1,0:T(8,128)S(1)} %get-tuple-element.29), channel_id=1, source_target_pairs={{0,28},{1,29},{2,30},{3,31},{4,8},{5,9},{6,10},{7,11},{8,4},{9,5},... | collective-permute-start | bytes 1155080 | tf_op jit(solution)/shard_map/ppermute | solution.py:729
  9.1 0.7 %collective-permute-start.2 = (f32[32,8,256]{2,1,0:T(8,128)S(1)}, f32[32,8,256]{2,1,0:T(8,128)S(1)}, u32[]{:S(2)}, u32[]{:S(2)}) collective-permute-start(f32[32,8,256]{2,1,0:T(8,128)S(1)} %get-tuple-element.30), channel_id=1, source_target_pairs={{1,2},{2,1},{5,6},{6,5},{9,10},{10,9},{13,14},{14,13},{17,18},{18,... | collective-permute-start | bytes 786440 | tf_op jit(solution)/shard_map/ppermute | solution.py:729
  9.8 2.0 %shard_map.113 = f32[32,128]{1,0:T(8,128)S(1)} custom-call(f32[11,8,16,256]{3,2,1,0:T(8,128)S(1)} %get-tuple-element.27.work), custom_call_target="tpu_custom_call" | custom-call | tf_op jit(solution)/shard_map/pallas_call | solution.py:694
  11.7 12.3 %all_to_all.22 = f32[32,1,128]{2,1,0:T(1,128)S(1)} all-to-all(f32[32,1,128]{2,1,0:T(1,128)S(1)} %bitcast.13), channel_id=1, replica_groups=mesh['sector'=8,'band'=4] {'sector','band'}, dimensions={0} | all-to-all | bytes 32768 | tf_op jit(solution)/shard_map/all_to_all | solution.py:754
  24.1 0.0 collective-permute-done.2.band_b
  24.1 0.0 collective-permute-done.slab_a
  24.1 0.0 collective-permute-done.1.slab_b
  24.1 0.2 shard_map.114
  24.3 0.1 collective-permute-start.3
  24.3 0.7 %collective-permute-start.4 = (f32[16,8,256]{2,1,0:T(8,128)S(1)}, f32[16,8,256]{2,1,0:T(8,128)S(1)}, u32[]{:S(2)}, u32[]{:S(2)}) collective-permute-start(f32[16,8,256]{2,1,0:T(8,128)S(1)} %get-tuple-element.44), channel_id=1, source_target_pairs={{1,2},{2,1},{5,6},{6,5},{9,10},{10,9},{13,14},{14,13},{17,18},{18,... | collective-permute-start | bytes 393224 | tf_op jit(solution)/shard_map/ppermute | solution.py:729
  25.0 1.0 %collective-permute-done.3.corner_a = f32[48,8,256]{2,1,0:T(8,128)S(1)} collective-permute-done((f32[48,8,256]{2,1,0:T(8,128)S(1)}, f32[48,8,256]{2,1,0:T(8,128)S(1)}, u32[]{:S(2)}, u32[]{:S(2)}) %collective-permute-start.3) | collective-permute-done | bytes 393248 | tf_op jit(solution)/shard_map/ppermute | solution.py:729
  26.0 4.8 %shard_map.115 = (f32[3,16,24,256]{3,2,1,0:T(8,128)S(1)}, f32[3,16,24,256]{3,2,1,0:T(8,128)S(1)}, f32[3,16,24,256]{3,2,1,0:T(8,128)S(1)}, f32[3,16,24,256]{3,2,1...) custom-call(f32[11,8,16,256]{3,2,1,0:T(8,128)S(1)} %get-tuple-elemen, ...), custom_call_target="tpu_custom_call" | custom-call | tf_op jit(solution)/shard_map/pallas_call | solution.py:694
  30.9 0.0 collective-permute-done.4.corner_b
  30.9 2.0 %shard_map.116 = (f32[3,8,16,256]{3,2,1,0:T(8,128)S(1)}, f32[3,8,16,256]{3,2,1,0:T(8,128)S(1)}, f32[3,8,16,256]{3,2,1,0:T(8,128)S(1)}, f32[3,8,16,256]{3,2,1,0:T...) custom-call(f32[3,16,24,256]{3,2,1,0:T(8,128)S(1)} %get-tuple-element.32.t0, ...), custom_call_target="tpu_custom_call" | custom-call | tf_op jit(solution)/shard_map/pallas_call | solution.py:694
  32.9 12.6 %all_to_all.23 = f32[32,1,128]{2,1,0:T(1,128)S(1)} all-to-all(f32[32,1,128]{2,1,0:T(1,128)S(1)} %bitcast.14), channel_id=1, replica_groups=mesh['sector'=8,'band'=4] {'sector','band'}, dimensions={0} | all-to-all | bytes 32768 | tf_op jit(solution)/shard_map/all_to_all | solution.py:780
  45.5 1.3 %shard_map.117 = (f32[3,8,16,256]{3,2,1,0:T(8,128)}, f32[3,8,16,256]{3,2,1,0:T(8,128)}, f32[3,4]{1,0:T(4,128)}) custom-call(f32[32,128]{1,0:T(8,128)S(1)} %bitcast.12, f32[32,128]{1,0:T(8,128)S(1)} %bitcast.11, f32[3,8,16,256]{3,2,1,0:T(8,128)S(1)} %get-tuple-element.46.b0, f32[3,8,16,256]{3,2,1,0:T(8,128)S(1)} %get-tuple-element.47.b1, ...), custom_call_target="tpu_custom_call" | custom-call | tf_op jit(solution)/shard_map/pallas_call | solution.py:694
Async XLA Ops:
  2.5 21.6 %collective-permute-start = (f32[376,256]{1,0:T(8,128)S(1)}, f32[376,256]{1,0:T(8,128)S(1)}, u32[]{:S(2)}, u32[]{:S(2)}) collective-permute-start(f32[376,256]{1,0:T(8,128)S(1)} %get-tuple-element.28), channel_id=1, source_target_pairs={{0,4},{1,5},{2,6},{3,7},{4,0},{5,1},{6,2},{7,3},{8,12},{9,13},{10,... | collective-permute-start | bytes 1155080 | tf_op jit(solution)/shard_map/ppermute | solution.py:729
  5.5 18.6 %collective-permute-start.1 = (f32[376,256]{1,0:T(8,128)S(1)}, f32[376,256]{1,0:T(8,128)S(1)}, u32[]{:S(2)}, u32[]{:S(2)}) collective-permute-start(f32[376,256]{1,0:T(8,128)S(1)} %get-tuple-element.29), channel_id=1, source_target_pairs={{0,28},{1,29},{2,30},{3,31},{4,8},{5,9},{6,10},{7,11},{8,4},{9,5},... | collective-permute-start | bytes 1155080 | tf_op jit(solution)/shard_map/ppermute | solution.py:729
  9.1 15.0 %collective-permute-start.2 = (f32[32,8,256]{2,1,0:T(8,128)S(1)}, f32[32,8,256]{2,1,0:T(8,128)S(1)}, u32[]{:S(2)}, u32[]{:S(2)}) collective-permute-start(f32[32,8,256]{2,1,0:T(8,128)S(1)} %get-tuple-element.30), channel_id=1, source_target_pairs={{1,2},{2,1},{5,6},{6,5},{9,10},{10,9},{13,14},{14,13},{17,18},{18,... | collective-permute-start | bytes 786440 | tf_op jit(solution)/shard_map/ppermute | solution.py:729
  24.3 1.8 %collective-permute-start.3 = (f32[48,8,256]{2,1,0:T(8,128)S(1)}, f32[48,8,256]{2,1,0:T(8,128)S(1)}, u32[]{:S(2)}, u32[]{:S(2)}) collective-permute-start(f32[48,8,256]{2,1,0:T(8,128)S(1)} %get-tuple-element.31), channel_id=1, source_target_pairs={{0,1},{1,0},{2,3},{3,2},{4,5},{5,4},{6,7},{7,6},{8,9},{9,8},{10,11... | collective-permute-start | bytes 1179656 | tf_op jit(solution)/shard_map/ppermute | solution.py:729
  24.3 6.5 %collective-permute-start.4 = (f32[16,8,256]{2,1,0:T(8,128)S(1)}, f32[16,8,256]{2,1,0:T(8,128)S(1)}, u32[]{:S(2)}, u32[]{:S(2)}) collective-permute-start(f32[16,8,256]{2,1,0:T(8,128)S(1)} %get-tuple-element.44), channel_id=1, source_target_pairs={{1,2},{2,1},{5,6},{6,5},{9,10},{10,9},{13,14},{14,13},{17,18},{18,... | collective-permute-start | bytes 393224 | tf_op jit(solution)/shard_map/ppermute | solution.py:729

commit v5 on v4

--- a/solution.py
+++ b/solution.py
@@ -73,16 +73,30 @@
 class SectorSlab:
     def __init__(self, comps, layers):
         d = DEPTH
-        self.layers = layers
-        self.stiff = comps * d * layers
-        self.mass = self.stiff + d * layers
-        self.disp = self.mass + (d - 1) * layers
-        self.low = self.disp + comps * layers
-        self.high = self.low + comps * d
-        self.rows = round_up(self.high + comps * d, 8)
+        self.comps, self.layers = comps, layers
+        self.stiff = comps * (d - 1) * layers
+        self.mass = self.stiff + (d - 1) * layers
+        self.disp = self.mass + (d - 2) * layers
+        self.image = self.disp + comps * layers
+        self.low = self.image + comps * layers
+        self.rims = comps * (d - 1) + comps + 2
+        self.high = self.low + self.rims
+        self.rows = round_up(self.high + self.rims, 8)
 
     def residual_at(self, c, i):
-        return (c * DEPTH + i) * self.layers
+        return (c * (DEPTH - 1) + i) * self.layers
+
+    def rim_disp(self, c, n):
+        return c * (DEPTH - 1) + n - 2
+
+    def rim_residual(self, c):
+        return self.comps * (DEPTH - 1) + c
+
+    def rim_stiff(self):
+        return self.rims - 2
+
+    def rim_mass(self):
+        return self.rims - 1
 
 
 def parts_of(work):
@@ -163,18 +177,35 @@
     slab = SectorSlab(comps, layers)
     even = lax.rem(lax.axis_index("sector"), 2) == 0
     for out, upper in ((slab_a, even), (slab_b, jnp.logical_not(even))):
-        first = jnp.where(upper, rows - d, 0)
-        for i in range(d):
+
+        def row(n, upper=upper):
+            return jnp.where(upper, rows - n, n - 1)
+
+        for i in range(d - 1):
+            first = jnp.where(upper, rows - (d - 1), 0)
             for c in range(comps):
                 out[pl.ds(slab.residual_at(c, i), layers)] = r[c, first + i]
-                out[pl.ds(slab.low + c * d + i, 1)] = u[c, first + i, 0:1]
-                out[pl.ds(slab.high + c * d + i, 1)] = u[c, first + i, layers - 1 : layers]
             out[pl.ds(slab.stiff + i * layers, layers)] = stiff[first + i]
-        for i in range(d - 1):
-            out[pl.ds(slab.mass + i * layers, layers)] = mass[jnp.where(upper, rows - (d - 1), 0) + i]
-        for c in range(comps):
-            out[pl.ds(slab.disp + c * layers, layers)] = u[c, jnp.where(upper, rows - 1, 0)]
-        end = slab.high + comps * d
+        for i in range(d - 2):
+            out[pl.ds(slab.mass + i * layers, layers)] = mass[jnp.where(upper, rows - (d - 2), 0) + i]
+        at = row(d - 1)
+        k_r, k_h, k_next, k_back = cond[0, at], cond[1, at], cond[2, at], cond[2, at - 1]
+        for c in range(comps):
+            out[pl.ds(slab.disp + c * layers, layers)] = u[c, row(1)]
+            v = r[c, at]
+            flux_r = k_r * (ahead(v, 1) - v)
+            flux_h = k_h * (ahead(v, 0) - v)
+            total = flux_r - behind(flux_r, 1) + flux_h - behind(flux_h, 0)
+            total = total + k_next * (r[c, at + 1] - v) - k_back * (v - r[c, at - 1])
+            out[pl.ds(slab.image + c * layers, layers)] = mass[at] * v - COMPONENT_SCALE[c] * total
+        for group, layer_of in ((slab.low, slice(0, 1)), (slab.high, slice(layers - 1, layers))):
+            for c in range(comps):
+                for n in range(2, d + 1):
+                    out[pl.ds(group + slab.rim_disp(c, n), 1)] = u[c, row(n), layer_of]
+                out[pl.ds(group + slab.rim_residual(c), 1)] = r[c, row(d), layer_of]
+            out[pl.ds(group + slab.rim_stiff(), 1)] = stiff[row(d), layer_of]
+            out[pl.ds(group + slab.rim_mass(), 1)] = mass[row(d - 1), layer_of]
+        end = slab.high + slab.rims
         if slab.rows > end:
             out[pl.ds(end, slab.rows - end)] = jnp.zeros((slab.rows - end, width), F32)
 
@@ -231,6 +262,20 @@
         def step(n, count, above=above):
             return jnp.where(above, n - 1, count - n)
 
+        def rim(at, side=side):
+            return [side[pl.ds(group + at, 1)] for group in (slab.low, slab.high)]
+
+        def stiff_of(n):
+            if n < d:
+                return plane(slab.stiff + step(n, d - 1) * layers)
+            return jnp.concatenate([jnp.broadcast_to(x, (layers // 2, x.shape[1])) for x in rim(slab.rim_stiff())], axis=0)
+
+        def disp_rim(c, n):
+            if n > 1:
+                return rim(slab.rim_disp(c, n))
+            row = plane(slab.disp + c * layers)
+            return [row[0:1], row[layers - 1 :]]
+
         for out, top in ((corner_a, band_even), (corner_b, jnp.logical_not(band_even))):
             put_wedge(
                 out,
@@ -238,11 +283,11 @@
                 comps,
                 layers,
                 top,
-                lambda c, n: plane(slab.residual_at(c, step(n, d))),
-                lambda n: plane(slab.stiff + step(n, d) * layers),
-                lambda n: plane(slab.mass + step(min(n, d - 1), d - 1) * layers),
+                lambda c, n: plane(slab.residual_at(c, step(min(n, d - 1), d - 1))),
+                stiff_of,
+                lambda n: plane(slab.mass + step(min(n, d - 2), d - 2) * layers),
                 lambda c: plane(slab.disp + c * layers),
-                lambda c, n: [side[pl.ds(at + c * d + step(n, d), 1)] for at in (slab.low, slab.high)],
+                disp_rim,
             )
     r, u, _, mass, stiff = parts_of(work)
     put_band(corner_a, 2 * wedge.blocks, r, u, stiff, mass, band_even)
@@ -360,8 +405,8 @@
 
 def early_kernel(
     work, slab_a, slab_b, band_b, corner_a, survey,
-    t0, t1, t2, t3, t4, kx, kh, late_t, late_u, late_m, raft, payload,
-    raw, ux, mx, ks, kr, kh_back, kr_back, diag,
+    t0, t1, t2, t3, t4, kx, kh, late_t, late_u, late_m, late_image, raft, payload,
+    raw, ux, mx, ks, kr, kh_back, kr_back, diag, image, turn,
     *, bearings, sectors, bands,
 ):
     r, u, _, mass, stiff = parts_of(work)
@@ -381,19 +426,33 @@
         kx[d + a, own] = stiff[a]
         mx[d + a, own] = mass[a]
     sides = ((slab_a, sector_even), (slab_b, jnp.logical_not(sector_even)))
+    empty = jnp.zeros((all_layers, width), F32)
     for side, above in sides:
-        base = jnp.where(above, d + rows, 0)
-        nearest = jnp.where(above, d + rows, d - 1)
-        for i in range(d):
-            for c in range(comps):
-                raw[c, base + i, own] = side[pl.ds(slab.residual_at(c, i), layers)]
-                ux[c, base + i, d : d + 1] = side[pl.ds(slab.low + c * d + i, 1)]
-                ux[c, base + i, d + layers - 1 : d + layers] = side[pl.ds(slab.high + c * d + i, 1)]
-            kx[base + i, own] = side[pl.ds(slab.stiff + i * layers, layers)]
+
+        def row(n, above=above):
+            return jnp.where(above, d + rows - 1 + n, d - n)
+
+        for c in range(comps):
+            raw[c, row(d)] = empty
+        kx[row(d)], mx[row(d - 1)] = empty, empty
         for i in range(d - 1):
-            mx[jnp.where(above, d + rows, 1) + i, own] = side[pl.ds(slab.mass + i * layers, layers)]
-        for c in range(comps):
-            ux[c, nearest, own] = side[pl.ds(slab.disp + c * layers, layers)]
+            first = jnp.where(above, d + rows, 1)
+            for c in range(comps):
+                raw[c, first + i, own] = side[pl.ds(slab.residual_at(c, i), layers)]
+            kx[first + i, own] = side[pl.ds(slab.stiff + i * layers, layers)]
+        for i in range(d - 2):
+            mx[jnp.where(above, d + rows, 2) + i, own] = side[pl.ds(slab.mass + i * layers, layers)]
+        for c in range(comps):
+            ux[c, row(1), own] = side[pl.ds(slab.disp + c * layers, layers)]
+            image[c, jnp.where(above, 1, 0), own] = side[pl.ds(slab.image + c * layers, layers)]
+        for group, at in ((slab.low, slice(d, d + 1)), (slab.high, slice(d + layers - 1, d + layers))):
+            rim = lambda place, group=group: side[pl.ds(group + place, 1)]
+            for c in range(comps):
+                for n in range(2, d + 1):
+                    ux[c, row(n), at] = rim(slab.rim_disp(c, n))
+                raw[c, row(d), at] = rim(slab.rim_residual(c))
+            kx[row(d), at] = rim(slab.rim_stiff())
+            mx[row(d - 1), at] = rim(slab.rim_mass())
 
     def place_bands(even):
         for side, first_block, upward in ((corner_a, 2 * wedge.blocks, even), (band_b, 0, not even)):
@@ -415,6 +474,9 @@
                 late_t[c, a] = raw[c, a, late]
                 late_u[c, a] = ux[c, a, late]
             late_m[a] = mx[a, late]
+        for c in range(comps):
+            for n in range(2):
+                late_image[c, n] = image[c, n, late]
 
     @pl.when(band_even)
     def _():
@@ -475,21 +537,21 @@
 
     interface = (layer == d - 1) | (layer == d + layers - 1)
 
-    def faces(a, carry):
+    given = {1: 0, all_rows - 2: 1}
+    for a in range(all_rows):
         k = kx[a]
         k_h = conductance(k, ahead(k, 0))
         k_r = jnp.where(lane < width - 1, conductance(k, ahead(k, 1)), 0.0)
         kh[a], kh_back[a], kr[a], kr_back[a] = k_h, behind(k_h, 0), k_r, behind(k_r, 1)
-        ks[a] = conductance(k, kx[jnp.minimum(a + 1, all_rows - 1)])
+        ks[a] = conductance(k, kx[min(a + 1, all_rows - 1)])
         for c in range(comps):
             v = ux[c, a]
             flux = jnp.where(interface, k_h * (ahead(v, 0) - v), 0.0)
             change = COMPONENT_SCALE[c] * (flux - behind(flux, 0))
-            change = change - jnp.where(layer == d, raft[c, pl.ds(a, 1)], 0.0)
+            change = change - jnp.where(layer == d, raft[c, a : a + 1], 0.0)
             t0[c, a] = raw[c, a] + change
-        return carry
-
-    lax.fori_loop(0, all_rows, faces, 0, unroll=True)
+            if a in given:
+                turn[c, given[a]] = change
     for a in (d - 1, d + rows - 1):
         for c in range(comps):
             flux = COMPONENT_SCALE[c] * (ks[a] * (ux[c, a + 1] - ux[c, a]))
@@ -531,12 +593,20 @@
                     if step > 1:
                         centre = centre - c_k * levels[step - 2][c, a, part]
                     dst[c, a, part] = centre - (around if COMPONENT_SCALE[c] == 1.0 else COMPONENT_SCALE[c] * around)
+        if step == 1:
+            a_wide = jnp.broadcast_to(shift_of[0], (all_layers, width))
+            inside = (layer > d) & (layer < d + layers - 1)
+            for a, n in given.items():
+                for c in range(comps):
+                    x = turn[c, n]
+                    known = image[c, n] - COMPONENT_SCALE[c] * (kh[a] * ahead(x, 0) + kh_back[a] * behind(x, 0))
+                    dst[c, a] = jnp.where(inside, known - a_wide * src[c, a], dst[c, a])
 
 
 def late_kernel(
-    t0, t1, t2, t3, t4, kx, kh, late_t, late_u, late_m, raft, payload_in, corner_b, survey,
+    t0, t1, t2, t3, t4, kx, kh, late_t, late_u, late_m, late_image, raft, payload_in, corner_b, survey,
     b0, b1, b2, b3, b4, payload,
-    s0, s1, s2, s3, s4, raw, ux, k_tile, m_tile, ks, kh_tile, kh_back, kr, kr_back, diag,
+    s0, s1, s2, s3, s4, raw, ux, k_tile, m_tile, ks, kh_tile, kh_back, kr, kr_back, diag, turn,
 ):
     comps, rows, layers, width = b0.shape
     d = DEPTH
@@ -573,6 +643,8 @@
         for m, above in enumerate((sector_even, jnp.logical_not(sector_even))):
             place_wedge(raw, ux, k_tile, m_tile, corner_b, m * wedge.blocks, wedge, comps, rows, above, near, not even)
 
+        given = {1: 0, all_rows - 2: 1}
+        inside = (layer + off > d) & (layer + off < d + layers - 1)
         crossing = layer == (d - 1 if even else d + layers - 1 - off)
         on_raft = layer == d
         for a in range(all_rows):
@@ -590,6 +662,8 @@
                 if even:
                     change = change - jnp.where(on_raft, raft[c, a : a + 1], 0.0)
                 s0[c, a] = raw[c, a] + change
+                if a in given:
+                    turn[c, given[a]] = change
         for a in (d - 1, d + rows - 1):
             for c in range(comps):
                 flux = COMPONENT_SCALE[c] * (ks[a] * (ux[c, a + 1] - ux[c, a]))
@@ -614,7 +688,14 @@
                     centre = centres[0 if c < 2 else 1] * v
                     if step > 1:
                         centre = centre - link_of[step - 1] * late[step - 2][c, a]
-                    dst[c, a] = centre - (around if COMPONENT_SCALE[c] == 1.0 else COMPONENT_SCALE[c] * around)
+                    out = centre - (around if COMPONENT_SCALE[c] == 1.0 else COMPONENT_SCALE[c] * around)
+                    if step == 1 and a in given:
+                        x = turn[c, given[a]]
+                        known = late_image[c, given[a]] - COMPONENT_SCALE[c] * (
+                            kh_tile[a] * ahead(x, 0) + kh_back[a] * behind(x, 0)
+                        )
+                        out = jnp.where(inside, known - shift_of[0] * v, out)
+                    dst[c, a] = out
 
         sums = [jnp.zeros((8, width), F32) for _ in pairs]
         for a in range(rows):
@@ -767,15 +848,15 @@
         functools.partial(early_kernel, bearings=bearings, sectors=sectors, bands=bands),
         [(comps, *extended)] * (ITERS + 1)
         + [extended] * 2
-        + [tile_field, tile_field, tile_block, (comps + 2, all_rows, radial), (devices, 128)],
+        + [tile_field, tile_field, tile_block, (comps, 2, TILE, radial), (comps + 2, all_rows, radial), (devices, 128)],
         (work, slab_a, slab_b, band_b, corner_a, survey),
-        scratch=[(comps, *extended)] * 2 + [extended] * 5 + [(2, *extended)],
+        scratch=[(comps, *extended)] * 2 + [extended] * 5 + [(2, *extended)] + [(comps, 2, *extended[1:])] * 2,
     )
     *basis, payload = kernel_call(
         late_kernel,
         [field] * (ITERS + 1) + [(devices, 128)],
         (*early, payload, corner_b, survey),
-        scratch=[tile_field] * (ITERS + 3) + [tile_block] * 7 + [(2, *tile_block)],
+        scratch=[tile_field] * (ITERS + 3) + [tile_block] * 7 + [(2, *tile_block), (comps, 2, TILE, radial)],
     )
     received = lax.all_to_all(payload, AXES, 0, 0, tiled=True)
     increment, residual, force = kernel_call(

time: 47 us -> 46.1 us (0.981)
  blocking collectives: 24.9 us -> 23.9 us
    all_to_all x1, blocking collectives: 12.3 us -> 11.3 us  [per_device(): survey = lax.all_to_all(survey, AXES, 0, 0, tiled=True)]
  transfers between devices with their start and end apart: 5 -> 5, of which waited for: 1 -> 1; matrix products, arithmetic and copies ran while one was open for 0% -> 0% of each run, Pallas kernels for 14% -> 15%
where the time goes in v5:
time: 46.1 us; the launch traced here: 45.9 us
  blocking collectives  23.9 us (52%)
  Pallas kernels  12.3 us (27%)
  starting transfers between devices  7.98 us (17%)
  waiting for transfers between devices  1.04 us (2%)
  between operations  0.7 us (2%)
    all_to_all x1, blocking collectives, per_device(): received = lax.all_to_all(payload, AXES, 0, 0, tiled=True)  12.6 us
    pallas_call x6, Pallas kernels, kernel_call(): pl.pallas_call(body, out_shape=[jax.ShapeDtypeStruct(s, F32) for s in out...  12.3 us
    all_to_all x1, blocking collectives, per_device(): survey = lax.all_to_all(survey, AXES, 0, 0, tiled=True)  11.3 us
    ppermute x5, starting transfers between devices, exchange(): return lax.ppermute(x, AXES, pairs)  7.98 us
    ppermute x5, waiting for transfers between devices, exchange(): return lax.ppermute(x, AXES, pairs)  1.04 us
  transfers between devices with their start and end apart: 5, of which 1 were waited for; matrix products, arithmetic and copies ran while one was open for 0% of the time, Pallas kernels for 15%

profile of v5, /device:TPU:0, one launch (start us, length us, event | category | flops | bytes accessed | tf_op | source)
XLA Modules:
  0.0 45.9 jit_solution(18352039173608885055)
XLA Ops:
  0.6 2.0 %shard_map.112 = (f32[11,8,16,256]{3,2,1,0:T(8,128)S(1)}, f32[352,256]{1,0:T(8,128)S(1)}, f32[352,256]{1,0:T(8,128)S(1)}, f32[32,8,256]{2,1,0:T(8,128)S(1)}) custom-call(f32[3,8,16,256]{3,2,1,0:T(8,128)} %u_far.1, f32[3,8,16,256]{3,2,1,0:T(8,128)} %load_far.1, f32[8,16,256]{2,1,0:T(8,128)} %mass_far.1, f32[8,16,256]{2,1,0:T(8,128)} %stiff_far.1, s32[4]{0:T(128)} %node_far.1, ...), custom_call_target="tpu_custom_call" | custom-call | tf_op jit(solution)/shard_map/pallas_call | solution.py:775
  2.6 3.0 %collective-permute-start = (f32[352,256]{1,0:T(8,128)S(1)}, f32[352,256]{1,0:T(8,128)S(1)}, u32[]{:S(2)}, u32[]{:S(2)}) collective-permute-start(f32[352,256]{1,0:T(8,128)S(1)} %get-tuple-element.29), channel_id=1, source_target_pairs={{0,4},{1,5},{2,6},{3,7},{4,0},{5,1},{6,2},{7,3},{8,12},{9,13},{10,... | collective-permute-start | bytes 1081352 | tf_op jit(solution)/shard_map/ppermute | solution.py:810
  5.7 3.6 %collective-permute-start.1 = (f32[352,256]{1,0:T(8,128)S(1)}, f32[352,256]{1,0:T(8,128)S(1)}, u32[]{:S(2)}, u32[]{:S(2)}) collective-permute-start(f32[352,256]{1,0:T(8,128)S(1)} %get-tuple-element.30), channel_id=1, source_target_pairs={{0,28},{1,29},{2,30},{3,31},{4,8},{5,9},{6,10},{7,11},{8,4},{9,5},... | collective-permute-start | bytes 1081352 | tf_op jit(solution)/shard_map/ppermute | solution.py:810
  9.2 0.7 %collective-permute-start.2 = (f32[32,8,256]{2,1,0:T(8,128)S(1)}, f32[32,8,256]{2,1,0:T(8,128)S(1)}, u32[]{:S(2)}, u32[]{:S(2)}) collective-permute-start(f32[32,8,256]{2,1,0:T(8,128)S(1)} %get-tuple-element.31), channel_id=1, source_target_pairs={{1,2},{2,1},{5,6},{6,5},{9,10},{10,9},{13,14},{14,13},{17,18},{18,... | collective-permute-start | bytes 786440 | tf_op jit(solution)/shard_map/ppermute | solution.py:810
  9.9 2.0 %shard_map.113 = f32[32,128]{1,0:T(8,128)S(1)} custom-call(f32[11,8,16,256]{3,2,1,0:T(8,128)S(1)} %get-tuple-element.28.work), custom_call_target="tpu_custom_call" | custom-call | tf_op jit(solution)/shard_map/pallas_call | solution.py:775
  11.9 11.3 %all_to_all.22 = f32[32,1,128]{2,1,0:T(1,128)S(1)} all-to-all(f32[32,1,128]{2,1,0:T(1,128)S(1)} %bitcast.13), channel_id=1, replica_groups=mesh['sector'=8,'band'=4] {'sector','band'}, dimensions={0} | all-to-all | bytes 32768 | tf_op jit(solution)/shard_map/all_to_all | solution.py:835
  23.1 0.0 collective-permute-done.2.band_b
  23.1 0.0 collective-permute-done.slab_a
  23.1 0.0 collective-permute-done.1.slab_b
  23.2 0.1 shard_map.114
  23.3 0.1 collective-permute-start.3
  23.4 0.7 %collective-permute-start.4 = (f32[16,8,256]{2,1,0:T(8,128)S(1)}, f32[16,8,256]{2,1,0:T(8,128)S(1)}, u32[]{:S(2)}, u32[]{:S(2)}) collective-permute-start(f32[16,8,256]{2,1,0:T(8,128)S(1)} %get-tuple-element.46), channel_id=1, source_target_pairs={{1,2},{2,1},{5,6},{6,5},{9,10},{10,9},{13,14},{14,13},{17,18},{18,... | collective-permute-start | bytes 393224 | tf_op jit(solution)/shard_map/ppermute | solution.py:810
  24.0 1.0 %collective-permute-done.3.corner_a = f32[48,8,256]{2,1,0:T(8,128)S(1)} collective-permute-done((f32[48,8,256]{2,1,0:T(8,128)S(1)}, f32[48,8,256]{2,1,0:T(8,128)S(1)}, u32[]{:S(2)}, u32[]{:S(2)}) %collective-permute-start.3) | collective-permute-done | bytes 393248 | tf_op jit(solution)/shard_map/ppermute | solution.py:810
  25.1 4.9 %shard_map.115 = (f32[3,16,24,256]{3,2,1,0:T(8,128)S(1)}, f32[3,16,24,256]{3,2,1,0:T(8,128)S(1)}, f32[3,16,24,256]{3,2,1,0:T(8,128)S(1)}, f32[3,16,24,256]{3,2,1...) custom-call(f32[11,8,16,256]{3,2,1,0:T(8,128)S(1)} %get-tuple-elemen, ...), custom_call_target="tpu_custom_call" | custom-call | tf_op jit(solution)/shard_map/pallas_call | solution.py:775
  30.0 0.0 collective-permute-done.4.corner_b
  30.0 2.0 %shard_map.116 = (f32[3,8,16,256]{3,2,1,0:T(8,128)S(1)}, f32[3,8,16,256]{3,2,1,0:T(8,128)S(1)}, f32[3,8,16,256]{3,2,1,0:T(8,128)S(1)}, f32[3,8,16,256]{3,2,1,0:T...) custom-call(f32[3,16,24,256]{3,2,1,0:T(8,128)S(1)} %get-tuple-element.33.t0, ...), custom_call_target="tpu_custom_call" | custom-call | tf_op jit(solution)/shard_map/pallas_call | solution.py:775
  32.0 12.6 %all_to_all.23 = f32[32,1,128]{2,1,0:T(1,128)S(1)} all-to-all(f32[32,1,128]{2,1,0:T(1,128)S(1)} %bitcast.14), channel_id=1, replica_groups=mesh['sector'=8,'band'=4] {'sector','band'}, dimensions={0} | all-to-all | bytes 32768 | tf_op jit(solution)/shard_map/all_to_all | solution.py:861
  44.6 1.3 %shard_map.117 = (f32[3,8,16,256]{3,2,1,0:T(8,128)}, f32[3,8,16,256]{3,2,1,0:T(8,128)}, f32[3,4]{1,0:T(4,128)}) custom-call(f32[32,128]{1,0:T(8,128)S(1)} %bitcast.12, f32[32,128]{1,0:T(8,128)S(1)} %bitcast.11, f32[3,8,16,256]{3,2,1,0:T(8,128)S(1)} %get-tuple-element.48.b0, f32[3,8,16,256]{3,2,1,0:T(8,128)S(1)} %get-tuple-element.49.b1, ...), custom_call_target="tpu_custom_call" | custom-call | tf_op jit(solution)/shard_map/pallas_call | solution.py:775
Async XLA Ops:
  2.6 20.5 %collective-permute-start = (f32[352,256]{1,0:T(8,128)S(1)}, f32[352,256]{1,0:T(8,128)S(1)}, u32[]{:S(2)}, u32[]{:S(2)}) collective-permute-start(f32[352,256]{1,0:T(8,128)S(1)} %get-tuple-element.29), channel_id=1, source_target_pairs={{0,4},{1,5},{2,6},{3,7},{4,0},{5,1},{6,2},{7,3},{8,12},{9,13},{10,... | collective-permute-start | bytes 1081352 | tf_op jit(solution)/shard_map/ppermute | solution.py:810
  5.7 17.5 %collective-permute-start.1 = (f32[352,256]{1,0:T(8,128)S(1)}, f32[352,256]{1,0:T(8,128)S(1)}, u32[]{:S(2)}, u32[]{:S(2)}) collective-permute-start(f32[352,256]{1,0:T(8,128)S(1)} %get-tuple-element.30), channel_id=1, source_target_pairs={{0,28},{1,29},{2,30},{3,31},{4,8},{5,9},{6,10},{7,11},{8,4},{9,5},... | collective-permute-start | bytes 1081352 | tf_op jit(solution)/shard_map/ppermute | solution.py:810
  9.2 13.9 %collective-permute-start.2 = (f32[32,8,256]{2,1,0:T(8,128)S(1)}, f32[32,8,256]{2,1,0:T(8,128)S(1)}, u32[]{:S(2)}, u32[]{:S(2)}) collective-permute-start(f32[32,8,256]{2,1,0:T(8,128)S(1)} %get-tuple-element.31), channel_id=1, source_target_pairs={{1,2},{2,1},{5,6},{6,5},{9,10},{10,9},{13,14},{14,13},{17,18},{18,... | collective-permute-start | bytes 786440 | tf_op jit(solution)/shard_map/ppermute | solution.py:810
  23.3 1.8 %collective-permute-start.3 = (f32[48,8,256]{2,1,0:T(8,128)S(1)}, f32[48,8,256]{2,1,0:T(8,128)S(1)}, u32[]{:S(2)}, u32[]{:S(2)}) collective-permute-start(f32[48,8,256]{2,1,0:T(8,128)S(1)} %get-tuple-element.32), channel_id=1, source_target_pairs={{0,1},{1,0},{2,3},{3,2},{4,5},{5,4},{6,7},{7,6},{8,9},{9,8},{10,11... | collective-permute-start | bytes 1179656 | tf_op jit(solution)/shard_map/ppermute | solution.py:810
  23.4 6.6 %collective-permute-start.4 = (f32[16,8,256]{2,1,0:T(8,128)S(1)}, f32[16,8,256]{2,1,0:T(8,128)S(1)}, u32[]{:S(2)}, u32[]{:S(2)}) collective-permute-start(f32[16,8,256]{2,1,0:T(8,128)S(1)} %get-tuple-element.46), channel_id=1, source_target_pairs={{1,2},{2,1},{5,6},{6,5},{9,10},{10,9},{13,14},{14,13},{17,18},{18,... | collective-permute-start | bytes 393224 | tf_op jit(solution)/shard_map/ppermute | solution.py:810

commit v6 on v5

--- a/solution.py
+++ b/solution.py
@@ -383,7 +383,7 @@
 
 
 def gram_pairs():
-    return [(i, j) for i in range(ITERS) for j in range(i, ITERS + 1)]
+    return [(0, j) for j in range(ITERS + 1)] + [(i, ITERS) for i in range(1, ITERS)]
 
 
 def place_wedge(t, ux, kx, mx, block, at, wedge, comps, rows, above, near, upward):
@@ -573,26 +573,34 @@
         src, dst = levels[step - 1], levels[step]
         a_k = jnp.broadcast_to(shift_of[step - 1], (8, width))
         c_k = jnp.broadcast_to(link_of[step - 1], (8, width)) if step > 1 else None
-        for a in range(step, all_rows - step):
-            for start in range(0, all_layers, 8):
-                part = slice(start, start + 8)
-                k_h, k_low, k_r, k_left = kh[a, part], kh_back[a, part], kr[a, part], kr_back[a, part]
-                k_next, k_back = ks[a, part], ks[a - 1, part]
-                centres = [diag[n, a, part] - a_k for n in range(2)]
-                for c in range(comps):
-                    v = src[c, a, part]
-                    upper, lower = ahead(v, 0), behind(v, 0)
-                    if start + 8 < all_layers:
-                        upper = jnp.where(within == 7, src[c, a, start + 8 : start + 9], upper)
-                    if start:
-                        lower = jnp.where(within == 0, src[c, a, start - 1 : start], lower)
-                    around = k_next * src[c, a + 1, part] + k_back * src[c, a - 1, part]
-                    around = around + (k_h * upper + k_low * lower)
-                    around = around + (k_r * shifted(v, 1, 1) + k_left * shifted(v, 1, -1))
-                    centre = centres[0 if c < 2 else 1] * v
-                    if step > 1:
-                        centre = centre - c_k * levels[step - 2][c, a, part]
-                    dst[c, a, part] = centre - (around if COMPONENT_SCALE[c] == 1.0 else COMPONENT_SCALE[c] * around)
+        def level_rows(starts, step=step, src=src, dst=dst, a_k=a_k, c_k=c_k):
+            for a in range(step, all_rows - step):
+                for start in starts:
+                    part = slice(start, start + 8)
+                    k_h, k_low, k_r, k_left = kh[a, part], kh_back[a, part], kr[a, part], kr_back[a, part]
+                    k_next, k_back = ks[a, part], ks[a - 1, part]
+                    centres = [diag[n, a, part] - a_k for n in range(2)]
+                    for c in range(comps):
+                        v = src[c, a, part]
+                        upper, lower = ahead(v, 0), behind(v, 0)
+                        if start + 8 < all_layers:
+                            upper = jnp.where(within == 7, src[c, a, start + 8 : start + 9], upper)
+                        if start:
+                            lower = jnp.where(within == 0, src[c, a, start - 1 : start], lower)
+                        around = k_next * src[c, a + 1, part] + k_back * src[c, a - 1, part]
+                        around = around + (k_h * upper + k_low * lower)
+                        around = around + (k_r * shifted(v, 1, 1) + k_left * shifted(v, 1, -1))
+                        centre = centres[0 if c < 2 else 1] * v
+                        if step > 1:
+                            centre = centre - c_k * levels[step - 2][c, a, part]
+                        dst[c, a, part] = centre - (around if COMPONENT_SCALE[c] == 1.0 else COMPONENT_SCALE[c] * around)
+
+        starts = range(0, all_layers, 8)
+        if step < ITERS:
+            level_rows(starts)
+        else:
+            pl.when(band_even)(functools.partial(level_rows, [x for x in starts if x >= TILE]))
+            pl.when(jnp.logical_not(band_even))(functools.partial(level_rows, [x for x in starts if x < all_layers - TILE]))
         if step == 1:
             a_wide = jnp.broadcast_to(shift_of[0], (all_layers, width))
             inside = (layer > d) & (layer < d + layers - 1)
@@ -729,6 +737,10 @@
     col = lax.broadcasted_iota(jnp.int32, total.shape, 1)
     table = {ij: jnp.sum(jnp.where(col == p, total, 0.0), axis=1, keepdims=True) for p, ij in enumerate(gram_pairs())}
     shift_of, link_of = coefficients(survey[...])
+    for i in range(ITERS - 1):
+        for j in range(i + 1, ITERS):
+            value = table[i, j + 1] + (shift_of[j] - shift_of[i]) * table[i, j] + link_of[j] * table[min(i, j - 1), max(i, j - 1)]
+            table[i + 1, j] = value - link_of[i] * table[i - 1, j] if i else value
     g = lambda i, j: table[min(i, j), max(i, j)]
     zero, one = jnp.zeros_like(table[0, 0]), jnp.ones_like(table[0, 0])
     res = [one] + [zero] * ITERS

time: 46.1 us -> 45.9 us (level)
  no operation moved by 1% of the time
where the time goes in v6:
time: 45.9 us; the launch traced here: 45.7 us
  blocking collectives  23.9 us (52%)
  Pallas kernels  12.1 us (26%)
  starting transfers between devices  7.98 us (17%)
  waiting for transfers between devices  1.04 us (2%)
  between operations  0.7 us (2%)
    all_to_all x1, blocking collectives, per_device(): received = lax.all_to_all(payload, AXES, 0, 0, tiled=True)  12.6 us
    pallas_call x6, Pallas kernels, kernel_call(): pl.pallas_call(body, out_shape=[jax.ShapeDtypeStruct(s, F32) for s in out...  12.1 us
    all_to_all x1, blocking collectives, per_device(): survey = lax.all_to_all(survey, AXES, 0, 0, tiled=True)  11.3 us
    ppermute x5, starting transfers between devices, exchange(): return lax.ppermute(x, AXES, pairs)  7.98 us
    ppermute x5, waiting for transfers between devices, exchange(): return lax.ppermute(x, AXES, pairs)  1.04 us
  transfers between devices with their start and end apart: 5, of which 1 were waited for; matrix products, arithmetic and copies ran while one was open for 0% of the time, Pallas kernels for 15%

profile of v6, /device:TPU:0, one launch (start us, length us, event | category | flops | bytes accessed | tf_op | source)
XLA Modules:
  0.0 45.7 jit_solution(1351247062932876610)
XLA Ops:
  0.6 2.0 %shard_map.112 = (f32[11,8,16,256]{3,2,1,0:T(8,128)S(1)}, f32[352,256]{1,0:T(8,128)S(1)}, f32[352,256]{1,0:T(8,128)S(1)}, f32[32,8,256]{2,1,0:T(8,128)S(1)}) custom-call(f32[3,8,16,256]{3,2,1,0:T(8,128)} %u_far.1, f32[3,8,16,256]{3,2,1,0:T(8,128)} %load_far.1, f32[8,16,256]{2,1,0:T(8,128)} %mass_far.1, f32[8,16,256]{2,1,0:T(8,128)} %stiff_far.1, s32[4]{0:T(128)} %node_far.1, ...), custom_call_target="tpu_custom_call" | custom-call | tf_op jit(solution)/shard_map/pallas_call | solution.py:787
  2.6 3.0 %collective-permute-start = (f32[352,256]{1,0:T(8,128)S(1)}, f32[352,256]{1,0:T(8,128)S(1)}, u32[]{:S(2)}, u32[]{:S(2)}) collective-permute-start(f32[352,256]{1,0:T(8,128)S(1)} %get-tuple-element.29), channel_id=1, source_target_pairs={{0,4},{1,5},{2,6},{3,7},{4,0},{5,1},{6,2},{7,3},{8,12},{9,13},{10,... | collective-permute-start | bytes 1081352 | tf_op jit(solution)/shard_map/ppermute | solution.py:822
  5.7 3.6 %collective-permute-start.1 = (f32[352,256]{1,0:T(8,128)S(1)}, f32[352,256]{1,0:T(8,128)S(1)}, u32[]{:S(2)}, u32[]{:S(2)}) collective-permute-start(f32[352,256]{1,0:T(8,128)S(1)} %get-tuple-element.30), channel_id=1, source_target_pairs={{0,28},{1,29},{2,30},{3,31},{4,8},{5,9},{6,10},{7,11},{8,4},{9,5},... | collective-permute-start | bytes 1081352 | tf_op jit(solution)/shard_map/ppermute | solution.py:822
  9.2 0.7 %collective-permute-start.2 = (f32[32,8,256]{2,1,0:T(8,128)S(1)}, f32[32,8,256]{2,1,0:T(8,128)S(1)}, u32[]{:S(2)}, u32[]{:S(2)}) collective-permute-start(f32[32,8,256]{2,1,0:T(8,128)S(1)} %get-tuple-element.31), channel_id=1, source_target_pairs={{1,2},{2,1},{5,6},{6,5},{9,10},{10,9},{13,14},{14,13},{17,18},{18,... | collective-permute-start | bytes 786440 | tf_op jit(solution)/shard_map/ppermute | solution.py:822
  9.9 2.0 %shard_map.113 = f32[32,128]{1,0:T(8,128)S(1)} custom-call(f32[11,8,16,256]{3,2,1,0:T(8,128)S(1)} %get-tuple-element.28.work), custom_call_target="tpu_custom_call" | custom-call | tf_op jit(solution)/shard_map/pallas_call | solution.py:787
  11.9 11.3 %all_to_all.22 = f32[32,1,128]{2,1,0:T(1,128)S(1)} all-to-all(f32[32,1,128]{2,1,0:T(1,128)S(1)} %bitcast.13), channel_id=1, replica_groups=mesh['sector'=8,'band'=4] {'sector','band'}, dimensions={0} | all-to-all | bytes 32768 | tf_op jit(solution)/shard_map/all_to_all | solution.py:847
  23.1 0.0 collective-permute-done.2.band_b
  23.1 0.0 collective-permute-done.slab_a
  23.1 0.0 collective-permute-done.1.slab_b
  23.2 0.1 shard_map.114
  23.3 0.1 collective-permute-start.3
  23.4 0.7 %collective-permute-start.4 = (f32[16,8,256]{2,1,0:T(8,128)S(1)}, f32[16,8,256]{2,1,0:T(8,128)S(1)}, u32[]{:S(2)}, u32[]{:S(2)}) collective-permute-start(f32[16,8,256]{2,1,0:T(8,128)S(1)} %get-tuple-element.46), channel_id=1, source_target_pairs={{1,2},{2,1},{5,6},{6,5},{9,10},{10,9},{13,14},{14,13},{17,18},{18,... | collective-permute-start | bytes 393224 | tf_op jit(solution)/shard_map/ppermute | solution.py:822
  24.0 1.0 %collective-permute-done.3.corner_a = f32[48,8,256]{2,1,0:T(8,128)S(1)} collective-permute-done((f32[48,8,256]{2,1,0:T(8,128)S(1)}, f32[48,8,256]{2,1,0:T(8,128)S(1)}, u32[]{:S(2)}, u32[]{:S(2)}) %collective-permute-start.3) | collective-permute-done | bytes 393248 | tf_op jit(solution)/shard_map/ppermute | solution.py:822
  25.1 4.9 %shard_map.115 = (f32[3,16,24,256]{3,2,1,0:T(8,128)S(1)}, f32[3,16,24,256]{3,2,1,0:T(8,128)S(1)}, f32[3,16,24,256]{3,2,1,0:T(8,128)S(1)}, f32[3,16,24,256]{3,2,1...) custom-call(f32[11,8,16,256]{3,2,1,0:T(8,128)S(1)} %get-tuple-elemen, ...), custom_call_target="tpu_custom_call" | custom-call | tf_op jit(solution)/shard_map/pallas_call | solution.py:787
  29.9 0.0 collective-permute-done.4.corner_b
  30.0 1.8 %shard_map.116 = (f32[3,8,16,256]{3,2,1,0:T(8,128)S(1)}, f32[3,8,16,256]{3,2,1,0:T(8,128)S(1)}, f32[3,8,16,256]{3,2,1,0:T(8,128)S(1)}, f32[3,8,16,256]{3,2,1,0:T...) custom-call(f32[3,16,24,256]{3,2,1,0:T(8,128)S(1)} %get-tuple-element.33.t0, ...), custom_call_target="tpu_custom_call" | custom-call | tf_op jit(solution)/shard_map/pallas_call | solution.py:787
  31.8 12.6 %all_to_all.23 = f32[32,1,128]{2,1,0:T(1,128)S(1)} all-to-all(f32[32,1,128]{2,1,0:T(1,128)S(1)} %bitcast.14), channel_id=1, replica_groups=mesh['sector'=8,'band'=4] {'sector','band'}, dimensions={0} | all-to-all | bytes 32768 | tf_op jit(solution)/shard_map/all_to_all | solution.py:873
  44.4 1.3 %shard_map.117 = (f32[3,8,16,256]{3,2,1,0:T(8,128)}, f32[3,8,16,256]{3,2,1,0:T(8,128)}, f32[3,4]{1,0:T(4,128)}) custom-call(f32[32,128]{1,0:T(8,128)S(1)} %bitcast.12, f32[32,128]{1,0:T(8,128)S(1)} %bitcast.11, f32[3,8,16,256]{3,2,1,0:T(8,128)S(1)} %get-tuple-element.48.b0, f32[3,8,16,256]{3,2,1,0:T(8,128)S(1)} %get-tuple-element.49.b1, ...), custom_call_target="tpu_custom_call" | custom-call | tf_op jit(solution)/shard_map/pallas_call | solution.py:787
Async XLA Ops:
  2.6 20.5 %collective-permute-start = (f32[352,256]{1,0:T(8,128)S(1)}, f32[352,256]{1,0:T(8,128)S(1)}, u32[]{:S(2)}, u32[]{:S(2)}) collective-permute-start(f32[352,256]{1,0:T(8,128)S(1)} %get-tuple-element.29), channel_id=1, source_target_pairs={{0,4},{1,5},{2,6},{3,7},{4,0},{5,1},{6,2},{7,3},{8,12},{9,13},{10,... | collective-permute-start | bytes 1081352 | tf_op jit(solution)/shard_map/ppermute | solution.py:822
  5.7 17.5 %collective-permute-start.1 = (f32[352,256]{1,0:T(8,128)S(1)}, f32[352,256]{1,0:T(8,128)S(1)}, u32[]{:S(2)}, u32[]{:S(2)}) collective-permute-start(f32[352,256]{1,0:T(8,128)S(1)} %get-tuple-element.30), channel_id=1, source_target_pairs={{0,28},{1,29},{2,30},{3,31},{4,8},{5,9},{6,10},{7,11},{8,4},{9,5},... | collective-permute-start | bytes 1081352 | tf_op jit(solution)/shard_map/ppermute | solution.py:822
  9.2 13.9 %collective-permute-start.2 = (f32[32,8,256]{2,1,0:T(8,128)S(1)}, f32[32,8,256]{2,1,0:T(8,128)S(1)}, u32[]{:S(2)}, u32[]{:S(2)}) collective-permute-start(f32[32,8,256]{2,1,0:T(8,128)S(1)} %get-tuple-element.31), channel_id=1, source_target_pairs={{1,2},{2,1},{5,6},{6,5},{9,10},{10,9},{13,14},{14,13},{17,18},{18,... | collective-permute-start | bytes 786440 | tf_op jit(solution)/shard_map/ppermute | solution.py:822
  23.3 1.8 %collective-permute-start.3 = (f32[48,8,256]{2,1,0:T(8,128)S(1)}, f32[48,8,256]{2,1,0:T(8,128)S(1)}, u32[]{:S(2)}, u32[]{:S(2)}) collective-permute-start(f32[48,8,256]{2,1,0:T(8,128)S(1)} %get-tuple-element.32), channel_id=1, source_target_pairs={{0,1},{1,0},{2,3},{3,2},{4,5},{5,4},{6,7},{7,6},{8,9},{9,8},{10,11... | collective-permute-start | bytes 1179656 | tf_op jit(solution)/shard_map/ppermute | solution.py:822
  23.4 6.6 %collective-permute-start.4 = (f32[16,8,256]{2,1,0:T(8,128)S(1)}, f32[16,8,256]{2,1,0:T(8,128)S(1)}, u32[]{:S(2)}, u32[]{:S(2)}) collective-permute-start(f32[16,8,256]{2,1,0:T(8,128)S(1)} %get-tuple-element.46), channel_id=1, source_target_pairs={{1,2},{2,1},{5,6},{6,5},{9,10},{10,9},{13,14},{14,13},{17,18},{18,... | collective-permute-start | bytes 393224 | tf_op jit(solution)/shard_map/ppermute | solution.py:822
